TPU v7x, 32 devices: a whole 2x2x4 slice. The times are simulated.
32 devices in a mesh: segment: 2 (over x), seq: 4 (over z), mp: 4 (over y, core).
Axes of the slice: x: 2, y: 2, z: 4, core: 2. Of those that a mesh axis runs over, the one named last changes fastest.
Arguments:
- memory: bfloat16 [2, 1024, 4096], P(None, 'seq', 'mp')
- decoder_rows: bfloat16 [2, 256, 4096], P(None, 'seq', 'mp')
- gains: bfloat16 [2, 4096], P('segment'), may hold values from 0.5 to 1.5
- weights: bfloat16 [2, 2, 4096, 4096], P('segment', None, None, 'mp')
- lengths: int32 [2], replicated, may hold values from 128 to 1024, as said below
Outputs:
- decoder_out: bfloat16 [2, 256, 4096], P(None, 'seq', ('segment', 'mp'))
Inputs may be any that keep to these rules, and one draw needn't show every extreme that they name: memory positions of document b at or beyond lengths[b] are padding; some document has all 1024 positions.
All inputs are finite; a program needn't handle non-finite values.
Results may differ from a plain program's by a relative error of at most 0.015.
The roundings to bfloat16 on the way count: a program that leaves them out, or rounds other values in their place, can miss the bound.
Values may be sent and summed in bfloat16 or wider, within the bound.
No kernel may reach another device: no remote copies, remote signals or barrier semaphores. Data moves between devices by JAX's collectives and lax.ppermute only.
A program may use at most 192 MiB of HBM per device.

v0:
```python
import jax
import jax.numpy as jnp
from jax import lax
from jax.sharding import PartitionSpec as P

DKV = 64


norm_eps = 1e-06
masked_score = -1e30


def passed_along(shard, axis, by):
    count = lax.axis_size(axis)
    pairs = [(i, i + by) for i in range(count) if 0 <= i + by < count]
    return lax.ppermute(shard, axis, pairs)


def rms_rows(rows, gain):
    wide = rows.astype(jnp.float32)
    inverse = lax.rsqrt(jnp.mean(wide * wide, axis=1, keepdims=True) + norm_eps)
    return (wide * inverse * gain.astype(jnp.float32)[None, :]).astype(jnp.bfloat16)


def fold_block(running, queries, key_block, value_block, first_pos, lengths):
    maxima, totals, summed = running
    doc_count, span = (key_block.shape[0], key_block.shape[1])
    heads_here = queries.shape[2]
    key_heads = key_block.reshape(doc_count, span, heads_here, DKV)
    value_heads = value_block.reshape(doc_count, span, heads_here, DKV)
    scores = jnp.einsum("bqhd,bkhd->bhqk", queries, key_heads, preferred_element_type=jnp.float32)
    positions = first_pos + lax.iota(jnp.int32, span)
    valid_keys = (positions[None, :] < lengths[:, None])[:, None, None, :]
    masked = jnp.where(valid_keys, scores, masked_score)
    new_max = jnp.maximum(maxima, jnp.max(masked, axis=-1))
    exp_scores = jnp.where(valid_keys, jnp.exp(masked - new_max[..., None]), 0.0)
    rescale = jnp.exp(maxima - new_max)
    totals = totals * rescale + jnp.sum(exp_scores, axis=-1)
    summed = summed * rescale[..., None] + jnp.einsum(
        "bhqk,bkhd->bhqd",
        exp_scores.astype(jnp.bfloat16),
        value_heads,
        preferred_element_type=jnp.float32,
    )
    return (new_max, totals, summed)


def on_device(memory, decoder_rows, gains, weights, lengths):
    segment_index = lax.axis_index("segment")
    decoding = segment_index == 1
    doc_count, mem_dev, part_width = memory.shape
    pos_dev = decoder_rows.shape[1]
    mem_count = doc_count * mem_dev
    row_count = doc_count * pos_dev
    mem_full, dec_full = (
        lax.all_gather(memory.reshape(mem_count, part_width), "mp", axis=1, tiled=True),
        lax.all_gather(decoder_rows.reshape(row_count, part_width), "mp", axis=1, tiled=True),
    )
    first_weight = weights[0, 0]
    second_weight = weights[0, 1]
    section_gain = gains[0]
    head_width = first_weight.shape[1]
    heads_here = head_width // DKV

    def encode(source):
        normed = rms_rows(source, section_gain)
        key_out = jnp.dot(normed, first_weight, preferred_element_type=jnp.float32).astype(
            jnp.bfloat16
        )
        value_out = jnp.dot(normed, second_weight, preferred_element_type=jnp.float32).astype(
            jnp.bfloat16
        )
        return (key_out, value_out)

    def skip_encode(source):
        empty = jnp.zeros((mem_count, head_width), jnp.bfloat16)
        return (empty, empty)

    key_local, value_local = lax.cond(decoding, skip_encode, encode, mem_full)
    query_rows = lax.cond(
        decoding,
        lambda source: jnp.dot(
            rms_rows(source, section_gain), first_weight, preferred_element_type=jnp.float32
        ).astype(jnp.bfloat16),
        lambda source: jnp.zeros((row_count, head_width), jnp.bfloat16),
        dec_full,
    )
    key_rows, value_rows = passed_along((key_local, value_local), "segment", 1)
    key_flat = key_rows.reshape(doc_count, mem_dev, head_width)
    value_flat = value_rows.reshape(doc_count, mem_dev, head_width)
    queries = query_rows.reshape(doc_count, pos_dev, heads_here, DKV)
    start_state = (
        jnp.full((doc_count, heads_here, pos_dev), masked_score, jnp.float32),
        jnp.zeros((doc_count, heads_here, pos_dev), jnp.float32),
        jnp.zeros((doc_count, heads_here, pos_dev, DKV), jnp.float32),
    )
    first_pos = jnp.int32(0)
    key_part = lax.all_gather(key_flat, "seq", axis=1, tiled=True)
    value_part = lax.all_gather(value_flat, "seq", axis=1, tiled=True)
    span = key_part.shape[1]
    width = 256

    def attend(state):
        for offset in range(0, span, width):
            state = fold_block(
                state,
                queries,
                key_part[:, offset : offset + width],
                value_part[:, offset : offset + width],
                first_pos + offset,
                lengths,
            )
        return state

    final_state = lax.cond(decoding, attend, lambda state: state, start_state)

    def finish(state):
        context = state[2] / state[1][..., None]
        return (
            jnp.transpose(context, (0, 2, 1, 3)).reshape(row_count, head_width).astype(jnp.bfloat16)
        )

    context_rows = lax.cond(
        decoding,
        finish,
        lambda state: jnp.zeros((row_count, head_width), jnp.bfloat16),
        final_state,
    )
    update_terms = lax.cond(
        decoding,
        lambda source: lax.dot_general(
            source, second_weight, (((1,), (1,)), ((), ())), preferred_element_type=jnp.float32
        ),
        lambda source: jnp.zeros((row_count, second_weight.shape[0]), jnp.float32),
        context_rows,
    )
    update = lax.psum_scatter(
        update_terms.astype(jnp.bfloat16), ("segment", "mp"), scatter_dimension=1, tiled=True
    ).astype(jnp.float32)
    out_width = update.shape[1]
    group_index = segment_index * lax.axis_size("mp") + lax.axis_index("mp")
    residual = lax.dynamic_slice_in_dim(dec_full, group_index * out_width, out_width, 1)
    decoder_out = (residual.astype(jnp.float32) + update).astype(jnp.bfloat16)
    return decoder_out.reshape(doc_count, pos_dev, out_width)


def solution(mesh):
    in_specs = (
        P(None, "seq", "mp"),
        P(None, "seq", "mp"),
        P("segment", None),
        P("segment", None, None, "mp"),
        P(),
    )
    out_specs = P(None, "seq", ("segment", "mp"))
    return jax.shard_map(
        on_device, mesh=mesh, in_specs=in_specs, out_specs=out_specs, check_vma=False
    )
```

profile of v0, /device:TPU:0, one launch (start us, length us, event | category | flops | bytes accessed | tf_op | source)
XLA Modules:
  0.0 330.5 jit_solution(8773757547934667956)
XLA Ops:
  6.5 0.0 all-gather.7.cloned.1.call-start
  6.5 0.7 all-gather.7.cloned.1.call-update
  7.3 0.0 all-gather.5.cloned.1.call-start
  7.3 0.7 all-gather.5.cloned.1.call-update
  8.0 0.0 copy-start.6
  8.0 0.0 all-gather.9.cloned.1.call-start
  8.1 12.0 %slice_bitcast_fusion = (bf16[4096,1024]{1,0:T(8,128)(2,1)}, bf16[4096,1024]{1,0:T(8,128)(2,1)}) fusion(bf16[1,2,4096,1024]{3,2,1,0:T(8,128)(2,1)} %param.18), kind=kLoop, calls=%fused_computation.88 | loop fusion | bytes 33554432 | tf_op jit(solution)/shard_map/squeeze | solution.py:60
  20.0 0.0 copy-done.6
  20.0 0.1 reduce
  20.1 26.1 %all-gather.7.cloned.1.call-done = bf16[512,4096]{1,0:T(8,128)(2,1)} async-done(((bf16[512,1024]{1,0:T(8,128)(2,1)}), bf16[512,4096]{1,0:T(8,128)(2,1)}) %all-gather.7.cloned.1.call-update) | async-done | bytes 4194320 | tf_op jit(solution)/shard_map/all_gather | solution.py:56
  46.1 17.3 %conditional.5 = (bf16[512,1024]{1,0:T(8,128)(2,1)S(1)}, bf16[512,1024]{1,0:T(8,128)(2,1)S(1)}) conditional(s32[]{:T(128)} %convert_element_type.68, (bf16[512,4096]{1,0:T(8,128)(2,1)}, bf16[4096]{0:T(1024)(128)(2,1)S(1)}, bf16[4096,1024]{1,0:T(8,128)(2,1)}, bf16[4096,1024]{1,0:T(8,128)(2,1)}) %tuple.43, () %tuple.44), branch_computations={%region_0.0_spmd, %region_2.0_spmd} | conditional | flops 8614055936 | bytes 73468000 | solution.py:79
  46.1 0.0 slice-start
  46.1 3.2 fusion
  49.4 0.0 slice-start.1
  49.4 0.0 copy-start
  49.4 9.4 %convolution_convert_fusion = bf16[512,1024]{1,0:T(8,128)(2,1)S(1)} fusion(bf16[4096,1024]{1,0:T(8,128)(2,1)} %get-tuple-element.48, bf16[512,4096]{1,0:T(8,128)(2,1)} %get-tuple-element.44, f32[4096]{0:T(1024)S(1)} %convert_element_type.47, f32[512]{0:T(512)S(1)} %add_rsqrt_fusion), kind=kOutput, calls=%fused_computation.5 | convolution fusion | flops 4303880192 | bytes 13649920 | tf_op jit(solution)/shard_map/cond/branch_0_fun/dot_general | solution.py:70
  58.8 0.0 slice-done
  58.8 0.0 slice-done.1
  58.8 0.0 copy-done
  58.9 4.6 %convolution_convert_fusion.1 = bf16[512,1024]{1,0:T(8,128)(2,1)S(1)} fusion(bf16[4096,1024]{1,0:T(8,128)(2,1)S(1)} %bitcast.35, bf16[512,4096]{1,0:T(8,128)(2,1)S(1)} %copy-done, f32[4096]{0:T(1024)S(1)} %convert_element_type.47, f32[512]{0:T(512)S(1)} %add_rsqrt_fusion), kind=kOutput, calls=%fused_computation.6 | convolution fusion | flops 4303880192 | bytes 13649920 | tf_op jit(solution)/shard_map/cond/branch_0_fun/dot_general | solution.py:67
  63.5 1.4 collective-permute-start
  64.8 23.0 %collective-permute-done = bf16[512,1024]{1,0:T(8,128)(2,1)S(1)} collective-permute-done((bf16[512,1024]{1,0:T(8,128)(2,1)S(1)}, bf16[512,1024]{1,0:T(8,128)(2,1)S(1)}, u32[]{:S(2)}, u32[]{:S(2)}) %collective-permute-start) | collective-permute-done | bytes 1048608 | tf_op jit(solution)/shard_map/ppermute | solution.py:16
  87.8 0.0 copy-start.3
  87.8 1.0 copy-done.3
  88.8 0.0 all-gather.9.cloned.1.call-update
  88.8 0.0 all-gather.11.cloned.1.call-start
  88.9 4.5 %collective-permute-start.1 = (bf16[512,1024]{1,0:T(8,128)(2,1)S(1)}, bf16[512,1024]{1,0:T(8,128)(2,1)S(1)}, u32[]{:S(2)}, u32[]{:S(2)}) collective-permute-start(bf16[512,1024]{1,0:T(8,128)(2,1)S(1)} %get-tuple-element.63), channel_id=1, source_target_pairs={{0,16},{1,17},{2,18},{3,19},{4,20},{5,21},{6,22},{7,23},{8,24},{9,... | collective-permute-start | bytes 3145736 | tf_op jit(solution)/shard_map/ppermute | solution.py:16
  93.3 22.3 %collective-permute-done.1 = bf16[512,1024]{1,0:T(8,128)(2,1)S(1)} collective-permute-done((bf16[512,1024]{1,0:T(8,128)(2,1)S(1)}, bf16[512,1024]{1,0:T(8,128)(2,1)S(1)}, u32[]{:S(2)}, u32[]{:S(2)}) %collective-permute-start.1) | collective-permute-done | bytes 1048608 | tf_op jit(solution)/shard_map/ppermute | solution.py:16
  115.6 0.0 copy-start.4
  115.6 1.0 copy-done.4
  116.6 0.0 all-gather.11.cloned.1.call-update
  116.6 0.0 reduce-scatter.2.cloned.1.call-start
  116.6 0.0 all-gather.5.cloned.1.call-done
  116.7 0.0 copy-start.7
  116.7 0.1 conditional.6
  116.7 0.1 reshape.196
  116.8 54.0 %all-gather.9.cloned.1.call-done = bf16[2,1024,1024]{2,1,0:T(8,128)(2,1)} async-done(((bf16[2,256,1024]{2,1,0:T(8,128)(2,1)}), bf16[2,1024,1024]{2,1,0:T(8,128)(2,1)}) %all-gather.9.cloned.1.call-update) | async-done | bytes 4194320 | tf_op jit(solution)/shard_map/all_gather | solution.py:98
  170.7 80.8 %all-gather.11.cloned.1.call-done = bf16[2,1024,1024]{2,1,0:T(8,128)(2,1)} async-done(((bf16[2,256,1024]{2,1,0:T(8,128)(2,1)}), bf16[2,1024,1024]{2,1,0:T(8,128)(2,1)}) %all-gather.11.cloned.1.call-update) | async-done | bytes 4194320 | tf_op jit(solution)/shard_map/all_gather | solution.py:99
  251.5 0.0 copy-done.7
  251.5 0.3 conditional.7
  251.5 0.1 broadcast_in_dim.77
  251.8 0.1 conditional.9
  251.8 0.1 broadcast.154
  252.0 0.0 copy-start.1
  252.0 1.0 copy-done.1
  252.9 0.0 reduce-scatter.2.cloned.1.call-update
  253.0 69.3 %reduce-scatter.2.cloned.1.call-done = bf16[128,512]{1,0:T(8,128)(2,1)} async-done(((bf16[128,4096]{1,0:T(8,128)(2,1)}), bf16[128,512]{1,0:T(8,128)(2,1)}) %reduce-scatter.2.cloned.1.call-update) | async-done | bytes 131088 | tf_op jit(solution)/shard_map/reduce_scatter | solution.py:137
  322.3 1.7 add_convert_fusion
  (6 shorter events, 0.1 us)
Async XLA Ops:
  6.5 39.6 %all-gather.7.cloned.1.call-start = ((), (), s32[]{:S(2)}) async-start(), calls=%async_computation.2 | async-start | bytes 5242880 | tf_op jit(solution)/shard_map/all_gather | solution.py:56
  7.3 109.4 %all-gather.5.cloned.1.call-start = ((), (), s32[]{:S(2)}) async-start(), calls=%async_computation.1 | async-start | bytes 1310720 | tf_op jit(solution)/shard_map/all_gather | solution.py:57
  8.0 12.0 %copy-start.6 = (bf16[1,4096]{1,0:T(2,128)(2,1)S(1)}, bf16[1,4096]{1,0:T(2,128)(2,1)}, u32[]{:S(2)}) copy-start(bf16[1,4096]{1,0:T(2,128)(2,1)} %param.17) | copy-start | bytes 24580
  8.0 162.7 %all-gather.9.cloned.1.call-start = ((), (), s32[]{:S(2)}) async-start(), calls=%async_computation.3 | async-start | bytes 5242880 | tf_op jit(solution)/shard_map/all_gather | solution.py:98
  46.1 12.7 %slice-start = ((s8[8388608]{0:T(1024)(128)(4,1)}), s8[4194304]{0:T(1024)(128)(4,1)S(1)}, s32[]{:S(2)}) async-start(s8[8388608]{0:T(1024)(128)(4,1)} %bitcast.34), calls=%async_computation.6 | async-start | bytes 8388608 | tf_op jit(solution)/shard_map/cond
  49.4 9.4 %slice-start.1 = ((s8[8388608]{0:T(1024)(128)(4,1)}), s8[4194304]{0:T(1024)(128)(4,1)S(1)}, s32[]{:S(2)}) async-start(s8[8388608]{0:T(1024)(128)(4,1)} %bitcast.34), calls=%async_computation.7 | async-start | bytes 8388608 | tf_op jit(solution)/shard_map/cond
  49.4 9.4 %copy-start = (bf16[512,4096]{1,0:T(8,128)(2,1)S(1)}, bf16[512,4096]{1,0:T(8,128)(2,1)}, u32[]{:S(2)}) copy-start(bf16[512,4096]{1,0:T(8,128)(2,1)} %get-tuple-element.44) | copy-start | bytes 12582916 | tf_op jit(solution)/shard_map/cond
  63.5 24.4 %collective-permute-start = (bf16[512,1024]{1,0:T(8,128)(2,1)S(1)}, bf16[512,1024]{1,0:T(8,128)(2,1)S(1)}, u32[]{:S(2)}, u32[]{:S(2)}) collective-permute-start(bf16[512,1024]{1,0:T(8,128)(2,1)S(1)} %get-tuple-element.62), channel_id=1, source_target_pairs={{0,16},{1,17},{2,18},{3,19},{4,20},{5,21},{6,22},{7,23},{8,24},{9,... | collective-permute-start | bytes 3145736 | tf_op jit(solution)/shard_map/ppermute | solution.py:16
  87.8 1.0 copy-start.3
  88.8 162.7 %all-gather.11.cloned.1.call-start = ((), (), s32[]{:S(2)}) async-start(), calls=%async_computation.4 | async-start | bytes 5242880 | tf_op jit(solution)/shard_map/all_gather | solution.py:99
  88.9 26.7 %collective-permute-start.1 = (bf16[512,1024]{1,0:T(8,128)(2,1)S(1)}, bf16[512,1024]{1,0:T(8,128)(2,1)S(1)}, u32[]{:S(2)}, u32[]{:S(2)}) collective-permute-start(bf16[512,1024]{1,0:T(8,128)(2,1)S(1)} %get-tuple-element.63), channel_id=1, source_target_pairs={{0,16},{1,17},{2,18},{3,19},{4,20},{5,21},{6,22},{7,23},{8,24},{9,... | collective-permute-start | bytes 3145736 | tf_op jit(solution)/shard_map/ppermute | solution.py:16
  115.6 1.0 copy-start.4
  116.6 205.7 %reduce-scatter.2.cloned.1.call-start = ((), (), s32[]{:S(2)}) async-start(), calls=%async_computation.5 | async-start | bytes 1179648 | tf_op jit(solution)/shard_map/reduce_scatter | solution.py:137
  116.7 134.8 %copy-start.7 = (s32[2]{0:T(128)S(1)}, s32[2]{0:T(128)}, u32[]{:S(2)}) copy-start(s32[2]{0:T(128)} %param.19) | copy-start | bytes 28
  252.0 1.0 copy-start.1
Sparse Core Ops, SparseCore 0:
  8.9 37.1 all-gather.6
  47.7 16.7 all-gather.4
  88.9 81.7 all-gather.8
  172.1 79.2 all-gather.10
  254.5 67.7 reduce-scatter.1
where the time goes:
time: 331 us; the launch traced here: 330 us
  waiting for transfers between devices  277 us (84%)
  local copies, waits for them, and re-layouts  15.2 us (5%)
  matrix products  14 us (4%)
  between operations  13.2 us (4%)
  starting transfers between devices  5.97 us (2%)
  other arithmetic  4.95 us (1%)
    all_gather x1, waiting for transfers between devices, on_device(): value_part = lax.all_gather(value_flat, 'seq', axis=1, tiled=True)  80.8 us
    reduce_scatter x1, waiting for transfers between devices, on_device(): lax.psum_scatter(update_terms.astype(jnp.bfloat16), ('segment', 'mp'), sc...  69.3 us
    all_gather x1, waiting for transfers between devices, on_device(): key_part = lax.all_gather(key_flat, 'seq', axis=1, tiled=True)  54 us
    ppermute x2, waiting for transfers between devices, passed_along(): return lax.ppermute(shard, axis, pairs)  45.3 us
    all_gather x1, waiting for transfers between devices, on_device(): lax.all_gather(memory.reshape(mem_count, part_width), 'mp', axis=1, tiled...  26.1 us
    squeeze x1, local copies, waits for them, and re-layouts, on_device(): second_weight = weights[0, 1]  12 us
    dot_general x1, matrix products, encode(): jnp.dot(normed, second_weight, preferred_element_type=jnp.float32)  9.4 us
  transfers between devices with their start and end apart: 7, of which 6 were waited for; matrix products, arithmetic and copies ran while one was open for 9% of the time, Pallas kernels for 0%

commit v1 on v0

v1 whole, which is shorter than its diff:
```python
import functools

import jax
import jax.numpy as jnp
from jax import lax
from jax.experimental import pallas as pl
from jax.experimental.pallas import tpu as pltpu
from jax.sharding import PartitionSpec as P

DKV = 64
norm_eps = 1e-06
masked_score = -1e30
PAIR = 2 * DKV
STEP_PAIRS = 2
STAT_ROWS = 16
VMEM = pl.BlockSpec(memory_space=pltpu.VMEM)
SMEM = pl.BlockSpec(memory_space=pltpu.SMEM)
ANY = pl.BlockSpec(memory_space=pl.ANY)
f32 = jnp.float32
bf16 = jnp.bfloat16


def params():
    return pltpu.CompilerParams(vmem_limit_bytes=48 * 1024 * 1024)


def normed_parts(parts, gain_ref, info):
    wide = [part[...].astype(f32) for part in parts]
    squares = sum(jnp.sum(w * w, axis=1, keepdims=True) for w in wide)
    features = sum(w.shape[1] for w in wide)
    inverse = lax.rsqrt(squares / features + norm_eps)
    return [
        (w * inverse * gain_ref[pl.ds(info[2 + k], 1), :]).astype(bf16)
        for k, w in enumerate(wide)
    ]


def query_kernel(info, x0, x1, x2, x3, gain, weights, out, res, wbuf, sem):
    parts = (x0, x1, x2, x3)
    width = x0.shape[1]

    def copy(k):
        return pltpu.make_async_copy(
            weights.at[0, 0, pl.ds(info[2 + k] * width, width), :], wbuf.at[k], sem.at[k]
        )

    @pl.when(info[0] == 1)
    def _():
        for k in range(4):
            copy(k).start()
        rows = normed_parts(parts, gain, info)
        half = width // 2
        offset = pl.multiple_of(info[6] * half, half)
        for k in range(4):
            for side in range(2):

                @pl.when(info[7 + side] == k)
                def _():
                    res[:, side * half : (side + 1) * half] = parts[k][:, pl.ds(offset, half)]

        total = None
        for k in range(4):
            copy(k).wait()
            term = jnp.dot(rows[k], wbuf[k], preferred_element_type=f32)
            total = term if total is None else total + term
        out[...] = total.astype(bf16)


def memory_kernel(info, x0, x1, x2, x3, gain, weights, key_out, value_out, wbuf, acc, sem):
    parts = (x0, x1, x2, x3)
    width = x0.shape[1]

    def copy(k, which):
        return pltpu.make_async_copy(
            weights.at[0, which, pl.ds(info[2 + k] * width, width), :],
            wbuf.at[k, which],
            sem.at[k, which],
        )

    @pl.when(info[0] == 0)
    def _():
        for k in range(4):
            for which in range(2):
                copy(k, which).start()
        rows = normed_parts(parts, gain, info)
        for k in range(4):
            for which in range(2):
                copy(k, which).wait()
                term = jnp.dot(rows[k], wbuf[k, which], preferred_element_type=f32)
                if k == 0:
                    acc[which] = term
                elif k < 3:
                    acc[which] += term
                else:
                    out = key_out if which == 0 else value_out
                    out[...] = (acc[which] + term).astype(bf16)


def attention_kernel(count, docs, info, lengths, *refs):
    q_refs, k_refs, v_refs = (
        refs[:count],
        refs[count : count + docs],
        refs[count + docs : count + 2 * docs],
    )
    out = refs[-1]
    span = k_refs[0].shape[0]
    pos = q_refs[0].shape[0] // docs
    group = min(4, count)
    lanes = group * pos

    @pl.when(info[0] == 0)
    def _():
        first = info[1] * span
        lane = lax.broadcasted_iota(jnp.int32, (1, PAIR), 1)
        low = lane < DKV
        positions = first + lax.broadcasted_iota(jnp.int32, (span, 1), 0)
        for base in range(0, count, group):
            stats = [[] for _ in range(group)]
            for pair in range(STEP_PAIRS):
                cols = slice(pair * PAIR, (pair + 1) * PAIR)
                contexts, lses = [], []
                for b in range(docs):
                    rows = jnp.concatenate(
                        [q_refs[base + j][b * pos : (b + 1) * pos, cols] for j in range(group)], axis=0
                    )
                    zero = jnp.zeros_like(rows)
                    both = jnp.concatenate(
                        [jnp.where(low, rows, zero), jnp.where(low, zero, rows)], axis=0
                    )
                    scores = lax.dot_general(
                        k_refs[b][:, cols], both, (((1,), (1,)), ((), ())), preferred_element_type=f32
                    )
                    masked = jnp.where(positions < lengths[b], scores, masked_score)
                    top = jnp.max(masked, axis=0, keepdims=True)
                    probs = jnp.exp(masked - top)
                    total = jnp.sum(probs, axis=0, keepdims=True)
                    summed = lax.dot_general(
                        v_refs[b][:, cols],
                        probs.astype(bf16),
                        (((0,), (0,)), ((), ())),
                        preferred_element_type=f32,
                    )
                    scaled = summed / total
                    lse = jnp.where(first < lengths[b], top + jnp.log(total), masked_score)
                    contexts.append(
                        jnp.concatenate([scaled[:DKV, :lanes], scaled[DKV:, lanes:]], axis=0)
                    )
                    lses.append(lse)
                for j in range(group):
                    block = slice((j // 2) * PAIR, (j // 2 + 1) * PAIR)

                    def placed(first_doc, second_doc):
                        if j % 2 == 0:
                            return jnp.where(low, first_doc, pltpu.roll(second_doc, DKV, 1))
                        return jnp.where(low, pltpu.roll(first_doc, DKV, 1), second_doc)

                    out[base + j, 0, pair * PAIR : (pair + 1) * PAIR, :] = placed(
                        contexts[0][:, block], contexts[1][:, block]
                    ).astype(bf16)
                    for head in range(2):
                        shifted = slice(block.start + head * lanes, block.stop + head * lanes)
                        stats[j].append(
                            placed(
                                jnp.broadcast_to(lses[0][:, shifted], (8, PAIR)),
                                jnp.broadcast_to(lses[1][:, shifted], (8, PAIR)),
                            )[:1]
                        )
            for j in range(group):
                lse = jnp.concatenate(stats[j], axis=0)
                high = lse.astype(bf16).astype(f32)
                middle = (lse - high).astype(bf16).astype(f32)
                rest = lse - high - middle
                packed = jnp.concatenate([high, middle, rest, jnp.zeros_like(rest)], axis=0)
                out[base + j, 0, STEP_PAIRS * PAIR :, :] = packed.astype(bf16)


def combine_kernel(info, *refs):
    sources, out = (refs[:-1], refs[-1])
    slabs = out.shape[0] // (STEP_PAIRS * PAIR)
    heads = 2 * STEP_PAIRS

    @pl.when(info[0] == 0)
    def _():
        for slab in range(slabs):
            lses = []
            for source in sources:
                packed = source[slab, STEP_PAIRS * PAIR :, :].astype(f32)
                lses.append(
                    packed[:heads] + packed[heads : 2 * heads] + packed[2 * heads : 3 * heads]
                )
            top = functools.reduce(jnp.maximum, lses)
            shares = [jnp.exp(lse - top) for lse in lses]
            inverse = 1.0 / sum(shares)
            shares = [share * inverse for share in shares]
            for head in range(heads):
                rows = slice(head * DKV, (head + 1) * DKV)
                context = sum(
                    source[slab, rows, :].astype(f32) * share[head : head + 1]
                    for source, share in zip(sources, shares)
                )
                start = slab * STEP_PAIRS * PAIR + head * DKV
                out[start : start + DKV, :] = context.astype(bf16)


def project_kernel(mask, info, context, weights, out, wbuf, sem):
    block = out.shape[0] // 4
    targets = [(mask ^ 2, 0), (mask ^ 2, 4), (mask, 0), (mask, 4)]

    def copy(i):
        k, add = targets[i]
        return pltpu.make_async_copy(
            weights.at[0, 1, pl.ds((info[2 + k] + add) * block, block), :], wbuf.at[i], sem.at[i]
        )

    @pl.when(info[0] == 1)
    def _():
        for i in range(4):
            copy(i).start()
        for i in range(4):
            copy(i).wait()
            out[i * block : (i + 1) * block, :] = jnp.dot(
                wbuf[i], context[...], preferred_element_type=f32
            ).astype(bf16)


def add_kernel(info, mine, other, out):
    @pl.when(info[0] == 1)
    def _():
        rows = out.shape[0]
        out[...] = (mine[:rows].astype(f32) + other[:rows].astype(f32)).astype(bf16)


def final_kernel(info, mine, sibling, across, res, out):
    @pl.when(info[0] == 1)
    def _():
        half = out.shape[2]
        rows = 2 * half
        for side in range(2):
            part = slice(rows + side * half, rows + (side + 1) * half)
            update = (
                mine[part].astype(f32)
                + sibling[part].astype(f32)
                + across[side * half : (side + 1) * half].astype(f32)
            )
            out[side] = (res[:, side * half : (side + 1) * half].astype(f32) + update.T).astype(bf16)


def call(kernel, out_shapes, args, specs, scratch=(), out_specs=None, flops=0, moved=0, **more):
    return pl.pallas_call(
        kernel,
        out_shape=out_shapes,
        in_specs=specs,
        out_specs=out_specs if out_specs is not None else jax.tree.map(lambda _: VMEM, out_shapes),
        scratch_shapes=list(scratch),
        compiler_params=params(),
        cost_estimate=pl.CostEstimate(flops=flops, bytes_accessed=moved, transcendentals=0),
        **more,
    )(*args)


def on_device(memory, decoder_rows, gains, weights, lengths):
    segment = lax.axis_index("segment")
    seq = lax.axis_index("seq")
    m = lax.axis_index("mp")
    count = lax.axis_size("seq")
    docs, span, width = memory.shape
    pos = decoder_rows.shape[1]
    rows = docs * pos
    head_width = weights.shape[3]

    info = jnp.stack(
        [segment, seq, m, m ^ 1, m ^ 2, m ^ 3, m % 2, m ^ (m // 2), m ^ (2 + m // 2)]
    ).astype(jnp.int32)
    gain = gains.astype(f32).reshape(4, width)
    lengths = lengths.astype(jnp.int32)

    def in_section(array, section, mask):
        pairs = [(section * 4 + i, section * 4 + (i ^ mask)) for i in range(4)]
        return lax.ppermute(array, ("segment", "mp"), pairs)

    def along_seq(array, section, by):
        pairs = [(section * count + i, section * count + (i + by) % count) for i in range(count)]
        return lax.ppermute(array, ("segment", "seq"), pairs)

    dec = decoder_rows.reshape(rows, width)
    dec_y = in_section(dec, 1, 2)
    dec_c = in_section(dec, 1, 1)
    mem_docs = [memory[b] for b in range(docs)]
    mem_c = [in_section(mem_docs[b], 0, 1) for b in range(docs)]
    mem_y = [in_section(mem_docs[b], 0, 2) for b in range(docs)]
    dec_yc = in_section(dec_y, 1, 1)

    queries, residual = call(
        query_kernel,
        (
            jax.ShapeDtypeStruct((rows, head_width), bf16),
            jax.ShapeDtypeStruct((rows, width), bf16),
        ),
        (info, dec, dec_c, dec_y, dec_yc, gain, weights),
        [SMEM, VMEM, VMEM, VMEM, VMEM, VMEM, ANY],
        [pltpu.VMEM((4, width, head_width), bf16), pltpu.SemaphoreType.DMA((4,))],
        flops=2 * rows * 4 * width * head_width,
        moved=8 * width * head_width,
    )
    pairs = [(1, 0)]
    q_pieces = [lax.ppermute(queries, "segment", pairs)]
    for by in range(1, count):
        q_pieces.append(along_seq(q_pieces[0], 0, by))

    keys, values = [], []
    for b in range(docs):
        mem_yc = in_section(mem_y[b], 0, 1)
        key, value = call(
            memory_kernel,
            (
                jax.ShapeDtypeStruct((span, head_width), bf16),
                jax.ShapeDtypeStruct((span, head_width), bf16),
            ),
            (info, mem_docs[b], mem_c[b], mem_y[b], mem_yc, gain, weights),
            [SMEM, VMEM, VMEM, VMEM, VMEM, VMEM, ANY],
            [
                pltpu.VMEM((4, 2, width, head_width), bf16),
                pltpu.VMEM((2, span, head_width), f32),
                pltpu.SemaphoreType.DMA((4, 2)),
            ],
            flops=4 * span * 4 * width * head_width,
            moved=16 * width * head_width,
        )
        keys.append(key)
        values.append(value)

    step_width = STEP_PAIRS * PAIR
    steps = head_width // step_width
    slab = step_width + STAT_ROWS
    column = lambda height: pl.BlockSpec((height, step_width), lambda i: (0, i))
    partial = call(
        functools.partial(attention_kernel, count, docs),
        jax.ShapeDtypeStruct((count, steps, slab, rows), bf16),
        (info, lengths, *q_pieces, *keys, *values),
        [SMEM, SMEM] + [column(rows)] * count + [column(span)] * (2 * docs),
        out_specs=pl.BlockSpec((count, 1, slab, rows), lambda i: (0, i, 0, 0)),
        grid=(steps,),
        flops=8 * rows * count * span * head_width,
        moved=4 * rows * count * head_width,
    )
    sources = [partial[0]] + [along_seq(partial[by], 0, -by) for by in range(1, count)]
    context = call(
        combine_kernel,
        jax.ShapeDtypeStruct((head_width, rows), bf16),
        (info, *sources),
        [SMEM] + [VMEM] * count,
        flops=8 * rows * count * head_width,
        moved=2 * rows * count * head_width,
    )
    context = lax.ppermute(context, "segment", [(0, 1)])

    block = 4 * width // 8

    def project(mask):
        return call(
            functools.partial(project_kernel, mask),
            jax.ShapeDtypeStruct((4 * block, rows), bf16),
            (info, context, weights),
            [SMEM, VMEM, ANY],
            [pltpu.VMEM((4, block, head_width), bf16), pltpu.SemaphoreType.DMA((4,))],
            flops=2 * rows * 4 * block * head_width,
            moved=8 * block * head_width,
        )

    for_sibling = project(1)
    sibling = in_section(for_sibling, 1, 1)
    mine = project(0)
    for_across = call(
        add_kernel,
        jax.ShapeDtypeStruct((2 * block, rows), bf16),
        (info, mine, sibling),
        [SMEM, VMEM, VMEM],
        moved=12 * block * rows,
    )
    across = in_section(for_across, 1, 2)
    done = call(
        final_kernel,
        jax.ShapeDtypeStruct((2, rows, block), bf16),
        (info, mine, sibling, across, residual),
        [SMEM, VMEM, VMEM, VMEM, VMEM],
        moved=20 * block * rows,
    )
    received = lax.ppermute(done[0], "segment", pairs)
    decoder_out = jnp.where(segment == 0, received, done[1])
    return decoder_out.reshape(docs, pos, block)


def solution(mesh):
    in_specs = (
        P(None, "seq", "mp"),
        P(None, "seq", "mp"),
        P("segment", None),
        P("segment", None, None, "mp"),
        P(),
    )
    out_specs = P(None, "seq", ("segment", "mp"))
    return jax.shard_map(
        on_device, mesh=mesh, in_specs=in_specs, out_specs=out_specs, check_vma=False
    )
```

time: 331 us -> 137 us (0.41)
  waiting for transfers between devices: 277 us -> 60.6 us
  starting transfers between devices: 5.97 us -> 45.4 us
  Pallas kernels: 0 us -> 27.4 us
  matrix products: 14 us -> 0 us
  local copies, waits for them, and re-layouts: 15.2 us -> 1.51 us
  between operations: 13.2 us -> 0.39 us
  other arithmetic: 4.95 us -> 0.72 us
    all_gather x4 -> x0, waiting for transfers between devices: 161 us -> none  [the longest x1 80.8 us: on_device(): value_part = lax.all_gather(value_flat, 'seq', axis=1, tiled=True)]
    reduce_scatter x1 -> x0, waiting for transfers between devices: 69.3 us -> none  [on_device(): lax.psum_scatter(update_terms.astype(jnp.bfloat16), ('segment', 'mp'), sc...]
    ppermute x2 -> x20, starting transfers between devices: 5.81 us -> 45.4 us  [the longest x6 21.1 us: along_seq(): return lax.ppermute(array, ('segment', 'seq'), pairs)]
    pallas_call x0 -> x9, Pallas kernels: none -> 27.4 us  [call(): pl.pallas_call(kernel, out_shape=out_shapes, in_specs=specs, out_specs=ou...]
    ppermute x2 -> x20, waiting for transfers between devices: 45.3 us -> 60.6 us  [the longest x1 25.2 us: on_device(): received = lax.ppermute(done[0], 'segment', pairs)]
    dot_general x2 -> x0, matrix products: 14 us -> none  [the longest x1 9.4 us: encode(): jnp.dot(normed, second_weight, preferred_element_type=jnp.float32)]
    squeeze x1 -> x3, local copies, waits for them, and re-layouts: 12 us -> 1.4 us  [the longest x1 1.31 us: on_device(): mem_docs = [memory[b] for b in range(docs)]]
  transfers between devices with their start and end apart: 7 -> 20, of which waited for: 6 -> 7; matrix products, arithmetic and copies ran while one was open for 9% -> 0% of each run, Pallas kernels for 0% -> 13%
where the time goes in v1:
time: 137 us; the launch traced here: 136 us
  waiting for transfers between devices  60.6 us (44%)
  starting transfers between devices  45.4 us (33%)
  Pallas kernels  27.4 us (20%)
  local copies, waits for them, and re-layouts  1.51 us (1%)
    pallas_call x9, Pallas kernels, call(): pl.pallas_call(kernel, out_shape=out_shapes, in_specs=specs, out_specs=ou...  27.4 us
    ppermute x1, waiting for transfers between devices, on_device(): received = lax.ppermute(done[0], 'segment', pairs)  25.2 us
    ppermute x6, starting transfers between devices, along_seq(): return lax.ppermute(array, ('segment', 'seq'), pairs)  21.1 us
    ppermute x6, waiting for transfers between devices, along_seq(): return lax.ppermute(array, ('segment', 'seq'), pairs)  20.5 us
    ppermute x11, starting transfers between devices, in_section(): return lax.ppermute(array, ('segment', 'mp'), pairs)  20.4 us
    ppermute x11, waiting for transfers between devices, in_section(): return lax.ppermute(array, ('segment', 'mp'), pairs)  8.21 us
    ppermute x1, waiting for transfers between devices, on_device(): context = lax.ppermute(context, 'segment', [(0, 1)])  5.14 us
  transfers between devices with their start and end apart: 20, of which 7 were waited for; matrix products, arithmetic and copies ran while one was open for 0% of the time, Pallas kernels for 13%

profile of v1, /device:TPU:0, one launch (start us, length us, event | category | flops | bytes accessed | tf_op | source)
XLA Modules:
  0.0 136.0 jit_solution(5080176238660530593)
XLA Ops:
  0.0 0.0 copy-start
  0.0 0.0 copy-start.2
  0.0 1.3 slice_bitcast_fusion
  1.3 4.9 %collective-permute-start.11 = (bf16[256,1024]{1,0:T(8,128)(2,1)S(1)}, bf16[256,1024]{1,0:T(8,128)(2,1)S(1)}, u32[]{:S(2)}, u32[]{:S(2)}) collective-permute-start(bf16[256,1024]{1,0:T(8,128)(2,1)S(1)} %get-tuple-element.21.x0), channel_id=1, source_target_pairs={{0,2},{1,3},{2,0},{3,1},{4,6},{5,7},{6,4},{7,5},{8,10},{9,11},{10,... | collective-permute-start | bytes 1572872 | tf_op jit(solution)/shard_map/ppermute | solution.py:279
  6.2 0.0 copy-done
  6.2 1.4 %collective-permute-start.1 = (bf16[128,1024]{1,0:T(8,128)(2,1)S(1)}, bf16[128,1024]{1,0:T(8,128)(2,1)}, u32[]{:S(2)}, u32[]{:S(2)}) collective-permute-start(bf16[128,1024]{1,0:T(8,128)(2,1)S(1)} %bitcast.29), channel_id=1, source_target_pairs={{16,18},{17,19},{18,16},{19,17},{20,22},{21,23},{22,20},{23,21},{2... | collective-permute-start | bytes 786440 | tf_op jit(solution)/shard_map/ppermute | solution.py:279
  7.6 1.9 %collective-permute-start.8 = (bf16[256,1024]{1,0:T(8,128)(2,1)S(1)}, bf16[256,1024]{1,0:T(8,128)(2,1)S(1)}, u32[]{:S(2)}, u32[]{:S(2)}) collective-permute-start(bf16[256,1024]{1,0:T(8,128)(2,1)S(1)} %get-tuple-element.22.x0), channel_id=1, source_target_pairs={{0,2},{1,3},{2,0},{3,1},{4,6},{5,7},{6,4},{7,5},{8,10},{9,11},{10,... | collective-permute-start | bytes 1572872 | tf_op jit(solution)/shard_map/ppermute | solution.py:279
  9.5 1.4 %collective-permute-start = (bf16[128,1024]{1,0:T(8,128)(2,1)S(1)}, bf16[128,1024]{1,0:T(8,128)(2,1)}, u32[]{:S(2)}, u32[]{:S(2)}) collective-permute-start(bf16[128,1024]{1,0:T(8,128)(2,1)S(1)} %bitcast.30), channel_id=1, source_target_pairs={{16,17},{17,16},{18,19},{19,18},{20,21},{21,20},{22,23},{23,22},{2... | collective-permute-start | bytes 786440 | tf_op jit(solution)/shard_map/ppermute | solution.py:279
  10.9 0.0 collective-permute-done.1.x2
  10.9 1.4 collective-permute-start.2
  12.2 1.9 %collective-permute-start.10 = (bf16[256,1024]{1,0:T(8,128)(2,1)S(1)}, bf16[256,1024]{1,0:T(8,128)(2,1)S(1)}, u32[]{:S(2)}, u32[]{:S(2)}) collective-permute-start(bf16[256,1024]{1,0:T(8,128)(2,1)S(1)} %get-tuple-element.21.x0), channel_id=1, source_target_pairs={{0,1},{1,0},{2,3},{3,2},{4,5},{5,4},{6,7},{7,6},{8,9},{9,8},{10,11... | collective-permute-start | bytes 1572872 | tf_op jit(solution)/shard_map/ppermute | solution.py:279
  14.1 4.8 %collective-permute-done.11.x2 = bf16[256,1024]{1,0:T(8,128)(2,1)S(1)} collective-permute-done((bf16[256,1024]{1,0:T(8,128)(2,1)S(1)}, bf16[256,1024]{1,0:T(8,128)(2,1)S(1)}, u32[]{:S(2)}, u32[]{:S(2)}) %collective-permute-start.11) | collective-permute-done | bytes 524320 | tf_op jit(solution)/shard_map/ppermute | solution.py:279
  18.9 1.9 %collective-permute-start.12 = (bf16[256,1024]{1,0:T(8,128)(2,1)S(1)}, bf16[256,1024]{1,0:T(8,128)(2,1)S(1)}, u32[]{:S(2)}, u32[]{:S(2)}) collective-permute-start(bf16[256,1024]{1,0:T(8,128)(2,1)S(1)} %collective-permute-done.11.x2), channel_id=1, source_target_pairs={{0,1},{1,0},{2,3},{3,2},{4,5},{5,4},{6,7},{7,6},{8,9},{9,8},{10,11... | collective-permute-start | bytes 1572872 | tf_op jit(solution)/shard_map/ppermute | solution.py:279
  20.9 0.0 copy-done.2
  21.0 0.1 stack.39.info
  21.1 0.0 collective-permute-done.x1
  21.1 0.0 collective-permute-done.2.x3
  21.1 1.2 shard_map.55
  22.2 1.3 collective-permute-start.3
  23.5 2.4 %collective-permute-start.7 = (bf16[256,1024]{1,0:T(8,128)(2,1)S(1)}, bf16[256,1024]{1,0:T(8,128)(2,1)S(1)}, u32[]{:S(2)}, u32[]{:S(2)}) collective-permute-start(bf16[256,1024]{1,0:T(8,128)(2,1)S(1)} %get-tuple-element.22.x0), channel_id=1, source_target_pairs={{0,1},{1,0},{2,3},{3,2},{4,5},{5,4},{6,7},{7,6},{8,9},{9,8},{10,11... | collective-permute-start | bytes 1572872 | tf_op jit(solution)/shard_map/ppermute | solution.py:279
  26.0 3.4 %collective-permute-done.8.x2 = bf16[256,1024]{1,0:T(8,128)(2,1)S(1)} collective-permute-done((bf16[256,1024]{1,0:T(8,128)(2,1)S(1)}, bf16[256,1024]{1,0:T(8,128)(2,1)S(1)}, u32[]{:S(2)}, u32[]{:S(2)}) %collective-permute-start.8) | collective-permute-done | bytes 524320 | tf_op jit(solution)/shard_map/ppermute | solution.py:279
  29.3 1.9 %collective-permute-start.9 = (bf16[256,1024]{1,0:T(8,128)(2,1)S(1)}, bf16[256,1024]{1,0:T(8,128)(2,1)S(1)}, u32[]{:S(2)}, u32[]{:S(2)}) collective-permute-start(bf16[256,1024]{1,0:T(8,128)(2,1)S(1)} %collective-permute-done.8.x2), channel_id=1, source_target_pairs={{0,1},{1,0},{2,3},{3,2},{4,5},{5,4},{6,7},{7,6},{8,9},{9,8},{10,11... | collective-permute-start | bytes 1572872 | tf_op jit(solution)/shard_map/ppermute | solution.py:279
  31.3 1.6 %collective-permute-done.3.refs_0_ = bf16[128,1024]{1,0:T(8,128)(2,1)S(1)} collective-permute-done((bf16[128,1024]{1,0:T(8,128)(2,1)S(1)}, bf16[128,1024]{1,0:T(8,128)(2,1)S(1)}, u32[]{:S(2)}, u32[]{:S(2)}) %collective-permute-start.3) | collective-permute-done | bytes 262176 | tf_op jit(solution)/shard_map/ppermute | solution.py:306
  32.8 4.0 %collective-permute-start.4 = (bf16[128,1024]{1,0:T(8,128)(2,1)S(1)}, bf16[128,1024]{1,0:T(8,128)(2,1)S(1)}, u32[]{:S(2)}, u32[]{:S(2)}) collective-permute-start(bf16[128,1024]{1,0:T(8,128)(2,1)S(1)} %collective-permute-done.3.refs_0_), channel_id=1, source_target_pairs={{0,4},{4,8},{8,12},{12,0},{1,5},{5,9},{9,13},{13,1},{2,6},{6,10},{... | collective-permute-start | bytes 786440 | tf_op jit(solution)/shard_map/ppermute | solution.py:283
  36.9 0.0 collective-permute-done.10.x1
  36.9 4.5 %collective-permute-start.5 = (bf16[128,1024]{1,0:T(8,128)(2,1)S(1)}, bf16[128,1024]{1,0:T(8,128)(2,1)S(1)}, u32[]{:S(2)}, u32[]{:S(2)}) collective-permute-start(bf16[128,1024]{1,0:T(8,128)(2,1)S(1)} %collective-permute-done.3.refs_0_), channel_id=1, source_target_pairs={{0,8},{4,12},{8,0},{12,4},{1,9},{5,13},{9,1},{13,5},{2,10},{6,14},... | collective-permute-start | bytes 786440 | tf_op jit(solution)/shard_map/ppermute | solution.py:283
  41.4 0.0 collective-permute-done.12.x3
  41.4 3.3 %collective-permute-start.6 = (bf16[128,1024]{1,0:T(8,128)(2,1)S(1)}, bf16[128,1024]{1,0:T(8,128)(2,1)S(1)}, u32[]{:S(2)}, u32[]{:S(2)}) collective-permute-start(bf16[128,1024]{1,0:T(8,128)(2,1)S(1)} %collective-permute-done.3.refs_0_), channel_id=1, source_target_pairs={{0,12},{4,0},{8,4},{12,8},{1,13},{5,1},{9,5},{13,9},{2,14},{6,2},{... | collective-permute-start | bytes 786440 | tf_op jit(solution)/shard_map/ppermute | solution.py:283
  44.6 7.8 %shard_map.57 = (bf16[256,1024]{1,0:T(8,128)(2,1)S(1)}, bf16[256,1024]{1,0:T(8,128)(2,1)S(1)}) custom-call(s32[9]{0:T(128)S(1)} %stack.39.info, bf16[256,1024]{1,0:T(8,128)(2,1)S(1)} %get-tuple-element.21.x0, bf16[256,1024]{1,0:T(8,128)(2,1)S(1)} %collective-permute-done.10.x1, bf16[256,1024]{1,0:T(8,128)(2,1)S(1)} %collective-permute-done.11.x2, ...), custom_call_target="tpu_custom_call" | custom-call | flops 4294967296 | bytes 16777216 | tf_op jit(solution)/shard_map/pallas_call | solution.py:249
  52.4 0.0 copy-start.1
  52.4 0.0 collective-permute-done.7.x1
  52.5 0.0 collective-permute-done.9.x3
  52.5 8.0 %shard_map.56 = (bf16[256,1024]{1,0:T(8,128)(2,1)S(1)}, bf16[256,1024]{1,0:T(8,128)(2,1)S(1)}) custom-call(s32[9]{0:T(128)S(1)} %stack.39.info, bf16[256,1024]{1,0:T(8,128)(2,1)S(1)} %get-tuple-element.22.x0, bf16[256,1024]{1,0:T(8,128)(2,1)S(1)} %collective-permute-done.7.x1, bf16[256,1024]{1,0:T(8,128)(2,1)S(1)} %collective-permute-done.8.x2, ...), custom_call_target="tpu_custom_call" | custom-call | flops 4294967296 | bytes 16777216 | tf_op jit(solution)/shard_map/pallas_call | solution.py:249
  60.4 0.0 collective-permute-done.4.refs_1_
  60.4 0.0 collective-permute-done.5.refs_2_
  60.4 0.0 collective-permute-done.6.refs_3_
  60.5 0.0 copy-done.1
  60.5 7.4 %shard_map.58 = bf16[4,4,272,128]{3,2,1,0:T(8,128)(2,1)S(1)} custom-call(s32[9]{0:T(128)S(1)} %stack.39.info, s32[2]{0:T(128)S(1)} %copy-done.1, bf16[128,1024]{1,0:T(8,128)(2,1)S(1)} %collective-permute-done.3.refs_0_, bf16[128,1024]{1,0:T(8,128)(2,1)S(1)} %collective-permute-done.4.refs_1_, bf16[128,1024]{1,0:T(8,128)(2,1)S(1)} %collective-permute-done.5.refs_2_, ...), custom_call_target="tpu_custom_call" | custom-call | flops 1073741824 | bytes 2097152 | tf_op jit(solution)/shard_map/pallas_call | solution.py:249
  67.8 0.1 slice_bitcast_fusion.2
  67.9 4.9 %collective-permute-start.13 = (bf16[4,272,128]{2,1,0:T(8,128)(2,1)S(1)}, bf16[4,272,128]{2,1,0:T(8,128)(2,1)S(1)}, u32[]{:S(2)}, u32[]{:S(2)}) collective-permute-start(bf16[4,272,128]{2,1,0:T(8,128)(2,1)S(1)} %get-tuple-element.19), channel_id=1, source_target_pairs={{0,12},{4,0},{8,4},{12,8},{1,13},{5,1},{9,5},{13,9},{2,14},{6,2},{... | collective-permute-start | bytes 835592 | tf_op jit(solution)/shard_map/ppermute | solution.py:283
  72.9 2.4 %collective-permute-start.14 = (bf16[4,272,128]{2,1,0:T(8,128)(2,1)S(1)}, bf16[4,272,128]{2,1,0:T(8,128)(2,1)S(1)}, u32[]{:S(2)}, u32[]{:S(2)}) collective-permute-start(bf16[4,272,128]{2,1,0:T(8,128)(2,1)S(1)} %get-tuple-element.18), channel_id=1, source_target_pairs={{0,8},{4,12},{8,0},{12,4},{1,9},{5,13},{9,1},{13,5},{2,10},{6,14},... | collective-permute-start | bytes 835592 | tf_op jit(solution)/shard_map/ppermute | solution.py:283
  75.3 2.0 %collective-permute-start.15 = (bf16[4,272,128]{2,1,0:T(8,128)(2,1)S(1)}, bf16[4,272,128]{2,1,0:T(8,128)(2,1)S(1)}, u32[]{:S(2)}, u32[]{:S(2)}) collective-permute-start(bf16[4,272,128]{2,1,0:T(8,128)(2,1)S(1)} %get-tuple-element.17), channel_id=1, source_target_pairs={{0,4},{4,8},{8,12},{12,0},{1,5},{5,9},{9,13},{13,1},{2,6},{6,10},{... | collective-permute-start | bytes 835592 | tf_op jit(solution)/shard_map/ppermute | solution.py:283
  77.3 2.7 %collective-permute-done.13.refs_1_ = bf16[4,272,128]{2,1,0:T(8,128)(2,1)S(1)} collective-permute-done((bf16[4,272,128]{2,1,0:T(8,128)(2,1)S(1)}, bf16[4,272,128]{2,1,0:T(8,128)(2,1)S(1)}, u32[]{:S(2)}, u32[]{:S(2)}) %collective-permute-start.13) | collective-permute-done | bytes 278560 | tf_op jit(solution)/shard_map/ppermute | solution.py:283
  80.0 17.8 %collective-permute-done.14.refs_2_ = bf16[4,272,128]{2,1,0:T(8,128)(2,1)S(1)} collective-permute-done((bf16[4,272,128]{2,1,0:T(8,128)(2,1)S(1)}, bf16[4,272,128]{2,1,0:T(8,128)(2,1)S(1)}, u32[]{:S(2)}, u32[]{:S(2)}) %collective-permute-start.14) | collective-permute-done | bytes 278560 | tf_op jit(solution)/shard_map/ppermute | solution.py:283
  97.8 0.0 collective-permute-done.15.refs_3_
  97.8 0.8 shard_map.59
  98.6 1.3 collective-permute-start.16
  99.9 5.1 %collective-permute-done.16.context = bf16[1024,128]{1,0:T(8,128)(2,1)S(1)} collective-permute-done((bf16[1024,128]{1,0:T(8,128)(2,1)S(1)}, bf16[1024,128]{1,0:T(8,128)(2,1)S(1)}, u32[]{:S(2)}, u32[]{:S(2)}) %collective-permute-start.16) | collective-permute-done | bytes 262176 | tf_op jit(solution)/shard_map/ppermute | solution.py:355
  105.1 0.6 shard_map.61
  105.7 0.7 collective-permute-start.17
  106.4 0.6 shard_map.60.mine
  107.0 0.0 collective-permute-done.17.other.sibling
  107.0 0.5 shard_map.62
  107.5 0.7 collective-permute-start.18
  108.2 0.0 collective-permute-done.18.across
  108.2 0.6 shard_map.63
  108.8 1.3 collective-permute-start.19
  110.1 25.2 %collective-permute-done.19 = bf16[128,512]{1,0:T(8,128)(2,1)S(1)} collective-permute-done((bf16[128,512]{1,0:T(8,128)(2,1)S(1)}, bf16[128,512]{1,0:T(8,128)(2,1)S(1)}, u32[]{:S(2)}, u32[]{:S(2)}) %collective-permute-start.19) | collective-permute-done | bytes 131104 | tf_op jit(solution)/shard_map/ppermute | solution.py:388
  135.3 0.7 fusion
  (3 shorter events, 0.1 us)
Async XLA Ops:
  0.0 6.2 %copy-start = (bf16[2,64,1024]{2,1,0:T(8,128)(2,1)S(1)}, bf16[2,64,1024]{2,1,0:T(8,128)(2,1)}, u32[]{:S(2)}) copy-start(bf16[2,64,1024]{2,1,0:T(8,128)(2,1)} %param.6) | copy-start | bytes 786436
  0.0 20.9 %copy-start.2 = (bf16[1,4096]{1,0:T(2,128)(2,1)S(1)}, bf16[1,4096]{1,0:T(2,128)(2,1)}, u32[]{:S(2)}) copy-start(bf16[1,4096]{1,0:T(2,128)(2,1)} %param.7) | copy-start | bytes 24580
  1.3 17.6 %collective-permute-start.11 = (bf16[256,1024]{1,0:T(8,128)(2,1)S(1)}, bf16[256,1024]{1,0:T(8,128)(2,1)S(1)}, u32[]{:S(2)}, u32[]{:S(2)}) collective-permute-start(bf16[256,1024]{1,0:T(8,128)(2,1)S(1)} %get-tuple-element.21.x0), channel_id=1, source_target_pairs={{0,2},{1,3},{2,0},{3,1},{4,6},{5,7},{6,4},{7,5},{8,10},{9,11},{10,... | collective-permute-start | bytes 1572872 | tf_op jit(solution)/shard_map/ppermute | solution.py:279
  6.2 4.7 %collective-permute-start.1 = (bf16[128,1024]{1,0:T(8,128)(2,1)S(1)}, bf16[128,1024]{1,0:T(8,128)(2,1)}, u32[]{:S(2)}, u32[]{:S(2)}) collective-permute-start(bf16[128,1024]{1,0:T(8,128)(2,1)S(1)} %bitcast.29), channel_id=1, source_target_pairs={{16,18},{17,19},{18,16},{19,17},{20,22},{21,23},{22,20},{23,21},{2... | collective-permute-start | bytes 786440 | tf_op jit(solution)/shard_map/ppermute | solution.py:279
  7.6 21.8 %collective-permute-start.8 = (bf16[256,1024]{1,0:T(8,128)(2,1)S(1)}, bf16[256,1024]{1,0:T(8,128)(2,1)S(1)}, u32[]{:S(2)}, u32[]{:S(2)}) collective-permute-start(bf16[256,1024]{1,0:T(8,128)(2,1)S(1)} %get-tuple-element.22.x0), channel_id=1, source_target_pairs={{0,2},{1,3},{2,0},{3,1},{4,6},{5,7},{6,4},{7,5},{8,10},{9,11},{10,... | collective-permute-start | bytes 1572872 | tf_op jit(solution)/shard_map/ppermute | solution.py:279
  9.5 11.6 %collective-permute-start = (bf16[128,1024]{1,0:T(8,128)(2,1)S(1)}, bf16[128,1024]{1,0:T(8,128)(2,1)}, u32[]{:S(2)}, u32[]{:S(2)}) collective-permute-start(bf16[128,1024]{1,0:T(8,128)(2,1)S(1)} %bitcast.30), channel_id=1, source_target_pairs={{16,17},{17,16},{18,19},{19,18},{20,21},{21,20},{22,23},{23,22},{2... | collective-permute-start | bytes 786440 | tf_op jit(solution)/shard_map/ppermute | solution.py:279
  10.9 10.2 %collective-permute-start.2 = (bf16[128,1024]{1,0:T(8,128)(2,1)}, bf16[128,1024]{1,0:T(8,128)(2,1)}, u32[]{:S(2)}, u32[]{:S(2)}) collective-permute-start(bf16[128,1024]{1,0:T(8,128)(2,1)} %collective-permute-done.1.x2), channel_id=1, source_target_pairs={{16,17},{17,16},{18,19},{19,18},{20,21},{21,20},{22,23},{23,22},{2... | collective-permute-start | bytes 786440 | tf_op jit(solution)/shard_map/ppermute | solution.py:279
  12.2 24.6 %collective-permute-start.10 = (bf16[256,1024]{1,0:T(8,128)(2,1)S(1)}, bf16[256,1024]{1,0:T(8,128)(2,1)S(1)}, u32[]{:S(2)}, u32[]{:S(2)}) collective-permute-start(bf16[256,1024]{1,0:T(8,128)(2,1)S(1)} %get-tuple-element.21.x0), channel_id=1, source_target_pairs={{0,1},{1,0},{2,3},{3,2},{4,5},{5,4},{6,7},{7,6},{8,9},{9,8},{10,11... | collective-permute-start | bytes 1572872 | tf_op jit(solution)/shard_map/ppermute | solution.py:279
  18.9 22.4 %collective-permute-start.12 = (bf16[256,1024]{1,0:T(8,128)(2,1)S(1)}, bf16[256,1024]{1,0:T(8,128)(2,1)S(1)}, u32[]{:S(2)}, u32[]{:S(2)}) collective-permute-start(bf16[256,1024]{1,0:T(8,128)(2,1)S(1)} %collective-permute-done.11.x2), channel_id=1, source_target_pairs={{0,1},{1,0},{2,3},{3,2},{4,5},{5,4},{6,7},{7,6},{8,9},{9,8},{10,11... | collective-permute-start | bytes 1572872 | tf_op jit(solution)/shard_map/ppermute | solution.py:279
  22.2 10.6 %collective-permute-start.3 = (bf16[128,1024]{1,0:T(8,128)(2,1)S(1)}, bf16[128,1024]{1,0:T(8,128)(2,1)S(1)}, u32[]{:S(2)}, u32[]{:S(2)}) collective-permute-start(bf16[128,1024]{1,0:T(8,128)(2,1)S(1)} %get-tuple-element.11), channel_id=1, source_target_pairs={{16,0},{17,1},{18,2},{19,3},{20,4},{21,5},{22,6},{23,7},{24,8},{25... | collective-permute-start | bytes 786440 | tf_op jit(solution)/shard_map/ppermute | solution.py:306
  23.5 28.9 %collective-permute-start.7 = (bf16[256,1024]{1,0:T(8,128)(2,1)S(1)}, bf16[256,1024]{1,0:T(8,128)(2,1)S(1)}, u32[]{:S(2)}, u32[]{:S(2)}) collective-permute-start(bf16[256,1024]{1,0:T(8,128)(2,1)S(1)} %get-tuple-element.22.x0), channel_id=1, source_target_pairs={{0,1},{1,0},{2,3},{3,2},{4,5},{5,4},{6,7},{7,6},{8,9},{9,8},{10,11... | collective-permute-start | bytes 1572872 | tf_op jit(solution)/shard_map/ppermute | solution.py:279
  29.3 23.1 %collective-permute-start.9 = (bf16[256,1024]{1,0:T(8,128)(2,1)S(1)}, bf16[256,1024]{1,0:T(8,128)(2,1)S(1)}, u32[]{:S(2)}, u32[]{:S(2)}) collective-permute-start(bf16[256,1024]{1,0:T(8,128)(2,1)S(1)} %collective-permute-done.8.x2), channel_id=1, source_target_pairs={{0,1},{1,0},{2,3},{3,2},{4,5},{5,4},{6,7},{7,6},{8,9},{9,8},{10,11... | collective-permute-start | bytes 1572872 | tf_op jit(solution)/shard_map/ppermute | solution.py:279
  32.8 27.6 %collective-permute-start.4 = (bf16[128,1024]{1,0:T(8,128)(2,1)S(1)}, bf16[128,1024]{1,0:T(8,128)(2,1)S(1)}, u32[]{:S(2)}, u32[]{:S(2)}) collective-permute-start(bf16[128,1024]{1,0:T(8,128)(2,1)S(1)} %collective-permute-done.3.refs_0_), channel_id=1, source_target_pairs={{0,4},{4,8},{8,12},{12,0},{1,5},{5,9},{9,13},{13,1},{2,6},{6,10},{... | collective-permute-start | bytes 786440 | tf_op jit(solution)/shard_map/ppermute | solution.py:283
  36.9 23.6 %collective-permute-start.5 = (bf16[128,1024]{1,0:T(8,128)(2,1)S(1)}, bf16[128,1024]{1,0:T(8,128)(2,1)S(1)}, u32[]{:S(2)}, u32[]{:S(2)}) collective-permute-start(bf16[128,1024]{1,0:T(8,128)(2,1)S(1)} %collective-permute-done.3.refs_0_), channel_id=1, source_target_pairs={{0,8},{4,12},{8,0},{12,4},{1,9},{5,13},{9,1},{13,5},{2,10},{6,14},... | collective-permute-start | bytes 786440 | tf_op jit(solution)/shard_map/ppermute | solution.py:283
  41.4 19.1 %collective-permute-start.6 = (bf16[128,1024]{1,0:T(8,128)(2,1)S(1)}, bf16[128,1024]{1,0:T(8,128)(2,1)S(1)}, u32[]{:S(2)}, u32[]{:S(2)}) collective-permute-start(bf16[128,1024]{1,0:T(8,128)(2,1)S(1)} %collective-permute-done.3.refs_0_), channel_id=1, source_target_pairs={{0,12},{4,0},{8,4},{12,8},{1,13},{5,1},{9,5},{13,9},{2,14},{6,2},{... | collective-permute-start | bytes 786440 | tf_op jit(solution)/shard_map/ppermute | solution.py:283
  52.4 8.0 %copy-start.1 = (s32[2]{0:T(128)S(1)}, s32[2]{0:T(128)}, u32[]{:S(2)}) copy-start(s32[2]{0:T(128)} %lengths.1) | copy-start | bytes 28
  67.9 12.1 %collective-permute-start.13 = (bf16[4,272,128]{2,1,0:T(8,128)(2,1)S(1)}, bf16[4,272,128]{2,1,0:T(8,128)(2,1)S(1)}, u32[]{:S(2)}, u32[]{:S(2)}) collective-permute-start(bf16[4,272,128]{2,1,0:T(8,128)(2,1)S(1)} %get-tuple-element.19), channel_id=1, source_target_pairs={{0,12},{4,0},{8,4},{12,8},{1,13},{5,1},{9,5},{13,9},{2,14},{6,2},{... | collective-permute-start | bytes 835592 | tf_op jit(solution)/shard_map/ppermute | solution.py:283
  72.9 24.9 %collective-permute-start.14 = (bf16[4,272,128]{2,1,0:T(8,128)(2,1)S(1)}, bf16[4,272,128]{2,1,0:T(8,128)(2,1)S(1)}, u32[]{:S(2)}, u32[]{:S(2)}) collective-permute-start(bf16[4,272,128]{2,1,0:T(8,128)(2,1)S(1)} %get-tuple-element.18), channel_id=1, source_target_pairs={{0,8},{4,12},{8,0},{12,4},{1,9},{5,13},{9,1},{13,5},{2,10},{6,14},... | collective-permute-start | bytes 835592 | tf_op jit(solution)/shard_map/ppermute | solution.py:283
  75.3 22.5 %collective-permute-start.15 = (bf16[4,272,128]{2,1,0:T(8,128)(2,1)S(1)}, bf16[4,272,128]{2,1,0:T(8,128)(2,1)S(1)}, u32[]{:S(2)}, u32[]{:S(2)}) collective-permute-start(bf16[4,272,128]{2,1,0:T(8,128)(2,1)S(1)} %get-tuple-element.17), channel_id=1, source_target_pairs={{0,4},{4,8},{8,12},{12,0},{1,5},{5,9},{9,13},{13,1},{2,6},{6,10},{... | collective-permute-start | bytes 835592 | tf_op jit(solution)/shard_map/ppermute | solution.py:283
  98.6 6.5 %collective-permute-start.16 = (bf16[1024,128]{1,0:T(8,128)(2,1)S(1)}, bf16[1024,128]{1,0:T(8,128)(2,1)S(1)}, u32[]{:S(2)}, u32[]{:S(2)}) collective-permute-start(bf16[1024,128]{1,0:T(8,128)(2,1)S(1)} %shard_map.59), channel_id=1, source_target_pairs={{0,16},{1,17},{2,18},{3,19},{4,20},{5,21},{6,22},{7,23},{8,24},{9,... | collective-permute-start | bytes 786440 | tf_op jit(solution)/shard_map/ppermute | solution.py:355
  105.7 1.3 collective-permute-start.17
  107.5 0.7 collective-permute-start.18
  108.8 26.5 %collective-permute-start.19 = (bf16[128,512]{1,0:T(8,128)(2,1)S(1)}, bf16[128,512]{1,0:T(8,128)(2,1)S(1)}, u32[]{:S(2)}, u32[]{:S(2)}) collective-permute-start(bf16[128,512]{1,0:T(8,128)(2,1)S(1)} %slice_bitcast_fusion.7), channel_id=1, source_target_pairs={{16,0},{17,1},{18,2},{19,3},{20,4},{21,5},{22,6},{23,7},{24,8},{25... | collective-permute-start | bytes 393224 | tf_op jit(solution)/shard_map/ppermute | solution.py:388

commit v2 on v0

v2 whole, which is shorter than its diff:
```python
import functools

import jax
import jax.numpy as jnp
from jax import lax
from jax.experimental import pallas as pl
from jax.experimental.pallas import tpu as pltpu
from jax.sharding import PartitionSpec as P

DKV = 64
norm_eps = 1e-06
masked_score = -1e30
PAIR = 2 * DKV
LANES = 128
STAT_LANES = 128
CHUNKS = 8
IN_FLIGHT = 99
VMEM = pl.BlockSpec(memory_space=pltpu.VMEM)
SMEM = pl.BlockSpec(memory_space=pltpu.SMEM)
ANY = pl.BlockSpec(memory_space=pl.ANY)
f32 = jnp.float32
bf16 = jnp.bfloat16


def params():
    return pltpu.CompilerParams(vmem_limit_bytes=44 * 1024 * 1024)


def position():
    m = lax.axis_index("mp")
    return (
        lax.axis_index("segment"),
        lax.axis_index("seq"),
        m,
        m ^ 1,
        m ^ 2,
        m ^ 3,
        m & 1,
        m ^ (m >> 1),
        m ^ (2 + (m >> 1)),
    )


def squares(parts):
    return sum(jnp.sum(jnp.square(part.astype(f32)), axis=1, keepdims=True) for part in parts)


def gained(rows, inverse, gains, block):
    width = rows.shape[1]
    gain = gains[:, pl.ds(pl.multiple_of(block * width, width), width)].astype(f32)
    return (rows.astype(f32) * inverse * gain).astype(bf16)


class WeightStream:
    def __init__(self, weights, order, width, wbuf, sem):
        height = wbuf.shape[1]
        self.copies = [
            pltpu.make_async_copy(
                weights.at[0, which, pl.ds(block * width + start, height), :],
                wbuf.at[i],
                sem.at[i],
            )
            for i, (which, block, start) in enumerate(
                (which, block, start)
                for which, block in order
                for start in range(0, width, height)
            )
        ]
        self.wbuf = wbuf
        self.started = self.used = 0
        for _ in range(IN_FLIGHT):
            self.start()

    def start(self):
        if self.started < len(self.copies):
            self.copies[self.started].start()
            self.started += 1

    def product(self, rows):
        height = self.wbuf.shape[1]
        total = None
        for start in range(0, rows.shape[1], height):
            self.copies[self.used].wait()
            self.start()
            term = jnp.dot(
                rows[:, start : start + height], self.wbuf[self.used], preferred_element_type=f32
            )
            total = term if total is None else total + term
            self.used += 1
        return total


def normed_rows(parts, gains, blocks):
    inverse = lax.rsqrt(squares(parts) / gains.shape[1] + norm_eps)
    return [gained(part, inverse, gains, block) for part, block in zip(parts, blocks)]


def streamed_product(rows, stream):
    return sum(stream.product(part) for part in rows)


def near_copy_kernel(dec, gains, dec_out, gains_out):
    dec_out[...] = dec[...]
    gains_out[...] = gains[...]


def query_kernel(x0, x1, x2, x3, gains, weights, first_out, second_out, res, wbuf, sem):
    info = position()
    blocks = info[2:6]
    rows_each = first_out.shape[0]

    @pl.when(info[0] == 1)
    def _():
        stream = WeightStream(weights, [(0, block) for block in blocks], x0.shape[1], wbuf, sem)
        half = res.shape[1] // 2
        offset = pl.multiple_of(info[6] * half, half)
        for k, part in enumerate((x0, x1, x2, x3)):
            for side in range(2):

                @pl.when(info[7 + side] == k)
                def _():
                    res[:, side * half : (side + 1) * half] = part[:, pl.ds(offset, half)]

        parts = (x0[...], x1[...], x2[...], x3[...])
        total = streamed_product(normed_rows(parts, gains, blocks), stream)
        first_out[...] = total[:rows_each].astype(bf16)
        second_out[...] = total[rows_each:].astype(bf16)


def memory_kernel(doc, matrices, x0, x1, x2, x3, gains, weights, out, wbuf, sem):
    info = position()
    blocks = info[2:6]
    span = x2.shape[0]
    here = slice(doc * span, (doc + 1) * span)

    @pl.when(info[0] == 0)
    def _():
        order = [(which, block) for which in matrices for block in blocks]
        stream = WeightStream(weights, order, x2.shape[1], wbuf, sem)
        parts = (x0[here], x1[here], x2[...], x3[...])
        rows = normed_rows(parts, gains, blocks)
        for i in range(len(matrices)):
            out[i] = streamed_product(rows, stream).astype(bf16)


def attention_kernel(count, lengths, *refs):
    info = position()
    for side in range(2):

        @pl.when(info[0] == side)
        def _():
            attend(
                lengths[1 - side],
                info[1],
                refs[:count],
                refs[count + side],
                refs[count + 2 :],
            )


def attend(length, seq, q_refs, key_values, outs):
    count = len(q_refs)
    keys, values = (key_values.at[0], key_values.at[1])
    span = keys.shape[0]
    pos, head_width = q_refs[0].shape
    group = min(4, count)
    rows_here = group * pos
    first = seq * span
    lane = lax.broadcasted_iota(jnp.int32, (1, PAIR), 1)
    low = lane < DKV
    valid = first + lax.broadcasted_iota(jnp.int32, (1, span), 1) < length
    for base in range(0, count, group):
        stats = jnp.zeros((rows_here, STAT_LANES), f32)
        for pair in range(head_width // PAIR):
            cols = slice(pair * PAIR, (pair + 1) * PAIR)
            rows = jnp.concatenate([q_refs[base + j][:, cols] for j in range(group)], axis=0)
            zero = jnp.zeros_like(rows)
            both = jnp.concatenate(
                [jnp.where(low, rows, zero), jnp.where(low, zero, rows)], axis=0
            )
            scores = lax.dot_general(
                both, keys[:, cols], (((1,), (1,)), ((), ())), preferred_element_type=f32
            )
            masked = jnp.where(valid, scores, masked_score)
            top = jnp.max(masked, axis=1, keepdims=True)
            probs = jnp.exp(masked - top)
            total = jnp.sum(probs, axis=1, keepdims=True)
            summed = jnp.dot(probs.astype(bf16), values[:, cols], preferred_element_type=f32)
            scaled = summed * (1.0 / total)
            lse = jnp.where(first < length, top + jnp.log(total), masked_score)
            context = jnp.where(low, scaled[:rows_here], scaled[rows_here:]).astype(bf16)
            for j in range(group):
                outs[base + j][:, cols] = context[j * pos : (j + 1) * pos]
            stats = jnp.where(lane == 2 * pair, lse[:rows_here], stats)
            stats = jnp.where(lane == 2 * pair + 1, lse[rows_here:], stats)
        heads = head_width // DKV
        high = stats.astype(bf16).astype(f32)
        middle = (stats - high).astype(bf16).astype(f32)
        rest = stats - high - middle
        packed = high + pltpu.roll(middle, heads, 1) + pltpu.roll(rest, 2 * heads, 1)
        for j in range(group):
            outs[base + j][:, head_width:] = packed[j * pos : (j + 1) * pos].astype(bf16)


def combine_kernel(*refs):
    sources, out = (refs[:-1], refs[-1])
    head_width = out.shape[1]
    heads = head_width // DKV
    low = lax.broadcasted_iota(jnp.int32, (1, PAIR), 1) < DKV
    lses = []
    for source in sources:
        packed = source[:, head_width:].astype(f32)
        lses.append(
            packed
            + pltpu.roll(packed, STAT_LANES - heads, 1)
            + pltpu.roll(packed, STAT_LANES - 2 * heads, 1)
        )
    top = functools.reduce(jnp.maximum, lses)
    shares = [jnp.exp(lse - top) for lse in lses]
    inverse = 1.0 / sum(shares)
    shares = [share * inverse for share in shares]
    for pair in range(heads // 2):
        cols = slice(pair * PAIR, (pair + 1) * PAIR)
        context = sum(
            source[:, cols].astype(f32)
            * jnp.where(low, share[:, 2 * pair : 2 * pair + 1], share[:, 2 * pair + 1 : 2 * pair + 2])
            for source, share in zip(sources, shares)
        )
        out[:, cols] = context.astype(bf16)


def load_kernel(weights, context, out, sem):
    info = position()
    @pl.when(info[0] == 1)
    def _():
        height = out.shape[0] // 8
        copies = [
            pltpu.make_async_copy(
                weights.at[0, 1, pl.ds(i * height, height), :],
                out.at[pl.ds(i * height, height), :],
                sem.at[i],
            )
            for i in range(8)
        ]
        for copy in copies:
            copy.start()
        for copy in copies:
            copy.wait()


def project_kernel(mask, first_context, second_context, weights, out):
    info = position()
    block = out.shape[0] // 4
    targets = [(mask ^ 2, 0), (mask ^ 2, 4), (mask, 0), (mask, 4)]

    @pl.when(info[0] == 1)
    def _():
        context = jnp.concatenate([first_context[...], second_context[...]], axis=0)
        for i, (k, add) in enumerate(targets):
            start = pl.multiple_of((info[2 + k] + add) * block, block)
            out[i * block : (i + 1) * block, :] = lax.dot_general(
                weights[pl.ds(start, block), :],
                context,
                (((1,), (1,)), ((), ())),
                preferred_element_type=f32,
            ).astype(bf16)


def add_kernel(mine, other, out):
    info = position()
    @pl.when(info[0] == 1)
    def _():
        rows = out.shape[0]
        out[...] = (mine[:rows].astype(f32) + other[:rows].astype(f32)).astype(bf16)


def final_kernel(mine, sibling, across, res, *outs):
    info = position()
    @pl.when(info[0] == 1)
    def _():
        half = outs[0].shape[1]
        rows = 2 * half
        for side, out in enumerate(outs):
            part = slice(rows + side * half, rows + (side + 1) * half)
            update = (
                mine[part].astype(f32)
                + sibling[part].astype(f32)
                + across[side * half : (side + 1) * half].astype(f32)
            )
            out[...] = (res[:, side * half : (side + 1) * half].astype(f32) + update.T).astype(bf16)


def call(kernel, out_shapes, args, specs, scratch=(), out_specs=None, flops=1, **more):
    return pl.pallas_call(
        kernel,
        out_shape=out_shapes,
        in_specs=specs,
        out_specs=out_specs if out_specs is not None else jax.tree.map(lambda _: VMEM, out_shapes),
        scratch_shapes=list(scratch),
        compiler_params=params(),
        cost_estimate=pl.CostEstimate(flops=flops, bytes_accessed=1, transcendentals=0),
        **more,
    )(*args)


def on_device(memory, decoder_rows, gains, weights, lengths):
    segment = lax.axis_index("segment")
    seq = lax.axis_index("seq")
    m = lax.axis_index("mp")
    count = lax.axis_size("seq")
    docs, span, width = memory.shape
    pos = decoder_rows.shape[1]
    rows = docs * pos
    head_width = weights.shape[3]

    lengths = lengths.astype(jnp.int32)
    shape = lambda *dims: jax.ShapeDtypeStruct(dims, bf16)
    after = lax.optimization_barrier

    def in_section(array, section, mask):
        pairs = [(section * 4 + i, section * 4 + (i ^ mask)) for i in range(4)]
        return lax.ppermute(array, ("segment", "mp"), pairs)

    def along_seq(array, by):
        return lax.ppermute(array, "seq", [(i, (i + by) % count) for i in range(count)])

    def to_encoder(array):
        return lax.ppermute(array, "segment", [(1, 0)])

    def to_decoder(array):
        return lax.ppermute(array, "segment", [(0, 1)])

    dec = decoder_rows.reshape(rows, width)
    dec_y = in_section(dec, 1, 2)
    dec_c = in_section(dec, 1, 1)
    extra = span * 64 // 256
    first_rows, memory = after((memory[0], memory))
    mem = memory.reshape(docs * span, width)
    mem_y = [in_section(first_rows, 0, 2), in_section(mem[span - extra :], 0, 2)]
    mem_c = in_section(mem, 0, 1)

    def weight_scratch(matrices):
        chunks = matrices * CHUNKS
        return [
            pltpu.VMEM((chunks, 4 * width // CHUNKS, head_width), bf16),
            pltpu.SemaphoreType.DMA((chunks,)),
        ]

    dec_here, gains = call(
        near_copy_kernel, (shape(rows, width), shape(*gains.shape)), (dec, gains), [VMEM] * 2
    )
    dec_y, _ = after((dec_y, gains))
    dec_yc = in_section(dec_y, 1, 1)
    first_queries, second_queries, residual = call(
        query_kernel,
        (shape(pos, head_width), shape(pos, head_width), shape(rows, width)),
        (dec_here, dec_c, dec_y, dec_yc, gains, weights),
        [VMEM] * 5 + [ANY],
        weight_scratch(1),
    )
    q_received = to_encoder(second_queries)

    def project_memory(doc, matrices, far, far_c, cost):
        return call(
            functools.partial(memory_kernel, doc, matrices),
            shape(len(matrices), span, head_width),
            (mem, mem_c, far, far_c, gains, weights),
            [VMEM] * 5 + [ANY],
            weight_scratch(len(matrices)),
            flops=int(cost),
        )

    far, _ = after((mem_y[0], second_queries))
    far_c = in_section(far, 0, 1)
    made = project_memory(0, (0, 1), far, far_c, 1)
    first_memory = to_decoder(made)
    q_received, _ = after((q_received, made))
    far, _ = after((mem_y[1], q_received))
    far = far[extra:]
    second_memory = project_memory(1, (0, 1), far, in_section(far, 0, 1), 4.8e9)

    encoding = segment == 0
    q_pieces = [jnp.where(encoding, q_received, first_queries)]
    for by in range(1, count):
        q_pieces.append(along_seq(q_pieces[0], by))

    partial = call(
        functools.partial(attention_kernel, count),
        (shape(pos, head_width + STAT_LANES),) * count,
        (lengths, *q_pieces, second_memory, first_memory),
        [SMEM] + [VMEM] * (count + 2),
    )
    sources = [partial[0]] + [along_seq(partial[by], -by) for by in range(1, count)]
    context = call(
        combine_kernel,
        shape(pos, head_width),
        tuple(sources),
        [VMEM] * count,
    )
    second_context = to_decoder(context)

    last_weights = call(
        load_kernel,
        shape(4 * width, head_width),
        (weights, context),
        [ANY, ANY],
        [pltpu.SemaphoreType.DMA((8,))],
    )
    block = 4 * width // 8

    def project(mask):
        return call(
            functools.partial(project_kernel, mask),
            shape(4 * block, rows),
            (context, second_context, last_weights),
            [VMEM, VMEM, VMEM],
        )

    for_sibling = project(1)
    sibling = in_section(for_sibling, 1, 1)
    mine = project(0)
    for_across = call(
        add_kernel,
        shape(2 * block, rows),
        (mine, sibling),
        [VMEM, VMEM],
    )
    across = in_section(for_across, 1, 2)
    for_encoder, own = call(
        final_kernel,
        (shape(rows, block), shape(rows, block)),
        (mine, sibling, across, residual),
        [VMEM, VMEM, VMEM, VMEM],
    )
    received = to_encoder(for_encoder)
    decoder_out = jnp.where(encoding, received, own)
    return decoder_out.reshape(docs, pos, block)


def solution(mesh):
    in_specs = (
        P(None, "seq", "mp"),
        P(None, "seq", "mp"),
        P("segment", None),
        P("segment", None, None, "mp"),
        P(),
    )
    out_specs = P(None, "seq", ("segment", "mp"))
    return jax.shard_map(
        on_device, mesh=mesh, in_specs=in_specs, out_specs=out_specs, check_vma=False
    )
```

time: 331 us -> 107 us (0.32)
  waiting for transfers between devices: 277 us -> 44.2 us
  starting transfers between devices: 5.97 us -> 35.6 us
  Pallas kernels: 0 us -> 20.6 us
  matrix products: 14 us -> 0 us
  between operations: 13.2 us -> 0.28 us
  local copies, waits for them, and re-layouts: 15.2 us -> 4.53 us
  other arithmetic: 4.95 us -> 1.6 us
    all_gather x4 -> x0, waiting for transfers between devices: 161 us -> none  [the longest x1 80.8 us: on_device(): value_part = lax.all_gather(value_flat, 'seq', axis=1, tiled=True)]
    reduce_scatter x1 -> x0, waiting for transfers between devices: 69.3 us -> none  [on_device(): lax.psum_scatter(update_terms.astype(jnp.bfloat16), ('segment', 'mp'), sc...]
    ppermute x2 -> x20, starting transfers between devices: 5.81 us -> 35.6 us  [the longest x10 16.2 us: in_section(): return lax.ppermute(array, ('segment', 'mp'), pairs)]
    pallas_call x0 -> x11, Pallas kernels: none -> 20.6 us  [call(): pl.pallas_call(kernel, out_shape=out_shapes, in_specs=specs, out_specs=ou...]
    dot_general x2 -> x0, matrix products: 14 us -> none  [the longest x1 9.4 us: encode(): jnp.dot(normed, second_weight, preferred_element_type=jnp.float32)]
    squeeze x1, local copies, waits for them, and re-layouts: 12 us -> 1.08 us  [on_device(): first_rows, memory = after((memory[0], memory))]
    ppermute x2 -> x20, waiting for transfers between devices: 45.3 us -> 44.2 us  [the longest x2 19.5 us: to_encoder(): return lax.ppermute(array, 'segment', [(1, 0)])]
  transfers between devices with their start and end apart: 7 -> 20, of which waited for: 6 -> 8; matrix products, arithmetic and copies ran while one was open for 9% -> 3% of each run, Pallas kernels for 0% -> 15%
where the time goes in v2:
time: 107 us
  waiting for transfers between devices  44.2 us (41%)
  starting transfers between devices  35.6 us (33%)
  Pallas kernels  20.6 us (19%)
  local copies, waits for them, and re-layouts  4.53 us (4%)
  other arithmetic  1.6 us (1%)
    pallas_call x11, Pallas kernels, call(): pl.pallas_call(kernel, out_shape=out_shapes, in_specs=specs, out_specs=ou...  20.6 us
    ppermute x2, waiting for transfers between devices, to_encoder(): return lax.ppermute(array, 'segment', [(1, 0)])  19.5 us
    ppermute x10, starting transfers between devices, in_section(): return lax.ppermute(array, ('segment', 'mp'), pairs)  16.2 us
    ppermute x6, waiting for transfers between devices, along_seq(): lax.ppermute(array, 'seq', [(i, (i + by) % count) for i in range(count)])  14.6 us
    ppermute x6, starting transfers between devices, along_seq(): lax.ppermute(array, 'seq', [(i, (i + by) % count) for i in range(count)])  10.2 us
    ppermute x2, starting transfers between devices, to_decoder(): return lax.ppermute(array, 'segment', [(0, 1)])  6.6 us
    ppermute x10, waiting for transfers between devices, in_section(): return lax.ppermute(array, ('segment', 'mp'), pairs)  5.01 us
    ppermute x2, waiting for transfers between devices, to_decoder(): return lax.ppermute(array, 'segment', [(0, 1)])  4.98 us
  transfers between devices with their start and end apart: 20, of which 8 were waited for; matrix products, arithmetic and copies ran while one was open for 3% of the time, Pallas kernels for 15%

profile of v2, /device:TPU:0, one launch (start us, length us, event | category | flops | bytes accessed | tf_op | source)
XLA Modules:
  0.0 106.7 jit_solution(81297059821054103)
XLA Ops:
  0.0 0.0 copy-start
  0.0 0.8 collective-permute-start.1
  0.8 1.1 %slice_bitcast_fusion = bf16[256,1024]{1,0:T(8,128)(2,1)S(1)} fusion(bf16[2,256,1024]{2,1,0:T(8,128)(2,1)} %param.5), kind=kLoop, calls=%fused_computation | loop fusion | bytes 1048576 | tf_op jit(solution)/shard_map/squeeze | solution.py:337
  1.9 4.9 %collective-permute-start.5 = (bf16[256,1024]{1,0:T(8,128)(2,1)S(1)}, bf16[256,1024]{1,0:T(8,128)(2,1)S(1)}, u32[]{:S(2)}, u32[]{:S(2)}) collective-permute-start(bf16[256,1024]{1,0:T(8,128)(2,1)S(1)} %slice_bitcast_fusion), channel_id=1, source_target_pairs={{0,2},{1,3},{2,0},{3,1},{4,6},{5,7},{6,4},{7,5},{8,10},{9,11},{10,... | collective-permute-start | bytes 1572872 | tf_op jit(solution)/shard_map/ppermute | solution.py:322
  6.8 1.9 %collective-permute-start.4 = (bf16[512,1024]{1,0:T(8,128)(2,1)}, bf16[512,1024]{1,0:T(8,128)(2,1)S(1)}, u32[]{:S(2)}, u32[]{:S(2)}) collective-permute-start(bf16[512,1024]{1,0:T(8,128)(2,1)} %bitcast.5), channel_id=1, source_target_pairs={{0,1},{1,0},{2,3},{3,2},{4,5},{5,4},{6,7},{7,6},{8,9},{9,8},{10,11... | collective-permute-start | bytes 3145736 | tf_op jit(solution)/shard_map/ppermute | solution.py:322
  8.7 0.7 collective-permute-start
  9.4 0.0 copy-start.1
  9.4 0.9 copy-done.1
  10.3 0.0 copy-start.2
  10.3 0.7 copy-done.2
  11.1 0.0 collective-permute-done.1.x2
  11.1 0.7 collective-permute-start.2
  11.8 1.1 %slice.12 = bf16[320,1024]{1,0:T(8,128)(2,1)S(1)} slice(bf16[512,1024]{1,0:T(8,128)(2,1)} %bitcast.6), slice={[192:512], [0:1024]} | slice | bytes 1310720 | tf_op jit(solution)/shard_map/slice | solution.py:339
  12.9 1.9 %collective-permute-start.10 = (bf16[320,1024]{1,0:T(8,128)(2,1)S(1)}, bf16[320,1024]{1,0:T(8,128)(2,1)S(1)}, u32[]{:S(2)}, u32[]{:S(2)}) collective-permute-start(bf16[320,1024]{1,0:T(8,128)(2,1)S(1)} %slice.12), channel_id=1, source_target_pairs={{0,2},{1,3},{2,0},{3,1},{4,6},{5,7},{6,4},{7,5},{8,10},{9,11},{10,... | collective-permute-start | bytes 1966088 | tf_op jit(solution)/shard_map/ppermute | solution.py:322
  14.9 0.0 collective-permute-done.x1
  14.9 0.0 collective-permute-done.2.x3
  14.9 0.1 shard_map.56
  15.0 4.4 %collective-permute-done.5.x2 = bf16[256,1024]{1,0:T(8,128)(2,1)S(1)} collective-permute-done((bf16[256,1024]{1,0:T(8,128)(2,1)S(1)}, bf16[256,1024]{1,0:T(8,128)(2,1)S(1)}, u32[]{:S(2)}, u32[]{:S(2)}) %collective-permute-start.5) | collective-permute-done | bytes 524320 | tf_op jit(solution)/shard_map/ppermute | solution.py:322
  19.4 1.9 %collective-permute-start.6 = (bf16[256,1024]{1,0:T(8,128)(2,1)S(1)}, bf16[256,1024]{1,0:T(8,128)(2,1)S(1)}, u32[]{:S(2)}, u32[]{:S(2)}) collective-permute-start(bf16[256,1024]{1,0:T(8,128)(2,1)S(1)} %collective-permute-done.5.x2), channel_id=1, source_target_pairs={{0,1},{1,0},{2,3},{3,2},{4,5},{5,4},{6,7},{7,6},{8,9},{9,8},{10,11... | collective-permute-start | bytes 1572872 | tf_op jit(solution)/shard_map/ppermute | solution.py:322
  21.3 1.3 %collective-permute-start.3 = (bf16[64,1024]{1,0:T(8,128)(2,1)S(1)}, bf16[64,1024]{1,0:T(8,128)(2,1)S(1)}, u32[]{:S(2)}, u32[]{:S(2)}) collective-permute-start(bf16[64,1024]{1,0:T(8,128)(2,1)S(1)} %get-tuple-element.25), channel_id=1, source_target_pairs={{16,0},{17,1},{18,2},{19,3},{20,4},{21,5},{22,6},{23,7},{24,8},{25... | collective-permute-start | bytes 393224 | tf_op jit(solution)/shard_map/ppermute | solution.py:328
  22.6 0.6 collective-permute-done.6.x3
  23.2 0.0 collective-permute-done.4.x1
  23.2 0.0 copy-done
  23.2 8.6 %shard_map.57 = bf16[2,256,1024]{2,1,0:T(8,128)(2,1)} custom-call(bf16[512,1024]{1,0:T(8,128)(2,1)S(1)} %bitcast.7, bf16[512,1024]{1,0:T(8,128)(2,1)S(1)} %collective-permute-done.4.x1, bf16[256,1024]{1,0:T(8,128)(2,1)S(1)} %collective-permute-done.5.x2, bf16[256,1024]{1,0:T(8,128)(2,1)S(1)} %collective-permute-done.6.x3, ...), custom_call_target="tpu_custom_call" | custom-call | flops 1 | bytes 1 | tf_op jit(solution)/shard_map/pallas_call | solution.py:294
  31.8 2.3 %collective-permute-start.12 = (bf16[2,256,1024]{2,1,0:T(8,128)(2,1)}, bf16[2,256,1024]{2,1,0:T(8,128)(2,1)}, u32[]{:S(2)}, u32[]{:S(2)}) collective-permute-start(bf16[2,256,1024]{2,1,0:T(8,128)(2,1)} %shard_map.57), channel_id=1, source_target_pairs={{0,16},{1,17},{2,18},{3,19},{4,20},{5,21},{6,22},{7,23},{8,24},{9,... | collective-permute-start | bytes 3145736 | tf_op jit(solution)/shard_map/ppermute | solution.py:331
  34.0 0.0 collective-permute-done.3
  34.0 0.0 copy-start.4
  34.0 0.0 collective-permute-done.10
  34.1 0.6 copy-done.4
  34.7 2.0 %collective-permute-start.11 = (bf16[256,1024]{1,0:T(8,128)(2,1)S(1)}, bf16[256,1024]{1,0:T(8,128)(2,1)S(1)}, u32[]{:S(2)}, u32[]{:S(2)}) collective-permute-start(bf16[256,1024]{1,0:T(8,128)(2,1)S(1)} %slice.11.x2), channel_id=1, source_target_pairs={{0,1},{1,0},{2,3},{3,2},{4,5},{5,4},{6,7},{7,6},{8,9},{9,8},{10,11... | collective-permute-start | bytes 1572872 | tf_op jit(solution)/shard_map/ppermute | solution.py:322
  36.7 0.0 copy-start.3
  36.7 0.9 broadcast_select_fusion.refs_0_
  37.7 4.1 %collective-permute-start.9 = (bf16[64,1024]{1,0:T(8,128)(2,1)S(1)}, bf16[64,1024]{1,0:T(8,128)(2,1)S(1)}, u32[]{:S(2)}, u32[]{:S(2)}) collective-permute-start(bf16[64,1024]{1,0:T(8,128)(2,1)S(1)} %broadcast_select_fusion.refs_0_), channel_id=1, source_target_pairs={{0,12},{4,0},{8,4},{12,8},{1,13},{5,1},{9,5},{13,9},{2,14},{6,2},{... | collective-permute-start | bytes 393224 | tf_op jit(solution)/shard_map/ppermute | solution.py:325
  41.8 0.0 collective-permute-start.8
  41.8 1.0 collective-permute-start.7
  42.8 0.0 collective-permute-done.11.x3
  42.8 7.6 %shard_map.58.refs_4_ = bf16[2,256,1024]{2,1,0:T(8,128)(2,1)S(1)} custom-call(bf16[512,1024]{1,0:T(8,128)(2,1)S(1)} %bitcast.8, bf16[512,1024]{1,0:T(8,128)(2,1)S(1)} %collective-permute-done.4.x1, bf16[256,1024]{1,0:T(8,128)(2,1)S(1)} %slice.11.x2, bf16[256,1024]{1,0:T(8,128)(2,1)S(1)} %collective-permute-done.11.x3, ...), custom_call_target="tpu_custom_call" | custom-call | flops 4800000000 | bytes 1 | tf_op jit(solution)/shard_map/pallas_call | solution.py:294
  50.4 0.0 collective-permute-done.9.refs_3_
  50.4 3.4 %collective-permute-done.8.refs_2_ = bf16[64,1024]{1,0:T(8,128)(2,1)S(1)} collective-permute-done((bf16[64,1024]{1,0:T(8,128)(2,1)S(1)}, bf16[64,1024]{1,0:T(8,128)(2,1)S(1)}, u32[]{:S(2)}, u32[]{:S(2)}) %collective-permute-start.8) | collective-permute-done | bytes 131104 | tf_op jit(solution)/shard_map/ppermute | solution.py:325
  53.8 0.0 collective-permute-done.7.refs_1_
  53.8 2.6 %collective-permute-done.12.refs_5_ = bf16[2,256,1024]{2,1,0:T(8,128)(2,1)} collective-permute-done((bf16[2,256,1024]{2,1,0:T(8,128)(2,1)}, bf16[2,256,1024]{2,1,0:T(8,128)(2,1)}, u32[]{:S(2)}, u32[]{:S(2)}) %collective-permute-start.12) | collective-permute-done | bytes 1048608 | tf_op jit(solution)/shard_map/ppermute | solution.py:331
  56.4 0.0 copy-done.3
  56.4 3.3 %shard_map.59 = (bf16[64,1152]{1,0:T(8,128)(2,1)S(1)}, bf16[64,1152]{1,0:T(8,128)(2,1)S(1)}, bf16[64,1152]{1,0:T(8,128)(2,1)S(1)}, bf16[64,1152]{1,0:T(8,128)(2,1)S(1)}) custom-call(s32[2]{0:T(128)S(1)} %copy-done.3, bf16[64,1024]{1,0:T(8,128)(2,1)S(1)} %broadcast_select_fusion.refs_0_, bf16[64,1024]{1,0:T(8,128)(2,1)S(1)} %collective-permute-done.7.refs_1_, ...), custom_call_target="tpu_custom_call" | custom-call | flops 1 | bytes 1 | tf_op jit(solution)/shard_map/pallas_call | solution.py:294
  59.7 4.1 %collective-permute-start.13 = (bf16[64,1152]{1,0:T(8,128)(2,1)S(1)}, bf16[64,1152]{1,0:T(8,128)(2,1)S(1)}, u32[]{:S(2)}, u32[]{:S(2)}) collective-permute-start(bf16[64,1152]{1,0:T(8,128)(2,1)S(1)} %get-tuple-element.33), channel_id=1, source_target_pairs={{0,12},{4,0},{8,4},{12,8},{1,13},{5,1},{9,5},{13,9},{2,14},{6,2},{... | collective-permute-start | bytes 442376 | tf_op jit(solution)/shard_map/ppermute | solution.py:325
  63.8 0.0 collective-permute-start.14
  63.8 1.0 collective-permute-start.15
  64.8 3.3 %collective-permute-done.13.refs_1_ = bf16[64,1152]{1,0:T(8,128)(2,1)S(1)} collective-permute-done((bf16[64,1152]{1,0:T(8,128)(2,1)S(1)}, bf16[64,1152]{1,0:T(8,128)(2,1)S(1)}, u32[]{:S(2)}, u32[]{:S(2)}) %collective-permute-start.13) | collective-permute-done | bytes 147488 | tf_op jit(solution)/shard_map/ppermute | solution.py:325
  68.1 8.0 %collective-permute-done.14.refs_2_ = bf16[64,1152]{1,0:T(8,128)(2,1)S(1)} collective-permute-done((bf16[64,1152]{1,0:T(8,128)(2,1)S(1)}, bf16[64,1152]{1,0:T(8,128)(2,1)S(1)}, u32[]{:S(2)}, u32[]{:S(2)}) %collective-permute-start.14) | collective-permute-done | bytes 147488 | tf_op jit(solution)/shard_map/ppermute | solution.py:325
  76.1 0.0 collective-permute-done.15.refs_3_
  76.1 0.8 shard_map.60.context.first_context
  76.9 4.3 %collective-permute-start.16 = (bf16[64,1024]{1,0:T(8,128)(2,1)S(1)}, bf16[64,1024]{1,0:T(8,128)(2,1)S(1)}, u32[]{:S(2)}, u32[]{:S(2)}) collective-permute-start(bf16[64,1024]{1,0:T(8,128)(2,1)S(1)} %shard_map.60.context.first_context), channel_id=1, source_target_pairs={{0,16},{1,17},{2,18},{3,19},{4,20},{5,21},{6,22},{7,23},{8,24},{9,... | collective-permute-start | bytes 393224 | tf_op jit(solution)/shard_map/ppermute | solution.py:331
  81.3 0.1 shard_map.61.weights
  81.4 2.4 %collective-permute-done.16.second_context = bf16[64,1024]{1,0:T(8,128)(2,1)S(1)} collective-permute-done((bf16[64,1024]{1,0:T(8,128)(2,1)S(1)}, bf16[64,1024]{1,0:T(8,128)(2,1)S(1)}, u32[]{:S(2)}, u32[]{:S(2)}) %collective-permute-start.16) | collective-permute-done | bytes 131104 | tf_op jit(solution)/shard_map/ppermute | solution.py:331
  83.8 0.7 collective-permute-start.17
  84.5 0.0 collective-permute-done.17.other.sibling
  84.5 0.7 collective-permute-start.18
  85.2 0.0 collective-permute-done.18.across
  85.2 1.3 %collective-permute-start.19 = (bf16[128,512]{1,0:T(8,128)(2,1)S(1)}, bf16[128,512]{1,0:T(8,128)(2,1)S(1)}, u32[]{:S(2)}, u32[]{:S(2)}) collective-permute-start(bf16[128,512]{1,0:T(8,128)(2,1)S(1)} %get-tuple-element.37), channel_id=1, source_target_pairs={{16,0},{17,1},{18,2},{19,3},{20,4},{21,5},{22,6},{23,7},{24,8},{25... | collective-permute-start | bytes 393224 | tf_op jit(solution)/shard_map/ppermute | solution.py:328
  86.5 19.5 %collective-permute-done.19 = bf16[128,512]{1,0:T(8,128)(2,1)S(1)} collective-permute-done((bf16[128,512]{1,0:T(8,128)(2,1)S(1)}, bf16[128,512]{1,0:T(8,128)(2,1)S(1)}, u32[]{:S(2)}, u32[]{:S(2)}) %collective-permute-start.19) | collective-permute-done | bytes 131104 | tf_op jit(solution)/shard_map/ppermute | solution.py:328
  106.1 0.7 broadcast_select_fusion.1
  (6 shorter events, 0.1 us)
Async XLA Ops:
  0.0 23.2 %copy-start = (bf16[2,256,1024]{2,1,0:T(8,128)(2,1)S(1)}, bf16[2,256,1024]{2,1,0:T(8,128)(2,1)}, u32[]{:S(2)}) copy-start(bf16[2,256,1024]{2,1,0:T(8,128)(2,1)} %param.5) | copy-start | bytes 3145732
  0.0 11.1 %collective-permute-start.1 = (bf16[128,1024]{1,0:T(8,128)(2,1)}, bf16[128,1024]{1,0:T(8,128)(2,1)S(1)}, u32[]{:S(2)}, u32[]{:S(2)}) collective-permute-start(bf16[128,1024]{1,0:T(8,128)(2,1)} %bitcast.9), channel_id=1, source_target_pairs={{16,18},{17,19},{18,16},{19,17},{20,22},{21,23},{22,20},{23,21},{2... | collective-permute-start | bytes 786440 | tf_op jit(solution)/shard_map/ppermute | solution.py:322
  1.9 17.5 %collective-permute-start.5 = (bf16[256,1024]{1,0:T(8,128)(2,1)S(1)}, bf16[256,1024]{1,0:T(8,128)(2,1)S(1)}, u32[]{:S(2)}, u32[]{:S(2)}) collective-permute-start(bf16[256,1024]{1,0:T(8,128)(2,1)S(1)} %slice_bitcast_fusion), channel_id=1, source_target_pairs={{0,2},{1,3},{2,0},{3,1},{4,6},{5,7},{6,4},{7,5},{8,10},{9,11},{10,... | collective-permute-start | bytes 1572872 | tf_op jit(solution)/shard_map/ppermute | solution.py:322
  6.8 16.4 %collective-permute-start.4 = (bf16[512,1024]{1,0:T(8,128)(2,1)}, bf16[512,1024]{1,0:T(8,128)(2,1)S(1)}, u32[]{:S(2)}, u32[]{:S(2)}) collective-permute-start(bf16[512,1024]{1,0:T(8,128)(2,1)} %bitcast.5), channel_id=1, source_target_pairs={{0,1},{1,0},{2,3},{3,2},{4,5},{5,4},{6,7},{7,6},{8,9},{9,8},{10,11... | collective-permute-start | bytes 3145736 | tf_op jit(solution)/shard_map/ppermute | solution.py:322
  8.7 6.2 %collective-permute-start = (bf16[128,1024]{1,0:T(8,128)(2,1)}, bf16[128,1024]{1,0:T(8,128)(2,1)S(1)}, u32[]{:S(2)}, u32[]{:S(2)}) collective-permute-start(bf16[128,1024]{1,0:T(8,128)(2,1)} %bitcast.10), channel_id=1, source_target_pairs={{16,17},{17,16},{18,19},{19,18},{20,21},{21,20},{22,23},{23,22},{2... | collective-permute-start | bytes 786440 | tf_op jit(solution)/shard_map/ppermute | solution.py:322
  9.4 1.0 copy-start.1
  10.3 0.7 copy-start.2
  11.1 3.8 %collective-permute-start.2 = (bf16[128,1024]{1,0:T(8,128)(2,1)S(1)}, bf16[128,1024]{1,0:T(8,128)(2,1)S(1)}, u32[]{:S(2)}, u32[]{:S(2)}) collective-permute-start(bf16[128,1024]{1,0:T(8,128)(2,1)S(1)} %collective-permute-done.1.x2), channel_id=1, source_target_pairs={{16,17},{17,16},{18,19},{19,18},{20,21},{21,20},{22,23},{23,22},{2... | collective-permute-start | bytes 786440 | tf_op jit(solution)/shard_map/ppermute | solution.py:322
  12.9 21.1 %collective-permute-start.10 = (bf16[320,1024]{1,0:T(8,128)(2,1)S(1)}, bf16[320,1024]{1,0:T(8,128)(2,1)S(1)}, u32[]{:S(2)}, u32[]{:S(2)}) collective-permute-start(bf16[320,1024]{1,0:T(8,128)(2,1)S(1)} %slice.12), channel_id=1, source_target_pairs={{0,2},{1,3},{2,0},{3,1},{4,6},{5,7},{6,4},{7,5},{8,10},{9,11},{10,... | collective-permute-start | bytes 1966088 | tf_op jit(solution)/shard_map/ppermute | solution.py:322
  19.4 3.8 %collective-permute-start.6 = (bf16[256,1024]{1,0:T(8,128)(2,1)S(1)}, bf16[256,1024]{1,0:T(8,128)(2,1)S(1)}, u32[]{:S(2)}, u32[]{:S(2)}) collective-permute-start(bf16[256,1024]{1,0:T(8,128)(2,1)S(1)} %collective-permute-done.5.x2), channel_id=1, source_target_pairs={{0,1},{1,0},{2,3},{3,2},{4,5},{5,4},{6,7},{7,6},{8,9},{9,8},{10,11... | collective-permute-start | bytes 1572872 | tf_op jit(solution)/shard_map/ppermute | solution.py:322
  21.3 12.7 %collective-permute-start.3 = (bf16[64,1024]{1,0:T(8,128)(2,1)S(1)}, bf16[64,1024]{1,0:T(8,128)(2,1)S(1)}, u32[]{:S(2)}, u32[]{:S(2)}) collective-permute-start(bf16[64,1024]{1,0:T(8,128)(2,1)S(1)} %get-tuple-element.25), channel_id=1, source_target_pairs={{16,0},{17,1},{18,2},{19,3},{20,4},{21,5},{22,6},{23,7},{24,8},{25... | collective-permute-start | bytes 393224 | tf_op jit(solution)/shard_map/ppermute | solution.py:328
  31.8 24.6 %collective-permute-start.12 = (bf16[2,256,1024]{2,1,0:T(8,128)(2,1)}, bf16[2,256,1024]{2,1,0:T(8,128)(2,1)}, u32[]{:S(2)}, u32[]{:S(2)}) collective-permute-start(bf16[2,256,1024]{2,1,0:T(8,128)(2,1)} %shard_map.57), channel_id=1, source_target_pairs={{0,16},{1,17},{2,18},{3,19},{4,20},{5,21},{6,22},{7,23},{8,24},{9,... | collective-permute-start | bytes 3145736 | tf_op jit(solution)/shard_map/ppermute | solution.py:331
  34.0 0.7 copy-start.4
  34.7 8.1 %collective-permute-start.11 = (bf16[256,1024]{1,0:T(8,128)(2,1)S(1)}, bf16[256,1024]{1,0:T(8,128)(2,1)S(1)}, u32[]{:S(2)}, u32[]{:S(2)}) collective-permute-start(bf16[256,1024]{1,0:T(8,128)(2,1)S(1)} %slice.11.x2), channel_id=1, source_target_pairs={{0,1},{1,0},{2,3},{3,2},{4,5},{5,4},{6,7},{7,6},{8,9},{9,8},{10,11... | collective-permute-start | bytes 1572872 | tf_op jit(solution)/shard_map/ppermute | solution.py:322
  36.7 19.6 %copy-start.3 = (s32[2]{0:T(128)S(1)}, s32[2]{0:T(128)}, u32[]{:S(2)}) copy-start(s32[2]{0:T(128)} %lengths.1) | copy-start | bytes 28
  37.7 12.7 %collective-permute-start.9 = (bf16[64,1024]{1,0:T(8,128)(2,1)S(1)}, bf16[64,1024]{1,0:T(8,128)(2,1)S(1)}, u32[]{:S(2)}, u32[]{:S(2)}) collective-permute-start(bf16[64,1024]{1,0:T(8,128)(2,1)S(1)} %broadcast_select_fusion.refs_0_), channel_id=1, source_target_pairs={{0,12},{4,0},{8,4},{12,8},{1,13},{5,1},{9,5},{13,9},{2,14},{6,2},{... | collective-permute-start | bytes 393224 | tf_op jit(solution)/shard_map/ppermute | solution.py:325
  41.8 12.0 %collective-permute-start.8 = (bf16[64,1024]{1,0:T(8,128)(2,1)S(1)}, bf16[64,1024]{1,0:T(8,128)(2,1)S(1)}, u32[]{:S(2)}, u32[]{:S(2)}) collective-permute-start(bf16[64,1024]{1,0:T(8,128)(2,1)S(1)} %broadcast_select_fusion.refs_0_), channel_id=1, source_target_pairs={{0,8},{4,12},{8,0},{12,4},{1,9},{5,13},{9,1},{13,5},{2,10},{6,14},... | collective-permute-start | bytes 393224 | tf_op jit(solution)/shard_map/ppermute | solution.py:325
  41.8 12.0 %collective-permute-start.7 = (bf16[64,1024]{1,0:T(8,128)(2,1)S(1)}, bf16[64,1024]{1,0:T(8,128)(2,1)S(1)}, u32[]{:S(2)}, u32[]{:S(2)}) collective-permute-start(bf16[64,1024]{1,0:T(8,128)(2,1)S(1)} %broadcast_select_fusion.refs_0_), channel_id=1, source_target_pairs={{0,4},{4,8},{8,12},{12,0},{1,5},{5,9},{9,13},{13,1},{2,6},{6,10},{... | collective-permute-start | bytes 393224 | tf_op jit(solution)/shard_map/ppermute | solution.py:325
  59.7 8.4 %collective-permute-start.13 = (bf16[64,1152]{1,0:T(8,128)(2,1)S(1)}, bf16[64,1152]{1,0:T(8,128)(2,1)S(1)}, u32[]{:S(2)}, u32[]{:S(2)}) collective-permute-start(bf16[64,1152]{1,0:T(8,128)(2,1)S(1)} %get-tuple-element.33), channel_id=1, source_target_pairs={{0,12},{4,0},{8,4},{12,8},{1,13},{5,1},{9,5},{13,9},{2,14},{6,2},{... | collective-permute-start | bytes 442376 | tf_op jit(solution)/shard_map/ppermute | solution.py:325
  63.8 12.3 %collective-permute-start.14 = (bf16[64,1152]{1,0:T(8,128)(2,1)S(1)}, bf16[64,1152]{1,0:T(8,128)(2,1)S(1)}, u32[]{:S(2)}, u32[]{:S(2)}) collective-permute-start(bf16[64,1152]{1,0:T(8,128)(2,1)S(1)} %get-tuple-element.34), channel_id=1, source_target_pairs={{0,8},{4,12},{8,0},{12,4},{1,9},{5,13},{9,1},{13,5},{2,10},{6,14},... | collective-permute-start | bytes 442376 | tf_op jit(solution)/shard_map/ppermute | solution.py:325
  63.8 12.3 %collective-permute-start.15 = (bf16[64,1152]{1,0:T(8,128)(2,1)S(1)}, bf16[64,1152]{1,0:T(8,128)(2,1)S(1)}, u32[]{:S(2)}, u32[]{:S(2)}) collective-permute-start(bf16[64,1152]{1,0:T(8,128)(2,1)S(1)} %get-tuple-element.35), channel_id=1, source_target_pairs={{0,4},{4,8},{8,12},{12,0},{1,5},{5,9},{9,13},{13,1},{2,6},{6,10},{... | collective-permute-start | bytes 442376 | tf_op jit(solution)/shard_map/ppermute | solution.py:325
  76.9 6.8 %collective-permute-start.16 = (bf16[64,1024]{1,0:T(8,128)(2,1)S(1)}, bf16[64,1024]{1,0:T(8,128)(2,1)S(1)}, u32[]{:S(2)}, u32[]{:S(2)}) collective-permute-start(bf16[64,1024]{1,0:T(8,128)(2,1)S(1)} %shard_map.60.context.first_context), channel_id=1, source_target_pairs={{0,16},{1,17},{2,18},{3,19},{4,20},{5,21},{6,22},{7,23},{8,24},{9,... | collective-permute-start | bytes 393224 | tf_op jit(solution)/shard_map/ppermute | solution.py:331
  83.8 0.7 collective-permute-start.17
  84.5 0.7 collective-permute-start.18
  85.2 20.8 %collective-permute-start.19 = (bf16[128,512]{1,0:T(8,128)(2,1)S(1)}, bf16[128,512]{1,0:T(8,128)(2,1)S(1)}, u32[]{:S(2)}, u32[]{:S(2)}) collective-permute-start(bf16[128,512]{1,0:T(8,128)(2,1)S(1)} %get-tuple-element.37), channel_id=1, source_target_pairs={{16,0},{17,1},{18,2},{19,3},{20,4},{21,5},{22,6},{23,7},{24,8},{25... | collective-permute-start | bytes 393224 | tf_op jit(solution)/shard_map/ppermute | solution.py:328

commit v3 on v2

--- a/solution.py
+++ b/solution.py
@@ -23,7 +23,7 @@
 
 
 def params():
-    return pltpu.CompilerParams(vmem_limit_bytes=44 * 1024 * 1024)
+    return pltpu.CompilerParams(vmem_limit_bytes=40 * 1024 * 1024)
 
 
 def position():
@@ -104,7 +104,7 @@
     gains_out[...] = gains[...]
 
 
-def query_kernel(x0, x1, x2, x3, gains, weights, first_out, second_out, res, wbuf, sem):
+def query_kernel(x0, x1, x2, x3, gains, weights, first_out, second_out, res1, wbuf, sem):
     info = position()
     blocks = info[2:6]
     rows_each = first_out.shape[0]
@@ -112,19 +112,25 @@
     @pl.when(info[0] == 1)
     def _():
         stream = WeightStream(weights, [(0, block) for block in blocks], x0.shape[1], wbuf, sem)
-        half = res.shape[1] // 2
+        half = res1.shape[1]
         offset = pl.multiple_of(info[6] * half, half)
         for k, part in enumerate((x0, x1, x2, x3)):
-            for side in range(2):
-
-                @pl.when(info[7 + side] == k)
-                def _():
-                    res[:, side * half : (side + 1) * half] = part[:, pl.ds(offset, half)]
+
+            @pl.when(info[7] == k)
+            def _():
+                for doc in range(part.shape[0] // rows_each):
+                    second_out[rows_each:, doc * half : (doc + 1) * half] = part[
+                        doc * rows_each : (doc + 1) * rows_each, pl.ds(offset, half)
+                    ]
+
+            @pl.when(info[8] == k)
+            def _():
+                res1[...] = part[:, pl.ds(offset, half)]
 
         parts = (x0[...], x1[...], x2[...], x3[...])
         total = streamed_product(normed_rows(parts, gains, blocks), stream)
         first_out[...] = total[:rows_each].astype(bf16)
-        second_out[...] = total[rows_each:].astype(bf16)
+        second_out[:rows_each] = total[rows_each:].astype(bf16)
 
 
 def memory_kernel(doc, matrices, x0, x1, x2, x3, gains, weights, out, wbuf, sem):
@@ -141,6 +147,24 @@
         rows = normed_rows(parts, gains, blocks)
         for i in range(len(matrices)):
             out[i] = streamed_product(rows, stream).astype(bf16)
+
+
+def first_memory_kernel(x0, x1, x2, x3, gains, key_weights, weights, out, wbuf, sem):
+    info = position()
+    blocks = info[2:6]
+    span, width = x2.shape
+
+    @pl.when(info[0] == 0)
+    def _():
+        stream = WeightStream(weights, [(1, block) for block in blocks], width, wbuf, sem)
+        rows = normed_rows((x0[:span], x1[:span], x2[...], x3[...]), gains, blocks)
+        total = None
+        for part, block in zip(rows, blocks):
+            matrix = key_weights[pl.ds(pl.multiple_of(block * width, width), width), :]
+            term = jnp.dot(part, matrix, preferred_element_type=f32)
+            total = term if total is None else total + term
+        out[0] = total.astype(bf16)
+        out[1] = streamed_product(rows, stream).astype(bf16)
 
 
 def attention_kernel(count, lengths, *refs):
@@ -229,14 +253,15 @@
         out[:, cols] = context.astype(bf16)
 
 
-def load_kernel(weights, context, out, sem):
-    info = position()
-    @pl.when(info[0] == 1)
+def load_kernel(section, which, weights, before, out, sem):
+    info = position()
+
+    @pl.when(info[0] == section)
     def _():
         height = out.shape[0] // 8
         copies = [
             pltpu.make_async_copy(
-                weights.at[0, 1, pl.ds(i * height, height), :],
+                weights.at[0, which, pl.ds(i * height, height), :],
                 out.at[pl.ds(i * height, height), :],
                 sem.at[i],
             )
@@ -266,28 +291,36 @@
             ).astype(bf16)
 
 
-def add_kernel(mine, other, out):
-    info = position()
+def add_kernel(mine, other, *outs):
+    info = position()
+
     @pl.when(info[0] == 1)
     def _():
-        rows = out.shape[0]
-        out[...] = (mine[:rows].astype(f32) + other[:rows].astype(f32)).astype(bf16)
-
-
-def final_kernel(mine, sibling, across, res, *outs):
-    info = position()
+        rows = outs[0].shape[0]
+        for i, out in enumerate(outs):
+            part = slice(i * rows, (i + 1) * rows)
+            out[...] = (mine[part].astype(f32) + other[part].astype(f32)).astype(bf16)
+
+
+def final_kernel(mine, sibling, across, residual1, direct, diagonal, residual0, out):
+    info = position()
+    block = out.shape[1]
+
     @pl.when(info[0] == 1)
     def _():
-        half = outs[0].shape[1]
-        rows = 2 * half
-        for side, out in enumerate(outs):
-            part = slice(rows + side * half, rows + (side + 1) * half)
-            update = (
-                mine[part].astype(f32)
-                + sibling[part].astype(f32)
-                + across[side * half : (side + 1) * half].astype(f32)
-            )
-            out[...] = (res[:, side * half : (side + 1) * half].astype(f32) + update.T).astype(bf16)
+        part = slice(3 * block, 4 * block)
+        update = mine[part].astype(f32) + sibling[part].astype(f32) + across[...].astype(f32)
+        out[...] = (residual1[...].astype(f32) + update.T).astype(bf16)
+
+    @pl.when(info[0] == 0)
+    def _():
+        update = direct[...].astype(f32) + diagonal[...].astype(f32)
+        update = update.T
+        pos = residual0.shape[0] // 2
+        for doc in range(out.shape[0] // pos):
+            here = slice(doc * pos, (doc + 1) * pos)
+            residual = residual0[pos:, doc * block : (doc + 1) * block].astype(f32)
+            out[here] = (residual + update[here]).astype(bf16)
 
 
 def call(kernel, out_shapes, args, specs, scratch=(), out_specs=None, flops=1, **more):
@@ -351,14 +384,14 @@
     )
     dec_y, _ = after((dec_y, gains))
     dec_yc = in_section(dec_y, 1, 1)
-    first_queries, second_queries, residual = call(
+    first_queries, for_encoder, residual1 = call(
         query_kernel,
-        (shape(pos, head_width), shape(pos, head_width), shape(rows, width)),
+        (shape(pos, head_width), shape(2 * pos, head_width), shape(rows, width // 2)),
         (dec_here, dec_c, dec_y, dec_yc, gains, weights),
         [VMEM] * 5 + [ANY],
         weight_scratch(1),
     )
-    q_received = to_encoder(second_queries)
+    from_decoder = to_encoder(for_encoder)
 
     def project_memory(doc, matrices, far, far_c, cost):
         return call(
@@ -370,17 +403,33 @@
             flops=int(cost),
         )
 
-    far, _ = after((mem_y[0], second_queries))
+    def load(section, which, before):
+        return call(
+            functools.partial(load_kernel, section, which),
+            shape(4 * width, head_width),
+            (weights, before),
+            [ANY, ANY],
+            [pltpu.SemaphoreType.DMA((8,))],
+        )
+
+    key_weights = load(0, 0, for_encoder)
+    far, _ = after((mem_y[0], key_weights))
     far_c = in_section(far, 0, 1)
-    made = project_memory(0, (0, 1), far, far_c, 1)
+    made = call(
+        first_memory_kernel,
+        shape(2, span, head_width),
+        (mem, mem_c, far, far_c, gains, key_weights, weights),
+        [VMEM] * 6 + [ANY],
+        weight_scratch(1),
+    )
     first_memory = to_decoder(made)
-    q_received, _ = after((q_received, made))
-    far, _ = after((mem_y[1], q_received))
+    from_decoder, _ = after((from_decoder, made))
+    far, _ = after((mem_y[1], from_decoder))
     far = far[extra:]
     second_memory = project_memory(1, (0, 1), far, in_section(far, 0, 1), 4.8e9)
 
     encoding = segment == 0
-    q_pieces = [jnp.where(encoding, q_received, first_queries)]
+    q_pieces = [jnp.where(encoding, from_decoder[:pos], first_queries)]
     for by in range(1, count):
         q_pieces.append(along_seq(q_pieces[0], by))
 
@@ -399,13 +448,7 @@
     )
     second_context = to_decoder(context)
 
-    last_weights = call(
-        load_kernel,
-        shape(4 * width, head_width),
-        (weights, context),
-        [ANY, ANY],
-        [pltpu.SemaphoreType.DMA((8,))],
-    )
+    last_weights = load(1, 1, context)
     block = 4 * width // 8
 
     def project(mask):
@@ -419,21 +462,23 @@
     for_sibling = project(1)
     sibling = in_section(for_sibling, 1, 1)
     mine = project(0)
-    for_across = call(
+    for_diagonal, for_across, for_direct = call(
         add_kernel,
-        shape(2 * block, rows),
+        (shape(block, rows),) * 3,
         (mine, sibling),
         [VMEM, VMEM],
     )
     across = in_section(for_across, 1, 2)
-    for_encoder, own = call(
+    direct = to_encoder(for_direct)
+    diagonal = lax.ppermute(
+        for_diagonal, ("segment", "mp"), [(4 + i, i ^ 2) for i in range(4)]
+    )
+    decoder_out = call(
         final_kernel,
-        (shape(rows, block), shape(rows, block)),
-        (mine, sibling, across, residual),
-        [VMEM, VMEM, VMEM, VMEM],
-    )
-    received = to_encoder(for_encoder)
-    decoder_out = jnp.where(encoding, received, own)
+        shape(rows, block),
+        (mine, sibling, across, residual1, direct, diagonal, from_decoder),
+        [VMEM] * 7,
+    )
     return decoder_out.reshape(docs, pos, block)
 
 

time: 107 us -> 102 us (0.953)
  waiting for transfers between devices: 44.2 us -> 36.3 us
  Pallas kernels: 20.6 us -> 23.5 us
  starting transfers between devices: 35.6 us -> 37.5 us
  other arithmetic: 1.6 us -> 0.02 us
    ppermute x2, waiting for transfers between devices: 19.5 us -> 12.8 us  [to_encoder(): return lax.ppermute(array, 'segment', [(1, 0)])]
    ppermute x2, waiting for transfers between devices: 4.98 us -> 8.73 us  [to_decoder(): return lax.ppermute(array, 'segment', [(0, 1)])]
    ppermute x10, waiting for transfers between devices: 5.01 us -> 1.57 us  [in_section(): return lax.ppermute(array, ('segment', 'mp'), pairs)]
    ppermute x6, waiting for transfers between devices: 14.6 us -> 11.5 us  [along_seq(): lax.ppermute(array, 'seq', [(i, (i + by) % count) for i in range(count)])]
    pallas_call x11 -> x12, Pallas kernels: 20.6 us -> 23.5 us  [call(): pl.pallas_call(kernel, out_shape=out_shapes, in_specs=specs, out_specs=ou...]
    ppermute x0 -> x1, waiting for transfers between devices: none -> 1.74 us  [on_device(): lax.ppermute(for_diagonal, ('segment', 'mp'), [(4 + i, i ^ 2) for i in ra...]
    select_n x2 -> x1, other arithmetic: 1.6 us -> 0.02 us  [on_device(): q_pieces = [jnp.where(encoding, from_decoder[:pos], first_queries)]]
    ppermute x0 -> x1, starting transfers between devices: none -> 1.29 us  [on_device(): lax.ppermute(for_diagonal, ('segment', 'mp'), [(4 + i, i ^ 2) for i in ra...]
  transfers between devices with their start and end apart: 20 -> 21, of which waited for: 8 -> 10; matrix products, arithmetic and copies ran while one was open for 3% -> 2% of each run, Pallas kernels for 15% -> 18%
where the time goes in v3:
time: 102 us
  starting transfers between devices  37.5 us (37%)
  waiting for transfers between devices  36.3 us (36%)
  Pallas kernels  23.5 us (23%)
  local copies, waits for them, and re-layouts  3.93 us (4%)
    pallas_call x12, Pallas kernels, call(): pl.pallas_call(kernel, out_shape=out_shapes, in_specs=specs, out_specs=ou...  23.5 us
    ppermute x10, starting transfers between devices, in_section(): return lax.ppermute(array, ('segment', 'mp'), pairs)  15.9 us
    ppermute x2, waiting for transfers between devices, to_encoder(): return lax.ppermute(array, 'segment', [(1, 0)])  12.8 us
    ppermute x6, waiting for transfers between devices, along_seq(): lax.ppermute(array, 'seq', [(i, (i + by) % count) for i in range(count)])  11.5 us
    ppermute x6, starting transfers between devices, along_seq(): lax.ppermute(array, 'seq', [(i, (i + by) % count) for i in range(count)])  11.1 us
    ppermute x2, waiting for transfers between devices, to_decoder(): return lax.ppermute(array, 'segment', [(0, 1)])  8.73 us
    ppermute x2, starting transfers between devices, to_decoder(): return lax.ppermute(array, 'segment', [(0, 1)])  6.61 us
    ppermute x2, starting transfers between devices, to_encoder(): return lax.ppermute(array, 'segment', [(1, 0)])  2.58 us
  transfers between devices with their start and end apart: 21, of which 10 were waited for; matrix products, arithmetic and copies ran while one was open for 2% of the time, Pallas kernels for 18%

profile of v3, /device:TPU:0, one launch (start us, length us, event | category | flops | bytes accessed | tf_op | source)
XLA Modules:
  0.0 101.5 jit_solution(10799347152227573844)
XLA Ops:
  0.0 0.7 collective-permute-start.1
  0.7 1.1 %slice_bitcast_fusion = bf16[256,1024]{1,0:T(8,128)(2,1)S(1)} fusion(bf16[2,256,1024]{2,1,0:T(8,128)(2,1)} %param.5), kind=kLoop, calls=%fused_computation | loop fusion | bytes 1048576 | tf_op jit(solution)/shard_map/squeeze | solution.py:370
  1.8 4.9 %collective-permute-start.5 = (bf16[256,1024]{1,0:T(8,128)(2,1)S(1)}, bf16[256,1024]{1,0:T(8,128)(2,1)S(1)}, u32[]{:S(2)}, u32[]{:S(2)}) collective-permute-start(bf16[256,1024]{1,0:T(8,128)(2,1)S(1)} %slice_bitcast_fusion), channel_id=1, source_target_pairs={{0,2},{1,3},{2,0},{3,1},{4,6},{5,7},{6,4},{7,5},{8,10},{9,11},{10,... | collective-permute-start | bytes 1572872 | tf_op jit(solution)/shard_map/ppermute | solution.py:355
  6.6 1.9 %collective-permute-start.4 = (bf16[512,1024]{1,0:T(8,128)(2,1)}, bf16[512,1024]{1,0:T(8,128)(2,1)S(1)}, u32[]{:S(2)}, u32[]{:S(2)}) collective-permute-start(bf16[512,1024]{1,0:T(8,128)(2,1)} %bitcast.5), channel_id=1, source_target_pairs={{0,1},{1,0},{2,3},{3,2},{4,5},{5,4},{6,7},{7,6},{8,9},{9,8},{10,11... | collective-permute-start | bytes 3145736 | tf_op jit(solution)/shard_map/ppermute | solution.py:355
  8.6 0.7 collective-permute-start
  9.3 0.0 copy-start.1
  9.3 0.9 copy-done.1
  10.2 0.0 copy-start.4
  10.2 0.7 copy-done.4
  11.0 0.0 collective-permute-done.1.x2
  11.0 0.7 collective-permute-start.2
  11.7 1.1 %slice.16 = bf16[320,1024]{1,0:T(8,128)(2,1)S(1)} slice(bf16[512,1024]{1,0:T(8,128)(2,1)} %bitcast.6), slice={[192:512], [0:1024]} | slice | bytes 1310720 | tf_op jit(solution)/shard_map/slice | solution.py:372
  12.8 1.9 %collective-permute-start.10 = (bf16[320,1024]{1,0:T(8,128)(2,1)S(1)}, bf16[320,1024]{1,0:T(8,128)(2,1)S(1)}, u32[]{:S(2)}, u32[]{:S(2)}) collective-permute-start(bf16[320,1024]{1,0:T(8,128)(2,1)S(1)} %slice.16), channel_id=1, source_target_pairs={{0,2},{1,3},{2,0},{3,1},{4,6},{5,7},{6,4},{7,5},{8,10},{9,11},{10,... | collective-permute-start | bytes 1966088 | tf_op jit(solution)/shard_map/ppermute | solution.py:355
  14.7 0.0 collective-permute-done.x1
  14.7 0.0 collective-permute-done.2.x3
  14.7 0.1 shard_map.56
  14.8 0.0 copy-start.2
  14.8 0.0 copy-start
  14.9 3.6 %shard_map.57.key_weights = bf16[4096,1024]{1,0:T(8,128)(2,1)S(1)} custom-call(bf16[1,2,4096,1024]{3,2,1,0:T(8,128)(2,1)} %weights.9, bf16[128,1024]{1,0:T(8,128)(2,1)S(1)} %get-tuple-element.26.before), custom_call_target="tpu_custom_call" | custom-call | flops 1 | bytes 1 | tf_op jit(solution)/shard_map/pallas_call | solution.py:327
  18.4 0.0 copy-done.2
  18.4 0.8 collective-permute-done.5.x2
  19.2 1.9 %collective-permute-start.6 = (bf16[256,1024]{1,0:T(8,128)(2,1)S(1)}, bf16[256,1024]{1,0:T(8,128)(2,1)S(1)}, u32[]{:S(2)}, u32[]{:S(2)}) collective-permute-start(bf16[256,1024]{1,0:T(8,128)(2,1)S(1)} %collective-permute-done.5.x2), channel_id=1, source_target_pairs={{0,1},{1,0},{2,3},{3,2},{4,5},{5,4},{6,7},{7,6},{8,9},{9,8},{10,11... | collective-permute-start | bytes 1572872 | tf_op jit(solution)/shard_map/ppermute | solution.py:355
  21.2 1.3 %collective-permute-start.3 = (bf16[128,1024]{1,0:T(8,128)(2,1)S(1)}, bf16[128,1024]{1,0:T(8,128)(2,1)S(1)}, u32[]{:S(2)}, u32[]{:S(2)}) collective-permute-start(bf16[128,1024]{1,0:T(8,128)(2,1)S(1)} %get-tuple-element.26.before), channel_id=1, source_target_pairs={{16,0},{17,1},{18,2},{19,3},{20,4},{21,5},{22,6},{23,7},{24,8},{25... | collective-permute-start | bytes 786440 | tf_op jit(solution)/shard_map/ppermute | solution.py:361
  22.5 0.6 collective-permute-done.6.x3
  23.0 0.0 collective-permute-done.4.x1
  23.0 0.0 copy-done
  23.0 7.1 %shard_map.58 = bf16[2,256,1024]{2,1,0:T(8,128)(2,1)} custom-call(bf16[512,1024]{1,0:T(8,128)(2,1)S(1)} %bitcast.7, bf16[512,1024]{1,0:T(8,128)(2,1)S(1)} %collective-permute-done.4.x1, bf16[256,1024]{1,0:T(8,128)(2,1)S(1)} %collective-permute-done.5.x2, bf16[256,1024]{1,0:T(8,128)(2,1)S(1)} %collective-permute-done.6.x3, ...), custom_call_target="tpu_custom_call" | custom-call | flops 1 | bytes 1 | tf_op jit(solution)/shard_map/pallas_call | solution.py:327
  30.1 2.3 %collective-permute-start.12 = (bf16[2,256,1024]{2,1,0:T(8,128)(2,1)}, bf16[2,256,1024]{2,1,0:T(8,128)(2,1)}, u32[]{:S(2)}, u32[]{:S(2)}) collective-permute-start(bf16[2,256,1024]{2,1,0:T(8,128)(2,1)} %shard_map.58), channel_id=1, source_target_pairs={{0,16},{1,17},{2,18},{3,19},{4,20},{5,21},{6,22},{7,23},{8,24},{9,... | collective-permute-start | bytes 3145736 | tf_op jit(solution)/shard_map/ppermute | solution.py:364
  32.4 0.0 collective-permute-done.3.residual0
  32.4 0.2 collective-permute-done.10
  32.6 1.9 %collective-permute-start.11 = (bf16[256,1024]{1,0:T(8,128)(2,1)S(1)}, bf16[256,1024]{1,0:T(8,128)(2,1)S(1)}, u32[]{:S(2)}, u32[]{:S(2)}) collective-permute-start(bf16[256,1024]{1,0:T(8,128)(2,1)S(1)} %slice.15.x2), channel_id=1, source_target_pairs={{0,1},{1,0},{2,3},{3,2},{4,5},{5,4},{6,7},{7,6},{8,9},{9,8},{10,11... | collective-permute-start | bytes 1572872 | tf_op jit(solution)/shard_map/ppermute | solution.py:355
  34.6 0.0 copy-start.5
  34.6 2.0 %collective-permute-start.7 = (bf16[64,1024]{1,0:T(8,128)(2,1)S(1)}, bf16[64,1024]{1,0:T(8,128)(2,1)S(1)}, u32[]{:S(2)}, u32[]{:S(2)}) collective-permute-start(bf16[64,1024]{1,0:T(8,128)(2,1)S(1)} %slice_select_fusion.refs_0_), channel_id=1, source_target_pairs={{0,4},{4,8},{8,12},{12,0},{1,5},{5,9},{9,13},{13,1},{2,6},{6,10},{... | collective-permute-start | bytes 393224 | tf_op jit(solution)/shard_map/ppermute | solution.py:358
  36.6 2.6 %collective-permute-start.8 = (bf16[64,1024]{1,0:T(8,128)(2,1)S(1)}, bf16[64,1024]{1,0:T(8,128)(2,1)S(1)}, u32[]{:S(2)}, u32[]{:S(2)}) collective-permute-start(bf16[64,1024]{1,0:T(8,128)(2,1)S(1)} %slice_select_fusion.refs_0_), channel_id=1, source_target_pairs={{0,8},{4,12},{8,0},{12,4},{1,9},{5,13},{9,1},{13,5},{2,10},{6,14},... | collective-permute-start | bytes 393224 | tf_op jit(solution)/shard_map/ppermute | solution.py:358
  39.2 1.3 %collective-permute-start.9 = (bf16[64,1024]{1,0:T(8,128)(2,1)S(1)}, bf16[64,1024]{1,0:T(8,128)(2,1)S(1)}, u32[]{:S(2)}, u32[]{:S(2)}) collective-permute-start(bf16[64,1024]{1,0:T(8,128)(2,1)S(1)} %slice_select_fusion.refs_0_), channel_id=1, source_target_pairs={{0,12},{4,0},{8,4},{12,8},{1,13},{5,1},{9,5},{13,9},{2,14},{6,2},{... | collective-permute-start | bytes 393224 | tf_op jit(solution)/shard_map/ppermute | solution.py:358
  40.6 0.0 collective-permute-done.11.x3
  40.6 7.6 %shard_map.59.refs_4_ = bf16[2,256,1024]{2,1,0:T(8,128)(2,1)S(1)} custom-call(bf16[512,1024]{1,0:T(8,128)(2,1)S(1)} %bitcast.8, bf16[512,1024]{1,0:T(8,128)(2,1)S(1)} %collective-permute-done.4.x1, bf16[256,1024]{1,0:T(8,128)(2,1)S(1)} %slice.15.x2, bf16[256,1024]{1,0:T(8,128)(2,1)S(1)} %collective-permute-done.11.x3, ...), custom_call_target="tpu_custom_call" | custom-call | flops 4800000000 | bytes 1 | tf_op jit(solution)/shard_map/pallas_call | solution.py:327
  48.2 0.0 collective-permute-done.7.refs_1_
  48.2 0.2 collective-permute-done.8.refs_2_
  48.4 0.0 collective-permute-done.9.refs_3_
  48.4 6.4 %collective-permute-done.12.refs_5_ = bf16[2,256,1024]{2,1,0:T(8,128)(2,1)} collective-permute-done((bf16[2,256,1024]{2,1,0:T(8,128)(2,1)}, bf16[2,256,1024]{2,1,0:T(8,128)(2,1)}, u32[]{:S(2)}, u32[]{:S(2)}) %collective-permute-start.12) | collective-permute-done | bytes 1048608 | tf_op jit(solution)/shard_map/ppermute | solution.py:364
  54.7 0.0 copy-done.5
  54.7 3.3 %shard_map.60 = (bf16[64,1152]{1,0:T(8,128)(2,1)S(1)}, bf16[64,1152]{1,0:T(8,128)(2,1)S(1)}, bf16[64,1152]{1,0:T(8,128)(2,1)S(1)}, bf16[64,1152]{1,0:T(8,128)(2,1)S(1)}) custom-call(s32[2]{0:T(128)S(1)} %copy-done.5, bf16[64,1024]{1,0:T(8,128)(2,1)S(1)} %slice_select_fusion.refs_0_, bf16[64,1024]{1,0:T(8,128)(2,1)S(1)} %collective-permute-done.7.refs_1_, ...), custom_call_target="tpu_custom_call" | custom-call | flops 1 | bytes 1 | tf_op jit(solution)/shard_map/pallas_call | solution.py:327
  58.1 4.1 %collective-permute-start.13 = (bf16[64,1152]{1,0:T(8,128)(2,1)S(1)}, bf16[64,1152]{1,0:T(8,128)(2,1)S(1)}, u32[]{:S(2)}, u32[]{:S(2)}) collective-permute-start(bf16[64,1152]{1,0:T(8,128)(2,1)S(1)} %get-tuple-element.34), channel_id=1, source_target_pairs={{0,12},{4,0},{8,4},{12,8},{1,13},{5,1},{9,5},{13,9},{2,14},{6,2},{... | collective-permute-start | bytes 442376 | tf_op jit(solution)/shard_map/ppermute | solution.py:358
  62.2 0.0 collective-permute-start.14
  62.2 1.0 collective-permute-start.15
  63.2 3.3 %collective-permute-done.13.refs_1_ = bf16[64,1152]{1,0:T(8,128)(2,1)S(1)} collective-permute-done((bf16[64,1152]{1,0:T(8,128)(2,1)S(1)}, bf16[64,1152]{1,0:T(8,128)(2,1)S(1)}, u32[]{:S(2)}, u32[]{:S(2)}) %collective-permute-start.13) | collective-permute-done | bytes 147488 | tf_op jit(solution)/shard_map/ppermute | solution.py:358
  66.5 8.0 %collective-permute-done.14.refs_2_ = bf16[64,1152]{1,0:T(8,128)(2,1)S(1)} collective-permute-done((bf16[64,1152]{1,0:T(8,128)(2,1)S(1)}, bf16[64,1152]{1,0:T(8,128)(2,1)S(1)}, u32[]{:S(2)}, u32[]{:S(2)}) %collective-permute-start.14) | collective-permute-done | bytes 147488 | tf_op jit(solution)/shard_map/ppermute | solution.py:358
  74.5 0.0 collective-permute-done.15.refs_3_
  74.5 0.8 shard_map.61.before.first_context
  75.3 4.3 %collective-permute-start.16 = (bf16[64,1024]{1,0:T(8,128)(2,1)S(1)}, bf16[64,1024]{1,0:T(8,128)(2,1)S(1)}, u32[]{:S(2)}, u32[]{:S(2)}) collective-permute-start(bf16[64,1024]{1,0:T(8,128)(2,1)S(1)} %shard_map.61.before.first_context), channel_id=1, source_target_pairs={{0,16},{1,17},{2,18},{3,19},{4,20},{5,21},{6,22},{7,23},{8,24},{9,... | collective-permute-start | bytes 393224 | tf_op jit(solution)/shard_map/ppermute | solution.py:364
  79.7 0.1 shard_map.62.weights
  79.8 0.0 copy-start.3
  79.8 2.4 %collective-permute-done.16.second_context = bf16[64,1024]{1,0:T(8,128)(2,1)S(1)} collective-permute-done((bf16[64,1024]{1,0:T(8,128)(2,1)S(1)}, bf16[64,1024]{1,0:T(8,128)(2,1)S(1)}, u32[]{:S(2)}, u32[]{:S(2)}) %collective-permute-start.16) | collective-permute-done | bytes 131104 | tf_op jit(solution)/shard_map/ppermute | solution.py:364
  82.1 0.7 collective-permute-start.17
  82.9 0.0 collective-permute-done.17.other.sibling
  82.9 0.7 collective-permute-start.18
  83.6 1.3 %collective-permute-start.19 = (bf16[512,128]{1,0:T(8,128)(2,1)S(1)}, bf16[512,128]{1,0:T(8,128)(2,1)S(1)}, u32[]{:S(2)}, u32[]{:S(2)}) collective-permute-start(bf16[512,128]{1,0:T(8,128)(2,1)S(1)} %get-tuple-element.39), channel_id=1, source_target_pairs={{16,0},{17,1},{18,2},{19,3},{20,4},{21,5},{22,6},{23,7},{24,8},{25... | collective-permute-start | bytes 393224 | tf_op jit(solution)/shard_map/ppermute | solution.py:361
  84.9 1.3 %collective-permute-start.20 = (bf16[512,128]{1,0:T(8,128)(2,1)S(1)}, bf16[512,128]{1,0:T(8,128)(2,1)S(1)}, u32[]{:S(2)}, u32[]{:S(2)}) collective-permute-start(bf16[512,128]{1,0:T(8,128)(2,1)S(1)} %get-tuple-element.40), channel_id=1, source_target_pairs={{16,2},{17,3},{18,0},{19,1},{20,6},{21,7},{22,4},{23,5},{24,10},{2... | collective-permute-start | bytes 393224 | tf_op jit(solution)/shard_map/ppermute | solution.py:473
  86.2 0.0 collective-permute-done.18.across
  86.2 12.8 %collective-permute-done.19.direct = bf16[512,128]{1,0:T(8,128)(2,1)S(1)} collective-permute-done((bf16[512,128]{1,0:T(8,128)(2,1)S(1)}, bf16[512,128]{1,0:T(8,128)(2,1)S(1)}, u32[]{:S(2)}, u32[]{:S(2)}) %collective-permute-start.19) | collective-permute-done | bytes 131104 | tf_op jit(solution)/shard_map/ppermute | solution.py:361
  99.0 1.7 %collective-permute-done.20.diagonal = bf16[512,128]{1,0:T(8,128)(2,1)S(1)} collective-permute-done((bf16[512,128]{1,0:T(8,128)(2,1)S(1)}, bf16[512,128]{1,0:T(8,128)(2,1)S(1)}, u32[]{:S(2)}, u32[]{:S(2)}) %collective-permute-start.20) | collective-permute-done | bytes 131104 | tf_op jit(solution)/shard_map/ppermute | solution.py:473
  100.7 0.0 copy-done.3
  100.7 0.8 shard_map.66
  (6 shorter events, 0.1 us)
Async XLA Ops:
  0.0 11.0 %collective-permute-start.1 = (bf16[128,1024]{1,0:T(8,128)(2,1)}, bf16[128,1024]{1,0:T(8,128)(2,1)S(1)}, u32[]{:S(2)}, u32[]{:S(2)}) collective-permute-start(bf16[128,1024]{1,0:T(8,128)(2,1)} %bitcast.9), channel_id=1, source_target_pairs={{16,18},{17,19},{18,16},{19,17},{20,22},{21,23},{22,20},{23,21},{2... | collective-permute-start | bytes 786440 | tf_op jit(solution)/shard_map/ppermute | solution.py:355
  1.8 17.5 %collective-permute-start.5 = (bf16[256,1024]{1,0:T(8,128)(2,1)S(1)}, bf16[256,1024]{1,0:T(8,128)(2,1)S(1)}, u32[]{:S(2)}, u32[]{:S(2)}) collective-permute-start(bf16[256,1024]{1,0:T(8,128)(2,1)S(1)} %slice_bitcast_fusion), channel_id=1, source_target_pairs={{0,2},{1,3},{2,0},{3,1},{4,6},{5,7},{6,4},{7,5},{8,10},{9,11},{10,... | collective-permute-start | bytes 1572872 | tf_op jit(solution)/shard_map/ppermute | solution.py:355
  6.6 16.4 %collective-permute-start.4 = (bf16[512,1024]{1,0:T(8,128)(2,1)}, bf16[512,1024]{1,0:T(8,128)(2,1)S(1)}, u32[]{:S(2)}, u32[]{:S(2)}) collective-permute-start(bf16[512,1024]{1,0:T(8,128)(2,1)} %bitcast.5), channel_id=1, source_target_pairs={{0,1},{1,0},{2,3},{3,2},{4,5},{5,4},{6,7},{7,6},{8,9},{9,8},{10,11... | collective-permute-start | bytes 3145736 | tf_op jit(solution)/shard_map/ppermute | solution.py:355
  8.6 6.2 %collective-permute-start = (bf16[128,1024]{1,0:T(8,128)(2,1)}, bf16[128,1024]{1,0:T(8,128)(2,1)S(1)}, u32[]{:S(2)}, u32[]{:S(2)}) collective-permute-start(bf16[128,1024]{1,0:T(8,128)(2,1)} %bitcast.10), channel_id=1, source_target_pairs={{16,17},{17,16},{18,19},{19,18},{20,21},{21,20},{22,23},{23,22},{2... | collective-permute-start | bytes 786440 | tf_op jit(solution)/shard_map/ppermute | solution.py:355
  9.3 1.0 copy-start.1
  10.2 0.7 copy-start.4
  11.0 3.8 %collective-permute-start.2 = (bf16[128,1024]{1,0:T(8,128)(2,1)S(1)}, bf16[128,1024]{1,0:T(8,128)(2,1)S(1)}, u32[]{:S(2)}, u32[]{:S(2)}) collective-permute-start(bf16[128,1024]{1,0:T(8,128)(2,1)S(1)} %collective-permute-done.1.x2), channel_id=1, source_target_pairs={{16,17},{17,16},{18,19},{19,18},{20,21},{21,20},{22,23},{23,22},{2... | collective-permute-start | bytes 786440 | tf_op jit(solution)/shard_map/ppermute | solution.py:355
  12.8 19.8 %collective-permute-start.10 = (bf16[320,1024]{1,0:T(8,128)(2,1)S(1)}, bf16[320,1024]{1,0:T(8,128)(2,1)S(1)}, u32[]{:S(2)}, u32[]{:S(2)}) collective-permute-start(bf16[320,1024]{1,0:T(8,128)(2,1)S(1)} %slice.16), channel_id=1, source_target_pairs={{0,2},{1,3},{2,0},{3,1},{4,6},{5,7},{6,4},{7,5},{8,10},{9,11},{10,... | collective-permute-start | bytes 1966088 | tf_op jit(solution)/shard_map/ppermute | solution.py:355
  14.8 3.6 %copy-start.2 = (bf16[128,512]{1,0:T(8,128)(2,1)}, bf16[128,512]{1,0:T(8,128)(2,1)S(1)}, u32[]{:S(2)}) copy-start(bf16[128,512]{1,0:T(8,128)(2,1)S(1)} %get-tuple-element.38.residual1) | copy-start | bytes 393220
  14.8 8.2 %copy-start = (bf16[2,256,1024]{2,1,0:T(8,128)(2,1)S(1)}, bf16[2,256,1024]{2,1,0:T(8,128)(2,1)}, u32[]{:S(2)}) copy-start(bf16[2,256,1024]{2,1,0:T(8,128)(2,1)} %param.5) | copy-start | bytes 3145732
  19.2 3.8 %collective-permute-start.6 = (bf16[256,1024]{1,0:T(8,128)(2,1)S(1)}, bf16[256,1024]{1,0:T(8,128)(2,1)S(1)}, u32[]{:S(2)}, u32[]{:S(2)}) collective-permute-start(bf16[256,1024]{1,0:T(8,128)(2,1)S(1)} %collective-permute-done.5.x2), channel_id=1, source_target_pairs={{0,1},{1,0},{2,3},{3,2},{4,5},{5,4},{6,7},{7,6},{8,9},{9,8},{10,11... | collective-permute-start | bytes 1572872 | tf_op jit(solution)/shard_map/ppermute | solution.py:355
  21.2 11.3 %collective-permute-start.3 = (bf16[128,1024]{1,0:T(8,128)(2,1)S(1)}, bf16[128,1024]{1,0:T(8,128)(2,1)S(1)}, u32[]{:S(2)}, u32[]{:S(2)}) collective-permute-start(bf16[128,1024]{1,0:T(8,128)(2,1)S(1)} %get-tuple-element.26.before), channel_id=1, source_target_pairs={{16,0},{17,1},{18,2},{19,3},{20,4},{21,5},{22,6},{23,7},{24,8},{25... | collective-permute-start | bytes 786440 | tf_op jit(solution)/shard_map/ppermute | solution.py:361
  30.1 24.6 %collective-permute-start.12 = (bf16[2,256,1024]{2,1,0:T(8,128)(2,1)}, bf16[2,256,1024]{2,1,0:T(8,128)(2,1)}, u32[]{:S(2)}, u32[]{:S(2)}) collective-permute-start(bf16[2,256,1024]{2,1,0:T(8,128)(2,1)} %shard_map.58), channel_id=1, source_target_pairs={{0,16},{1,17},{2,18},{3,19},{4,20},{5,21},{6,22},{7,23},{8,24},{9,... | collective-permute-start | bytes 3145736 | tf_op jit(solution)/shard_map/ppermute | solution.py:364
  32.6 7.9 %collective-permute-start.11 = (bf16[256,1024]{1,0:T(8,128)(2,1)S(1)}, bf16[256,1024]{1,0:T(8,128)(2,1)S(1)}, u32[]{:S(2)}, u32[]{:S(2)}) collective-permute-start(bf16[256,1024]{1,0:T(8,128)(2,1)S(1)} %slice.15.x2), channel_id=1, source_target_pairs={{0,1},{1,0},{2,3},{3,2},{4,5},{5,4},{6,7},{7,6},{8,9},{9,8},{10,11... | collective-permute-start | bytes 1572872 | tf_op jit(solution)/shard_map/ppermute | solution.py:355
  34.6 20.1 %copy-start.5 = (s32[2]{0:T(128)S(1)}, s32[2]{0:T(128)}, u32[]{:S(2)}) copy-start(s32[2]{0:T(128)} %lengths.1) | copy-start | bytes 28
  34.6 13.6 %collective-permute-start.7 = (bf16[64,1024]{1,0:T(8,128)(2,1)S(1)}, bf16[64,1024]{1,0:T(8,128)(2,1)S(1)}, u32[]{:S(2)}, u32[]{:S(2)}) collective-permute-start(bf16[64,1024]{1,0:T(8,128)(2,1)S(1)} %slice_select_fusion.refs_0_), channel_id=1, source_target_pairs={{0,4},{4,8},{8,12},{12,0},{1,5},{5,9},{9,13},{13,1},{2,6},{6,10},{... | collective-permute-start | bytes 393224 | tf_op jit(solution)/shard_map/ppermute | solution.py:358
  36.6 11.7 %collective-permute-start.8 = (bf16[64,1024]{1,0:T(8,128)(2,1)S(1)}, bf16[64,1024]{1,0:T(8,128)(2,1)S(1)}, u32[]{:S(2)}, u32[]{:S(2)}) collective-permute-start(bf16[64,1024]{1,0:T(8,128)(2,1)S(1)} %slice_select_fusion.refs_0_), channel_id=1, source_target_pairs={{0,8},{4,12},{8,0},{12,4},{1,9},{5,13},{9,1},{13,5},{2,10},{6,14},... | collective-permute-start | bytes 393224 | tf_op jit(solution)/shard_map/ppermute | solution.py:358
  39.2 9.1 %collective-permute-start.9 = (bf16[64,1024]{1,0:T(8,128)(2,1)S(1)}, bf16[64,1024]{1,0:T(8,128)(2,1)S(1)}, u32[]{:S(2)}, u32[]{:S(2)}) collective-permute-start(bf16[64,1024]{1,0:T(8,128)(2,1)S(1)} %slice_select_fusion.refs_0_), channel_id=1, source_target_pairs={{0,12},{4,0},{8,4},{12,8},{1,13},{5,1},{9,5},{13,9},{2,14},{6,2},{... | collective-permute-start | bytes 393224 | tf_op jit(solution)/shard_map/ppermute | solution.py:358
  58.1 8.4 %collective-permute-start.13 = (bf16[64,1152]{1,0:T(8,128)(2,1)S(1)}, bf16[64,1152]{1,0:T(8,128)(2,1)S(1)}, u32[]{:S(2)}, u32[]{:S(2)}) collective-permute-start(bf16[64,1152]{1,0:T(8,128)(2,1)S(1)} %get-tuple-element.34), channel_id=1, source_target_pairs={{0,12},{4,0},{8,4},{12,8},{1,13},{5,1},{9,5},{13,9},{2,14},{6,2},{... | collective-permute-start | bytes 442376 | tf_op jit(solution)/shard_map/ppermute | solution.py:358
  62.2 12.3 %collective-permute-start.14 = (bf16[64,1152]{1,0:T(8,128)(2,1)S(1)}, bf16[64,1152]{1,0:T(8,128)(2,1)S(1)}, u32[]{:S(2)}, u32[]{:S(2)}) collective-permute-start(bf16[64,1152]{1,0:T(8,128)(2,1)S(1)} %get-tuple-element.35), channel_id=1, source_target_pairs={{0,8},{4,12},{8,0},{12,4},{1,9},{5,13},{9,1},{13,5},{2,10},{6,14},... | collective-permute-start | bytes 442376 | tf_op jit(solution)/shard_map/ppermute | solution.py:358
  62.2 12.3 %collective-permute-start.15 = (bf16[64,1152]{1,0:T(8,128)(2,1)S(1)}, bf16[64,1152]{1,0:T(8,128)(2,1)S(1)}, u32[]{:S(2)}, u32[]{:S(2)}) collective-permute-start(bf16[64,1152]{1,0:T(8,128)(2,1)S(1)} %get-tuple-element.36), channel_id=1, source_target_pairs={{0,4},{4,8},{8,12},{12,0},{1,5},{5,9},{9,13},{13,1},{2,6},{6,10},{... | collective-permute-start | bytes 442376 | tf_op jit(solution)/shard_map/ppermute | solution.py:358
  75.3 6.8 %collective-permute-start.16 = (bf16[64,1024]{1,0:T(8,128)(2,1)S(1)}, bf16[64,1024]{1,0:T(8,128)(2,1)S(1)}, u32[]{:S(2)}, u32[]{:S(2)}) collective-permute-start(bf16[64,1024]{1,0:T(8,128)(2,1)S(1)} %shard_map.61.before.first_context), channel_id=1, source_target_pairs={{0,16},{1,17},{2,18},{3,19},{4,20},{5,21},{6,22},{7,23},{8,24},{9,... | collective-permute-start | bytes 393224 | tf_op jit(solution)/shard_map/ppermute | solution.py:364
  79.8 21.0 %copy-start.3 = (bf16[128,512]{1,0:T(8,128)(2,1)S(1)}, bf16[128,512]{1,0:T(8,128)(2,1)}, u32[]{:S(2)}) copy-start(bf16[128,512]{1,0:T(8,128)(2,1)} %copy-done.2) | copy-start | bytes 393220
  82.1 0.7 collective-permute-start.17
  82.9 3.3 %collective-permute-start.18 = (bf16[512,128]{1,0:T(8,128)(2,1)S(1)}, bf16[512,128]{1,0:T(8,128)(2,1)S(1)}, u32[]{:S(2)}, u32[]{:S(2)}) collective-permute-start(bf16[512,128]{1,0:T(8,128)(2,1)S(1)} %get-tuple-element.37), channel_id=1, source_target_pairs={{16,18},{17,19},{18,16},{19,17},{20,22},{21,23},{22,20},{23,21},{2... | collective-permute-start | bytes 393224 | tf_op jit(solution)/shard_map/ppermute | solution.py:355
  83.6 15.4 %collective-permute-start.19 = (bf16[512,128]{1,0:T(8,128)(2,1)S(1)}, bf16[512,128]{1,0:T(8,128)(2,1)S(1)}, u32[]{:S(2)}, u32[]{:S(2)}) collective-permute-start(bf16[512,128]{1,0:T(8,128)(2,1)S(1)} %get-tuple-element.39), channel_id=1, source_target_pairs={{16,0},{17,1},{18,2},{19,3},{20,4},{21,5},{22,6},{23,7},{24,8},{25... | collective-permute-start | bytes 393224 | tf_op jit(solution)/shard_map/ppermute | solution.py:361
  84.9 15.9 %collective-permute-start.20 = (bf16[512,128]{1,0:T(8,128)(2,1)S(1)}, bf16[512,128]{1,0:T(8,128)(2,1)S(1)}, u32[]{:S(2)}, u32[]{:S(2)}) collective-permute-start(bf16[512,128]{1,0:T(8,128)(2,1)S(1)} %get-tuple-element.40), channel_id=1, source_target_pairs={{16,2},{17,3},{18,0},{19,1},{20,6},{21,7},{22,4},{23,5},{24,10},{2... | collective-permute-start | bytes 393224 | tf_op jit(solution)/shard_map/ppermute | solution.py:473

commit v4 on v3

--- a/solution.py
+++ b/solution.py
@@ -157,7 +157,7 @@
     @pl.when(info[0] == 0)
     def _():
         stream = WeightStream(weights, [(1, block) for block in blocks], width, wbuf, sem)
-        rows = normed_rows((x0[:span], x1[:span], x2[...], x3[...]), gains, blocks)
+        rows = normed_rows((x0[...], x1[:span], x2[...], x3[...]), gains, blocks)
         total = None
         for part, block in zip(rows, blocks):
             matrix = key_weights[pl.ds(pl.multiple_of(block * width, width), width), :]
@@ -226,8 +226,13 @@
             outs[base + j][:, head_width:] = packed[j * pos : (j + 1) * pos].astype(bf16)
 
 
-def combine_kernel(*refs):
-    sources, out = (refs[:-1], refs[-1])
+def combine_kernel(section, *refs):
+    @pl.when(position()[0] == section)
+    def _():
+        combine(refs[:-1], refs[-1])
+
+
+def combine(sources, out):
     head_width = out.shape[1]
     heads = head_width // DKV
     low = lax.broadcasted_iota(jnp.int32, (1, PAIR), 1) < DKV
@@ -418,7 +423,7 @@
     made = call(
         first_memory_kernel,
         shape(2, span, head_width),
-        (mem, mem_c, far, far_c, gains, key_weights, weights),
+        (first_rows, mem_c, far, far_c, gains, key_weights, weights),
         [VMEM] * 6 + [ANY],
         weight_scratch(1),
     )
@@ -440,13 +445,18 @@
         [SMEM] + [VMEM] * (count + 2),
     )
     sources = [partial[0]] + [along_seq(partial[by], -by) for by in range(1, count)]
-    context = call(
-        combine_kernel,
-        shape(pos, head_width),
-        tuple(sources),
-        [VMEM] * count,
-    )
-    second_context = to_decoder(context)
+    def combined(section, sources):
+        return call(
+            functools.partial(combine_kernel, section),
+            shape(pos, head_width),
+            tuple(sources),
+            [VMEM] * count,
+        )
+
+    second_context = combined(0, sources)
+    sources[0], _ = after((sources[0], second_context))
+    context = combined(1, sources)
+    second_context = to_decoder(second_context)
 
     last_weights = load(1, 1, context)
     block = 4 * width // 8

time: 102 us -> 101 us (level)
    pallas_call x12 -> x13, Pallas kernels: 23.5 us -> 23.4 us  [call(): pl.pallas_call(kernel, out_shape=out_shapes, in_specs=specs, out_specs=ou...]
where the time goes in v4:
time: 101 us
  starting transfers between devices  36.6 us (36%)
  waiting for transfers between devices  36.4 us (36%)
  Pallas kernels  23.4 us (23%)
  local copies, waits for them, and re-layouts  3.93 us (4%)
    pallas_call x13, Pallas kernels, call(): pl.pallas_call(kernel, out_shape=out_shapes, in_specs=specs, out_specs=ou...  23.4 us
    ppermute x10, starting transfers between devices, in_section(): return lax.ppermute(array, ('segment', 'mp'), pairs)  15.9 us
    ppermute x2, waiting for transfers between devices, to_encoder(): return lax.ppermute(array, 'segment', [(1, 0)])  12.8 us
    ppermute x6, waiting for transfers between devices, along_seq(): lax.ppermute(array, 'seq', [(i, (i + by) % count) for i in range(count)])  11.5 us
    ppermute x6, starting transfers between devices, along_seq(): lax.ppermute(array, 'seq', [(i, (i + by) % count) for i in range(count)])  11.1 us
    ppermute x2, waiting for transfers between devices, to_decoder(): return lax.ppermute(array, 'segment', [(0, 1)])  8.7 us
    ppermute x2, starting transfers between devices, to_decoder(): return lax.ppermute(array, 'segment', [(0, 1)])  5.75 us
    ppermute x2, starting transfers between devices, to_encoder(): return lax.ppermute(array, 'segment', [(1, 0)])  2.58 us
  transfers between devices with their start and end apart: 21, of which 10 were waited for; matrix products, arithmetic and copies ran while one was open for 2% of the time, Pallas kernels for 18%

profile of v4, /device:TPU:0, one launch (start us, length us, event | category | flops | bytes accessed | tf_op | source)
XLA Modules:
  0.0 100.7 jit_solution(10987068349560270589)
XLA Ops:
  0.0 0.7 collective-permute-start.1
  0.7 1.1 %slice_bitcast_fusion.x0 = bf16[256,1024]{1,0:T(8,128)(2,1)S(1)} fusion(bf16[2,256,1024]{2,1,0:T(8,128)(2,1)} %param.5), kind=kLoop, calls=%fused_computation | loop fusion | bytes 1048576 | tf_op jit(solution)/shard_map/squeeze | solution.py:375
  1.8 4.9 %collective-permute-start.5 = (bf16[256,1024]{1,0:T(8,128)(2,1)S(1)}, bf16[256,1024]{1,0:T(8,128)(2,1)S(1)}, u32[]{:S(2)}, u32[]{:S(2)}) collective-permute-start(bf16[256,1024]{1,0:T(8,128)(2,1)S(1)} %slice_bitcast_fusion.x0), channel_id=1, source_target_pairs={{0,2},{1,3},{2,0},{3,1},{4,6},{5,7},{6,4},{7,5},{8,10},{9,11},{10,... | collective-permute-start | bytes 1572872 | tf_op jit(solution)/shard_map/ppermute | solution.py:360
  6.6 1.9 %collective-permute-start.4 = (bf16[512,1024]{1,0:T(8,128)(2,1)}, bf16[512,1024]{1,0:T(8,128)(2,1)S(1)}, u32[]{:S(2)}, u32[]{:S(2)}) collective-permute-start(bf16[512,1024]{1,0:T(8,128)(2,1)} %bitcast.5), channel_id=1, source_target_pairs={{0,1},{1,0},{2,3},{3,2},{4,5},{5,4},{6,7},{7,6},{8,9},{9,8},{10,11... | collective-permute-start | bytes 3145736 | tf_op jit(solution)/shard_map/ppermute | solution.py:360
  8.6 0.7 collective-permute-start
  9.3 0.0 copy-start.1
  9.3 0.9 copy-done.1
  10.2 0.0 copy-start.4
  10.2 0.7 copy-done.4
  11.0 0.0 collective-permute-done.1.x2
  11.0 0.7 collective-permute-start.2
  11.7 1.1 %slice.16 = bf16[320,1024]{1,0:T(8,128)(2,1)S(1)} slice(bf16[512,1024]{1,0:T(8,128)(2,1)} %bitcast.6), slice={[192:512], [0:1024]} | slice | bytes 1310720 | tf_op jit(solution)/shard_map/slice | solution.py:377
  12.8 1.9 %collective-permute-start.10 = (bf16[320,1024]{1,0:T(8,128)(2,1)S(1)}, bf16[320,1024]{1,0:T(8,128)(2,1)S(1)}, u32[]{:S(2)}, u32[]{:S(2)}) collective-permute-start(bf16[320,1024]{1,0:T(8,128)(2,1)S(1)} %slice.16), channel_id=1, source_target_pairs={{0,2},{1,3},{2,0},{3,1},{4,6},{5,7},{6,4},{7,5},{8,10},{9,11},{10,... | collective-permute-start | bytes 1966088 | tf_op jit(solution)/shard_map/ppermute | solution.py:360
  14.7 0.0 collective-permute-done.x1
  14.7 0.0 collective-permute-done.2.x3
  14.7 0.1 shard_map.56
  14.8 0.0 copy-start.2
  14.8 3.5 %shard_map.57.key_weights = bf16[4096,1024]{1,0:T(8,128)(2,1)S(1)} custom-call(bf16[1,2,4096,1024]{3,2,1,0:T(8,128)(2,1)} %weights.9, bf16[128,1024]{1,0:T(8,128)(2,1)S(1)} %get-tuple-element.27.before), custom_call_target="tpu_custom_call" | custom-call | flops 1 | bytes 1 | tf_op jit(solution)/shard_map/pallas_call | solution.py:332
  18.4 0.0 copy-done.2
  18.4 0.0 copy-start
  18.4 0.8 collective-permute-done.5.x2
  19.2 1.9 %collective-permute-start.6 = (bf16[256,1024]{1,0:T(8,128)(2,1)S(1)}, bf16[256,1024]{1,0:T(8,128)(2,1)S(1)}, u32[]{:S(2)}, u32[]{:S(2)}) collective-permute-start(bf16[256,1024]{1,0:T(8,128)(2,1)S(1)} %collective-permute-done.5.x2), channel_id=1, source_target_pairs={{0,1},{1,0},{2,3},{3,2},{4,5},{5,4},{6,7},{7,6},{8,9},{9,8},{10,11... | collective-permute-start | bytes 1572872 | tf_op jit(solution)/shard_map/ppermute | solution.py:360
  21.2 1.3 %collective-permute-start.3 = (bf16[128,1024]{1,0:T(8,128)(2,1)S(1)}, bf16[128,1024]{1,0:T(8,128)(2,1)S(1)}, u32[]{:S(2)}, u32[]{:S(2)}) collective-permute-start(bf16[128,1024]{1,0:T(8,128)(2,1)S(1)} %get-tuple-element.27.before), channel_id=1, source_target_pairs={{16,0},{17,1},{18,2},{19,3},{20,4},{21,5},{22,6},{23,7},{24,8},{25... | collective-permute-start | bytes 786440 | tf_op jit(solution)/shard_map/ppermute | solution.py:366
  22.5 0.6 collective-permute-done.6.x3
  23.0 0.0 collective-permute-done.4.x1
  23.0 7.1 %shard_map.58 = bf16[2,256,1024]{2,1,0:T(8,128)(2,1)} custom-call(bf16[256,1024]{1,0:T(8,128)(2,1)S(1)} %slice_bitcast_fusion.x0, bf16[512,1024]{1,0:T(8,128)(2,1)S(1)} %collective-permute-done.4.x1, bf16[256,1024]{1,0:T(8,128)(2,1)S(1)} %collective-permute-done.5.x2, bf16[256,1024]{1,0:T(8,128)(2,1)S(1)} %collective-permute-done.6.x3, ...), custom_call_target="tpu_custom_call" | custom-call | flops 1 | bytes 1 | tf_op jit(solution)/shard_map/pallas_call | solution.py:332
  30.1 2.3 %collective-permute-start.12 = (bf16[2,256,1024]{2,1,0:T(8,128)(2,1)}, bf16[2,256,1024]{2,1,0:T(8,128)(2,1)}, u32[]{:S(2)}, u32[]{:S(2)}) collective-permute-start(bf16[2,256,1024]{2,1,0:T(8,128)(2,1)} %shard_map.58), channel_id=1, source_target_pairs={{0,16},{1,17},{2,18},{3,19},{4,20},{5,21},{6,22},{7,23},{8,24},{9,... | collective-permute-start | bytes 3145736 | tf_op jit(solution)/shard_map/ppermute | solution.py:369
  32.4 0.0 collective-permute-done.3.residual0
  32.4 0.2 collective-permute-done.10
  32.6 1.9 %collective-permute-start.11 = (bf16[256,1024]{1,0:T(8,128)(2,1)S(1)}, bf16[256,1024]{1,0:T(8,128)(2,1)S(1)}, u32[]{:S(2)}, u32[]{:S(2)}) collective-permute-start(bf16[256,1024]{1,0:T(8,128)(2,1)S(1)} %slice.15.x2), channel_id=1, source_target_pairs={{0,1},{1,0},{2,3},{3,2},{4,5},{5,4},{6,7},{7,6},{8,9},{9,8},{10,11... | collective-permute-start | bytes 1572872 | tf_op jit(solution)/shard_map/ppermute | solution.py:360
  34.6 0.0 copy-start.5
  34.6 2.0 %collective-permute-start.7 = (bf16[64,1024]{1,0:T(8,128)(2,1)S(1)}, bf16[64,1024]{1,0:T(8,128)(2,1)S(1)}, u32[]{:S(2)}, u32[]{:S(2)}) collective-permute-start(bf16[64,1024]{1,0:T(8,128)(2,1)S(1)} %slice_select_fusion.refs_0_), channel_id=1, source_target_pairs={{0,4},{4,8},{8,12},{12,0},{1,5},{5,9},{9,13},{13,1},{2,6},{6,10},{... | collective-permute-start | bytes 393224 | tf_op jit(solution)/shard_map/ppermute | solution.py:363
  36.6 2.6 %collective-permute-start.8 = (bf16[64,1024]{1,0:T(8,128)(2,1)S(1)}, bf16[64,1024]{1,0:T(8,128)(2,1)S(1)}, u32[]{:S(2)}, u32[]{:S(2)}) collective-permute-start(bf16[64,1024]{1,0:T(8,128)(2,1)S(1)} %slice_select_fusion.refs_0_), channel_id=1, source_target_pairs={{0,8},{4,12},{8,0},{12,4},{1,9},{5,13},{9,1},{13,5},{2,10},{6,14},... | collective-permute-start | bytes 393224 | tf_op jit(solution)/shard_map/ppermute | solution.py:363
  39.2 1.4 %collective-permute-start.9 = (bf16[64,1024]{1,0:T(8,128)(2,1)S(1)}, bf16[64,1024]{1,0:T(8,128)(2,1)S(1)}, u32[]{:S(2)}, u32[]{:S(2)}) collective-permute-start(bf16[64,1024]{1,0:T(8,128)(2,1)S(1)} %slice_select_fusion.refs_0_), channel_id=1, source_target_pairs={{0,12},{4,0},{8,4},{12,8},{1,13},{5,1},{9,5},{13,9},{2,14},{6,2},{... | collective-permute-start | bytes 393224 | tf_op jit(solution)/shard_map/ppermute | solution.py:363
  40.6 0.0 collective-permute-done.11.x3
  40.6 0.0 copy-done
  40.6 7.6 %shard_map.59.refs_4_ = bf16[2,256,1024]{2,1,0:T(8,128)(2,1)S(1)} custom-call(bf16[512,1024]{1,0:T(8,128)(2,1)S(1)} %bitcast.7, bf16[512,1024]{1,0:T(8,128)(2,1)S(1)} %collective-permute-done.4.x1, bf16[256,1024]{1,0:T(8,128)(2,1)S(1)} %slice.15.x2, bf16[256,1024]{1,0:T(8,128)(2,1)S(1)} %collective-permute-done.11.x3, ...), custom_call_target="tpu_custom_call" | custom-call | flops 4800000000 | bytes 1 | tf_op jit(solution)/shard_map/pallas_call | solution.py:332
  48.2 0.0 collective-permute-done.7.refs_1_
  48.2 0.2 collective-permute-done.8.refs_2_
  48.4 0.0 collective-permute-done.9.refs_3_
  48.4 6.4 %collective-permute-done.12.refs_5_ = bf16[2,256,1024]{2,1,0:T(8,128)(2,1)} collective-permute-done((bf16[2,256,1024]{2,1,0:T(8,128)(2,1)}, bf16[2,256,1024]{2,1,0:T(8,128)(2,1)}, u32[]{:S(2)}, u32[]{:S(2)}) %collective-permute-start.12) | collective-permute-done | bytes 1048608 | tf_op jit(solution)/shard_map/ppermute | solution.py:369
  54.7 0.0 copy-done.5
  54.7 3.3 %shard_map.60 = (bf16[64,1152]{1,0:T(8,128)(2,1)S(1)}, bf16[64,1152]{1,0:T(8,128)(2,1)S(1)}, bf16[64,1152]{1,0:T(8,128)(2,1)S(1)}, bf16[64,1152]{1,0:T(8,128)(2,1)S(1)}) custom-call(s32[2]{0:T(128)S(1)} %copy-done.5, bf16[64,1024]{1,0:T(8,128)(2,1)S(1)} %slice_select_fusion.refs_0_, bf16[64,1024]{1,0:T(8,128)(2,1)S(1)} %collective-permute-done.7.refs_1_, ...), custom_call_target="tpu_custom_call" | custom-call | flops 1 | bytes 1 | tf_op jit(solution)/shard_map/pallas_call | solution.py:332
  58.1 4.1 %collective-permute-start.13 = (bf16[64,1152]{1,0:T(8,128)(2,1)S(1)}, bf16[64,1152]{1,0:T(8,128)(2,1)S(1)}, u32[]{:S(2)}, u32[]{:S(2)}) collective-permute-start(bf16[64,1152]{1,0:T(8,128)(2,1)S(1)} %get-tuple-element.35), channel_id=1, source_target_pairs={{0,12},{4,0},{8,4},{12,8},{1,13},{5,1},{9,5},{13,9},{2,14},{6,2},{... | collective-permute-start | bytes 442376 | tf_op jit(solution)/shard_map/ppermute | solution.py:363
  62.2 0.0 collective-permute-start.14
  62.2 1.0 %collective-permute-start.15 = (bf16[64,1152]{1,0:T(8,128)(2,1)S(1)}, bf16[64,1152]{1,0:T(8,128)(2,1)S(1)}, u32[]{:S(2)}, u32[]{:S(2)}) collective-permute-start(bf16[64,1152]{1,0:T(8,128)(2,1)S(1)} %get-tuple-element.37), channel_id=1, source_target_pairs={{0,4},{4,8},{8,12},{12,0},{1,5},{5,9},{9,13},{13,1},{2,6},{6,10},{... | collective-permute-start | bytes 442376 | tf_op jit(solution)/shard_map/ppermute | solution.py:363
  63.2 3.3 %collective-permute-done.13.refs_1_ = bf16[64,1152]{1,0:T(8,128)(2,1)S(1)} collective-permute-done((bf16[64,1152]{1,0:T(8,128)(2,1)S(1)}, bf16[64,1152]{1,0:T(8,128)(2,1)S(1)}, u32[]{:S(2)}, u32[]{:S(2)}) %collective-permute-start.13) | collective-permute-done | bytes 147488 | tf_op jit(solution)/shard_map/ppermute | solution.py:363
  66.5 8.0 %collective-permute-done.14.refs_2_ = bf16[64,1152]{1,0:T(8,128)(2,1)S(1)} collective-permute-done((bf16[64,1152]{1,0:T(8,128)(2,1)S(1)}, bf16[64,1152]{1,0:T(8,128)(2,1)S(1)}, u32[]{:S(2)}, u32[]{:S(2)}) %collective-permute-start.14) | collective-permute-done | bytes 147488 | tf_op jit(solution)/shard_map/ppermute | solution.py:363
  74.4 0.0 collective-permute-done.15.refs_3_
  74.5 0.8 shard_map.61
  75.3 3.5 %collective-permute-start.16 = (bf16[64,1024]{1,0:T(8,128)(2,1)S(1)}, bf16[64,1024]{1,0:T(8,128)(2,1)S(1)}, u32[]{:S(2)}, u32[]{:S(2)}) collective-permute-start(bf16[64,1024]{1,0:T(8,128)(2,1)S(1)} %shard_map.61), channel_id=1, source_target_pairs={{0,16},{1,17},{2,18},{3,19},{4,20},{5,21},{6,22},{7,23},{8,24},{9,... | collective-permute-start | bytes 393224 | tf_op jit(solution)/shard_map/ppermute | solution.py:369
  78.8 0.1 shard_map.63.weights
  78.9 0.0 copy-start.3
  78.9 2.4 %collective-permute-done.16.second_context = bf16[64,1024]{1,0:T(8,128)(2,1)S(1)} collective-permute-done((bf16[64,1024]{1,0:T(8,128)(2,1)S(1)}, bf16[64,1024]{1,0:T(8,128)(2,1)S(1)}, u32[]{:S(2)}, u32[]{:S(2)}) %collective-permute-start.16) | collective-permute-done | bytes 131104 | tf_op jit(solution)/shard_map/ppermute | solution.py:369
  81.3 0.7 collective-permute-start.17
  82.0 0.0 collective-permute-done.17.other.sibling
  82.0 0.7 collective-permute-start.18
  82.7 1.3 %collective-permute-start.19 = (bf16[512,128]{1,0:T(8,128)(2,1)S(1)}, bf16[512,128]{1,0:T(8,128)(2,1)S(1)}, u32[]{:S(2)}, u32[]{:S(2)}) collective-permute-start(bf16[512,128]{1,0:T(8,128)(2,1)S(1)} %get-tuple-element.41), channel_id=1, source_target_pairs={{16,0},{17,1},{18,2},{19,3},{20,4},{21,5},{22,6},{23,7},{24,8},{25... | collective-permute-start | bytes 393224 | tf_op jit(solution)/shard_map/ppermute | solution.py:366
  84.0 1.3 %collective-permute-start.20 = (bf16[512,128]{1,0:T(8,128)(2,1)S(1)}, bf16[512,128]{1,0:T(8,128)(2,1)S(1)}, u32[]{:S(2)}, u32[]{:S(2)}) collective-permute-start(bf16[512,128]{1,0:T(8,128)(2,1)S(1)} %get-tuple-element.42), channel_id=1, source_target_pairs={{16,2},{17,3},{18,0},{19,1},{20,6},{21,7},{22,4},{23,5},{24,10},{2... | collective-permute-start | bytes 393224 | tf_op jit(solution)/shard_map/ppermute | solution.py:483
  85.3 0.0 collective-permute-done.18.across
  85.3 12.8 %collective-permute-done.19.direct = bf16[512,128]{1,0:T(8,128)(2,1)S(1)} collective-permute-done((bf16[512,128]{1,0:T(8,128)(2,1)S(1)}, bf16[512,128]{1,0:T(8,128)(2,1)S(1)}, u32[]{:S(2)}, u32[]{:S(2)}) %collective-permute-start.19) | collective-permute-done | bytes 131104 | tf_op jit(solution)/shard_map/ppermute | solution.py:366
  98.1 1.7 %collective-permute-done.20.diagonal = bf16[512,128]{1,0:T(8,128)(2,1)S(1)} collective-permute-done((bf16[512,128]{1,0:T(8,128)(2,1)S(1)}, bf16[512,128]{1,0:T(8,128)(2,1)S(1)}, u32[]{:S(2)}, u32[]{:S(2)}) %collective-permute-start.20) | collective-permute-done | bytes 131104 | tf_op jit(solution)/shard_map/ppermute | solution.py:483
  99.9 0.0 copy-done.3
  99.9 0.8 shard_map.67
  (7 shorter events, 0.1 us)
Async XLA Ops:
  0.0 11.0 %collective-permute-start.1 = (bf16[128,1024]{1,0:T(8,128)(2,1)}, bf16[128,1024]{1,0:T(8,128)(2,1)S(1)}, u32[]{:S(2)}, u32[]{:S(2)}) collective-permute-start(bf16[128,1024]{1,0:T(8,128)(2,1)} %bitcast.8), channel_id=1, source_target_pairs={{16,18},{17,19},{18,16},{19,17},{20,22},{21,23},{22,20},{23,21},{2... | collective-permute-start | bytes 786440 | tf_op jit(solution)/shard_map/ppermute | solution.py:360
  1.8 17.5 %collective-permute-start.5 = (bf16[256,1024]{1,0:T(8,128)(2,1)S(1)}, bf16[256,1024]{1,0:T(8,128)(2,1)S(1)}, u32[]{:S(2)}, u32[]{:S(2)}) collective-permute-start(bf16[256,1024]{1,0:T(8,128)(2,1)S(1)} %slice_bitcast_fusion.x0), channel_id=1, source_target_pairs={{0,2},{1,3},{2,0},{3,1},{4,6},{5,7},{6,4},{7,5},{8,10},{9,11},{10,... | collective-permute-start | bytes 1572872 | tf_op jit(solution)/shard_map/ppermute | solution.py:360
  6.6 16.4 %collective-permute-start.4 = (bf16[512,1024]{1,0:T(8,128)(2,1)}, bf16[512,1024]{1,0:T(8,128)(2,1)S(1)}, u32[]{:S(2)}, u32[]{:S(2)}) collective-permute-start(bf16[512,1024]{1,0:T(8,128)(2,1)} %bitcast.5), channel_id=1, source_target_pairs={{0,1},{1,0},{2,3},{3,2},{4,5},{5,4},{6,7},{7,6},{8,9},{9,8},{10,11... | collective-permute-start | bytes 3145736 | tf_op jit(solution)/shard_map/ppermute | solution.py:360
  8.6 6.2 %collective-permute-start = (bf16[128,1024]{1,0:T(8,128)(2,1)}, bf16[128,1024]{1,0:T(8,128)(2,1)S(1)}, u32[]{:S(2)}, u32[]{:S(2)}) collective-permute-start(bf16[128,1024]{1,0:T(8,128)(2,1)} %bitcast.9), channel_id=1, source_target_pairs={{16,17},{17,16},{18,19},{19,18},{20,21},{21,20},{22,23},{23,22},{2... | collective-permute-start | bytes 786440 | tf_op jit(solution)/shard_map/ppermute | solution.py:360
  9.3 1.0 copy-start.1
  10.2 0.7 copy-start.4
  11.0 3.8 %collective-permute-start.2 = (bf16[128,1024]{1,0:T(8,128)(2,1)S(1)}, bf16[128,1024]{1,0:T(8,128)(2,1)S(1)}, u32[]{:S(2)}, u32[]{:S(2)}) collective-permute-start(bf16[128,1024]{1,0:T(8,128)(2,1)S(1)} %collective-permute-done.1.x2), channel_id=1, source_target_pairs={{16,17},{17,16},{18,19},{19,18},{20,21},{21,20},{22,23},{23,22},{2... | collective-permute-start | bytes 786440 | tf_op jit(solution)/shard_map/ppermute | solution.py:360
  12.8 19.8 %collective-permute-start.10 = (bf16[320,1024]{1,0:T(8,128)(2,1)S(1)}, bf16[320,1024]{1,0:T(8,128)(2,1)S(1)}, u32[]{:S(2)}, u32[]{:S(2)}) collective-permute-start(bf16[320,1024]{1,0:T(8,128)(2,1)S(1)} %slice.16), channel_id=1, source_target_pairs={{0,2},{1,3},{2,0},{3,1},{4,6},{5,7},{6,4},{7,5},{8,10},{9,11},{10,... | collective-permute-start | bytes 1966088 | tf_op jit(solution)/shard_map/ppermute | solution.py:360
  14.8 3.5 %copy-start.2 = (bf16[128,512]{1,0:T(8,128)(2,1)}, bf16[128,512]{1,0:T(8,128)(2,1)S(1)}, u32[]{:S(2)}) copy-start(bf16[128,512]{1,0:T(8,128)(2,1)S(1)} %get-tuple-element.40.residual1) | copy-start | bytes 393220
  18.4 22.2 %copy-start = (bf16[2,256,1024]{2,1,0:T(8,128)(2,1)S(1)}, bf16[2,256,1024]{2,1,0:T(8,128)(2,1)}, u32[]{:S(2)}) copy-start(bf16[2,256,1024]{2,1,0:T(8,128)(2,1)} %param.5) | copy-start | bytes 3145732
  19.2 3.8 %collective-permute-start.6 = (bf16[256,1024]{1,0:T(8,128)(2,1)S(1)}, bf16[256,1024]{1,0:T(8,128)(2,1)S(1)}, u32[]{:S(2)}, u32[]{:S(2)}) collective-permute-start(bf16[256,1024]{1,0:T(8,128)(2,1)S(1)} %collective-permute-done.5.x2), channel_id=1, source_target_pairs={{0,1},{1,0},{2,3},{3,2},{4,5},{5,4},{6,7},{7,6},{8,9},{9,8},{10,11... | collective-permute-start | bytes 1572872 | tf_op jit(solution)/shard_map/ppermute | solution.py:360
  21.2 11.2 %collective-permute-start.3 = (bf16[128,1024]{1,0:T(8,128)(2,1)S(1)}, bf16[128,1024]{1,0:T(8,128)(2,1)S(1)}, u32[]{:S(2)}, u32[]{:S(2)}) collective-permute-start(bf16[128,1024]{1,0:T(8,128)(2,1)S(1)} %get-tuple-element.27.before), channel_id=1, source_target_pairs={{16,0},{17,1},{18,2},{19,3},{20,4},{21,5},{22,6},{23,7},{24,8},{25... | collective-permute-start | bytes 786440 | tf_op jit(solution)/shard_map/ppermute | solution.py:366
  30.1 24.6 %collective-permute-start.12 = (bf16[2,256,1024]{2,1,0:T(8,128)(2,1)}, bf16[2,256,1024]{2,1,0:T(8,128)(2,1)}, u32[]{:S(2)}, u32[]{:S(2)}) collective-permute-start(bf16[2,256,1024]{2,1,0:T(8,128)(2,1)} %shard_map.58), channel_id=1, source_target_pairs={{0,16},{1,17},{2,18},{3,19},{4,20},{5,21},{6,22},{7,23},{8,24},{9,... | collective-permute-start | bytes 3145736 | tf_op jit(solution)/shard_map/ppermute | solution.py:369
  32.6 7.9 %collective-permute-start.11 = (bf16[256,1024]{1,0:T(8,128)(2,1)S(1)}, bf16[256,1024]{1,0:T(8,128)(2,1)S(1)}, u32[]{:S(2)}, u32[]{:S(2)}) collective-permute-start(bf16[256,1024]{1,0:T(8,128)(2,1)S(1)} %slice.15.x2), channel_id=1, source_target_pairs={{0,1},{1,0},{2,3},{3,2},{4,5},{5,4},{6,7},{7,6},{8,9},{9,8},{10,11... | collective-permute-start | bytes 1572872 | tf_op jit(solution)/shard_map/ppermute | solution.py:360
  34.6 20.2 %copy-start.5 = (s32[2]{0:T(128)S(1)}, s32[2]{0:T(128)}, u32[]{:S(2)}) copy-start(s32[2]{0:T(128)} %lengths.1) | copy-start | bytes 28
  34.6 13.6 %collective-permute-start.7 = (bf16[64,1024]{1,0:T(8,128)(2,1)S(1)}, bf16[64,1024]{1,0:T(8,128)(2,1)S(1)}, u32[]{:S(2)}, u32[]{:S(2)}) collective-permute-start(bf16[64,1024]{1,0:T(8,128)(2,1)S(1)} %slice_select_fusion.refs_0_), channel_id=1, source_target_pairs={{0,4},{4,8},{8,12},{12,0},{1,5},{5,9},{9,13},{13,1},{2,6},{6,10},{... | collective-permute-start | bytes 393224 | tf_op jit(solution)/shard_map/ppermute | solution.py:363
  36.6 11.8 %collective-permute-start.8 = (bf16[64,1024]{1,0:T(8,128)(2,1)S(1)}, bf16[64,1024]{1,0:T(8,128)(2,1)S(1)}, u32[]{:S(2)}, u32[]{:S(2)}) collective-permute-start(bf16[64,1024]{1,0:T(8,128)(2,1)S(1)} %slice_select_fusion.refs_0_), channel_id=1, source_target_pairs={{0,8},{4,12},{8,0},{12,4},{1,9},{5,13},{9,1},{13,5},{2,10},{6,14},... | collective-permute-start | bytes 393224 | tf_op jit(solution)/shard_map/ppermute | solution.py:363
  39.2 9.2 %collective-permute-start.9 = (bf16[64,1024]{1,0:T(8,128)(2,1)S(1)}, bf16[64,1024]{1,0:T(8,128)(2,1)S(1)}, u32[]{:S(2)}, u32[]{:S(2)}) collective-permute-start(bf16[64,1024]{1,0:T(8,128)(2,1)S(1)} %slice_select_fusion.refs_0_), channel_id=1, source_target_pairs={{0,12},{4,0},{8,4},{12,8},{1,13},{5,1},{9,5},{13,9},{2,14},{6,2},{... | collective-permute-start | bytes 393224 | tf_op jit(solution)/shard_map/ppermute | solution.py:363
  58.1 8.4 %collective-permute-start.13 = (bf16[64,1152]{1,0:T(8,128)(2,1)S(1)}, bf16[64,1152]{1,0:T(8,128)(2,1)S(1)}, u32[]{:S(2)}, u32[]{:S(2)}) collective-permute-start(bf16[64,1152]{1,0:T(8,128)(2,1)S(1)} %get-tuple-element.35), channel_id=1, source_target_pairs={{0,12},{4,0},{8,4},{12,8},{1,13},{5,1},{9,5},{13,9},{2,14},{6,2},{... | collective-permute-start | bytes 442376 | tf_op jit(solution)/shard_map/ppermute | solution.py:363
  62.2 12.3 %collective-permute-start.14 = (bf16[64,1152]{1,0:T(8,128)(2,1)S(1)}, bf16[64,1152]{1,0:T(8,128)(2,1)S(1)}, u32[]{:S(2)}, u32[]{:S(2)}) collective-permute-start(bf16[64,1152]{1,0:T(8,128)(2,1)S(1)} %get-tuple-element.36), channel_id=1, source_target_pairs={{0,8},{4,12},{8,0},{12,4},{1,9},{5,13},{9,1},{13,5},{2,10},{6,14},... | collective-permute-start | bytes 442376 | tf_op jit(solution)/shard_map/ppermute | solution.py:363
  62.2 12.3 %collective-permute-start.15 = (bf16[64,1152]{1,0:T(8,128)(2,1)S(1)}, bf16[64,1152]{1,0:T(8,128)(2,1)S(1)}, u32[]{:S(2)}, u32[]{:S(2)}) collective-permute-start(bf16[64,1152]{1,0:T(8,128)(2,1)S(1)} %get-tuple-element.37), channel_id=1, source_target_pairs={{0,4},{4,8},{8,12},{12,0},{1,5},{5,9},{9,13},{13,1},{2,6},{6,10},{... | collective-permute-start | bytes 442376 | tf_op jit(solution)/shard_map/ppermute | solution.py:363
  75.3 6.0 %collective-permute-start.16 = (bf16[64,1024]{1,0:T(8,128)(2,1)S(1)}, bf16[64,1024]{1,0:T(8,128)(2,1)S(1)}, u32[]{:S(2)}, u32[]{:S(2)}) collective-permute-start(bf16[64,1024]{1,0:T(8,128)(2,1)S(1)} %shard_map.61), channel_id=1, source_target_pairs={{0,16},{1,17},{2,18},{3,19},{4,20},{5,21},{6,22},{7,23},{8,24},{9,... | collective-permute-start | bytes 393224 | tf_op jit(solution)/shard_map/ppermute | solution.py:369
  78.9 21.0 %copy-start.3 = (bf16[128,512]{1,0:T(8,128)(2,1)S(1)}, bf16[128,512]{1,0:T(8,128)(2,1)}, u32[]{:S(2)}) copy-start(bf16[128,512]{1,0:T(8,128)(2,1)} %copy-done.2) | copy-start | bytes 393220
  81.3 0.7 collective-permute-start.17
  82.0 3.3 %collective-permute-start.18 = (bf16[512,128]{1,0:T(8,128)(2,1)S(1)}, bf16[512,128]{1,0:T(8,128)(2,1)S(1)}, u32[]{:S(2)}, u32[]{:S(2)}) collective-permute-start(bf16[512,128]{1,0:T(8,128)(2,1)S(1)} %get-tuple-element.39), channel_id=1, source_target_pairs={{16,18},{17,19},{18,16},{19,17},{20,22},{21,23},{22,20},{23,21},{2... | collective-permute-start | bytes 393224 | tf_op jit(solution)/shard_map/ppermute | solution.py:360
  82.7 15.4 %collective-permute-start.19 = (bf16[512,128]{1,0:T(8,128)(2,1)S(1)}, bf16[512,128]{1,0:T(8,128)(2,1)S(1)}, u32[]{:S(2)}, u32[]{:S(2)}) collective-permute-start(bf16[512,128]{1,0:T(8,128)(2,1)S(1)} %get-tuple-element.41), channel_id=1, source_target_pairs={{16,0},{17,1},{18,2},{19,3},{20,4},{21,5},{22,6},{23,7},{24,8},{25... | collective-permute-start | bytes 393224 | tf_op jit(solution)/shard_map/ppermute | solution.py:366
  84.0 15.9 %collective-permute-start.20 = (bf16[512,128]{1,0:T(8,128)(2,1)S(1)}, bf16[512,128]{1,0:T(8,128)(2,1)S(1)}, u32[]{:S(2)}, u32[]{:S(2)}) collective-permute-start(bf16[512,128]{1,0:T(8,128)(2,1)S(1)} %get-tuple-element.42), channel_id=1, source_target_pairs={{16,2},{17,3},{18,0},{19,1},{20,6},{21,7},{22,4},{23,5},{24,10},{2... | collective-permute-start | bytes 393224 | tf_op jit(solution)/shard_map/ppermute | solution.py:483

commit v5 on v4

--- a/solution.py
+++ b/solution.py
@@ -360,7 +360,7 @@
         return lax.ppermute(array, ("segment", "mp"), pairs)
 
     def along_seq(array, by):
-        return lax.ppermute(array, "seq", [(i, (i + by) % count) for i in range(count)])
+        return lax.ppermute(array, "seq", [(i, i ^ by) for i in range(count)])
 
     def to_encoder(array):
         return lax.ppermute(array, "segment", [(1, 0)])
@@ -444,7 +444,8 @@
         (lengths, *q_pieces, second_memory, first_memory),
         [SMEM] + [VMEM] * (count + 2),
     )
-    sources = [partial[0]] + [along_seq(partial[by], -by) for by in range(1, count)]
+    order = sorted(range(1, count), key=lambda by: by == 1)
+    sources = [partial[0]] + [along_seq(partial[by], by) for by in order]
     def combined(section, sources):
         return call(
             functools.partial(combine_kernel, section),

time: 101 us -> 100 us (0.990)
  starting transfers between devices: 36.6 us -> 34.8 us
    ppermute x6, starting transfers between devices: 11.1 us -> 9.25 us  [along_seq(): return lax.ppermute(array, 'seq', [(i, i ^ by) for i in range(count)])]
    ppermute x2, waiting for transfers between devices: 8.7 us -> 7.53 us  [to_decoder(): return lax.ppermute(array, 'segment', [(0, 1)])]
  transfers between devices with their start and end apart: 21 -> 21, of which waited for: 10 -> 10; matrix products, arithmetic and copies ran while one was open for 2% -> 2% of each run, Pallas kernels for 18% -> 19%
where the time goes in v5:
time: 100 us; the launch traced here: 98.8 us
  waiting for transfers between devices  36.1 us (36%)
  starting transfers between devices  34.8 us (35%)
  Pallas kernels  23.6 us (24%)
  local copies, waits for them, and re-layouts  3.93 us (4%)
    pallas_call x13, Pallas kernels, call(): pl.pallas_call(kernel, out_shape=out_shapes, in_specs=specs, out_specs=ou...  23.6 us
    ppermute x10, starting transfers between devices, in_section(): return lax.ppermute(array, ('segment', 'mp'), pairs)  15.9 us
    ppermute x2, waiting for transfers between devices, to_encoder(): return lax.ppermute(array, 'segment', [(1, 0)])  12.9 us
    ppermute x6, waiting for transfers between devices, along_seq(): return lax.ppermute(array, 'seq', [(i, i ^ by) for i in range(count)])  12.3 us
    ppermute x6, starting transfers between devices, along_seq(): return lax.ppermute(array, 'seq', [(i, i ^ by) for i in range(count)])  9.25 us
    ppermute x2, waiting for transfers between devices, to_decoder(): return lax.ppermute(array, 'segment', [(0, 1)])  7.53 us
    ppermute x2, starting transfers between devices, to_decoder(): return lax.ppermute(array, 'segment', [(0, 1)])  5.75 us
    ppermute x2, starting transfers between devices, to_encoder(): return lax.ppermute(array, 'segment', [(1, 0)])  2.58 us
  transfers between devices with their start and end apart: 21, of which 10 were waited for; matrix products, arithmetic and copies ran while one was open for 2% of the time, Pallas kernels for 19%

profile of v5, /device:TPU:0, one launch (start us, length us, event | category | flops | bytes accessed | tf_op | source)
XLA Modules:
  0.0 98.8 jit_solution(13420353969613405582)
XLA Ops:
  0.0 0.7 collective-permute-start.1
  0.7 1.1 %slice_bitcast_fusion.x0 = bf16[256,1024]{1,0:T(8,128)(2,1)S(1)} fusion(bf16[2,256,1024]{2,1,0:T(8,128)(2,1)} %param.5), kind=kLoop, calls=%fused_computation | loop fusion | bytes 1048576 | tf_op jit(solution)/shard_map/squeeze | solution.py:375
  1.8 4.9 %collective-permute-start.5 = (bf16[256,1024]{1,0:T(8,128)(2,1)S(1)}, bf16[256,1024]{1,0:T(8,128)(2,1)S(1)}, u32[]{:S(2)}, u32[]{:S(2)}) collective-permute-start(bf16[256,1024]{1,0:T(8,128)(2,1)S(1)} %slice_bitcast_fusion.x0), channel_id=1, source_target_pairs={{0,2},{1,3},{2,0},{3,1},{4,6},{5,7},{6,4},{7,5},{8,10},{9,11},{10,... | collective-permute-start | bytes 1572872 | tf_op jit(solution)/shard_map/ppermute | solution.py:360
  6.6 1.9 %collective-permute-start.4 = (bf16[512,1024]{1,0:T(8,128)(2,1)}, bf16[512,1024]{1,0:T(8,128)(2,1)S(1)}, u32[]{:S(2)}, u32[]{:S(2)}) collective-permute-start(bf16[512,1024]{1,0:T(8,128)(2,1)} %bitcast.5), channel_id=1, source_target_pairs={{0,1},{1,0},{2,3},{3,2},{4,5},{5,4},{6,7},{7,6},{8,9},{9,8},{10,11... | collective-permute-start | bytes 3145736 | tf_op jit(solution)/shard_map/ppermute | solution.py:360
  8.6 0.7 collective-permute-start
  9.3 0.0 copy-start.1
  9.3 0.9 copy-done.1
  10.2 0.0 copy-start.4
  10.2 0.7 copy-done.4
  11.0 0.0 collective-permute-done.1.x2
  11.0 0.7 collective-permute-start.2
  11.7 1.1 %slice.16 = bf16[320,1024]{1,0:T(8,128)(2,1)S(1)} slice(bf16[512,1024]{1,0:T(8,128)(2,1)} %bitcast.6), slice={[192:512], [0:1024]} | slice | bytes 1310720 | tf_op jit(solution)/shard_map/slice | solution.py:377
  12.8 1.9 %collective-permute-start.10 = (bf16[320,1024]{1,0:T(8,128)(2,1)S(1)}, bf16[320,1024]{1,0:T(8,128)(2,1)S(1)}, u32[]{:S(2)}, u32[]{:S(2)}) collective-permute-start(bf16[320,1024]{1,0:T(8,128)(2,1)S(1)} %slice.16), channel_id=1, source_target_pairs={{0,2},{1,3},{2,0},{3,1},{4,6},{5,7},{6,4},{7,5},{8,10},{9,11},{10,... | collective-permute-start | bytes 1966088 | tf_op jit(solution)/shard_map/ppermute | solution.py:360
  14.7 0.0 collective-permute-done.x1
  14.7 0.0 collective-permute-done.2.x3
  14.7 0.1 shard_map.56
  14.8 0.0 copy-start.2
  14.8 3.5 %shard_map.57.key_weights = bf16[4096,1024]{1,0:T(8,128)(2,1)S(1)} custom-call(bf16[1,2,4096,1024]{3,2,1,0:T(8,128)(2,1)} %weights.9, bf16[128,1024]{1,0:T(8,128)(2,1)S(1)} %get-tuple-element.27.before), custom_call_target="tpu_custom_call" | custom-call | flops 1 | bytes 1 | tf_op jit(solution)/shard_map/pallas_call | solution.py:332
  18.4 0.0 copy-done.2
  18.4 0.0 copy-start
  18.4 0.8 collective-permute-done.5.x2
  19.2 1.9 %collective-permute-start.6 = (bf16[256,1024]{1,0:T(8,128)(2,1)S(1)}, bf16[256,1024]{1,0:T(8,128)(2,1)S(1)}, u32[]{:S(2)}, u32[]{:S(2)}) collective-permute-start(bf16[256,1024]{1,0:T(8,128)(2,1)S(1)} %collective-permute-done.5.x2), channel_id=1, source_target_pairs={{0,1},{1,0},{2,3},{3,2},{4,5},{5,4},{6,7},{7,6},{8,9},{9,8},{10,11... | collective-permute-start | bytes 1572872 | tf_op jit(solution)/shard_map/ppermute | solution.py:360
  21.2 1.3 %collective-permute-start.3 = (bf16[128,1024]{1,0:T(8,128)(2,1)S(1)}, bf16[128,1024]{1,0:T(8,128)(2,1)S(1)}, u32[]{:S(2)}, u32[]{:S(2)}) collective-permute-start(bf16[128,1024]{1,0:T(8,128)(2,1)S(1)} %get-tuple-element.27.before), channel_id=1, source_target_pairs={{16,0},{17,1},{18,2},{19,3},{20,4},{21,5},{22,6},{23,7},{24,8},{25... | collective-permute-start | bytes 786440 | tf_op jit(solution)/shard_map/ppermute | solution.py:366
  22.5 0.6 collective-permute-done.6.x3
  23.0 0.0 collective-permute-done.4.x1
  23.0 7.1 %shard_map.58 = bf16[2,256,1024]{2,1,0:T(8,128)(2,1)} custom-call(bf16[256,1024]{1,0:T(8,128)(2,1)S(1)} %slice_bitcast_fusion.x0, bf16[512,1024]{1,0:T(8,128)(2,1)S(1)} %collective-permute-done.4.x1, bf16[256,1024]{1,0:T(8,128)(2,1)S(1)} %collective-permute-done.5.x2, bf16[256,1024]{1,0:T(8,128)(2,1)S(1)} %collective-permute-done.6.x3, ...), custom_call_target="tpu_custom_call" | custom-call | flops 1 | bytes 1 | tf_op jit(solution)/shard_map/pallas_call | solution.py:332
  30.1 2.3 %collective-permute-start.12 = (bf16[2,256,1024]{2,1,0:T(8,128)(2,1)}, bf16[2,256,1024]{2,1,0:T(8,128)(2,1)}, u32[]{:S(2)}, u32[]{:S(2)}) collective-permute-start(bf16[2,256,1024]{2,1,0:T(8,128)(2,1)} %shard_map.58), channel_id=1, source_target_pairs={{0,16},{1,17},{2,18},{3,19},{4,20},{5,21},{6,22},{7,23},{8,24},{9,... | collective-permute-start | bytes 3145736 | tf_op jit(solution)/shard_map/ppermute | solution.py:369
  32.4 0.0 collective-permute-done.3.residual0
  32.4 0.2 collective-permute-done.10
  32.6 1.9 %collective-permute-start.11 = (bf16[256,1024]{1,0:T(8,128)(2,1)S(1)}, bf16[256,1024]{1,0:T(8,128)(2,1)S(1)}, u32[]{:S(2)}, u32[]{:S(2)}) collective-permute-start(bf16[256,1024]{1,0:T(8,128)(2,1)S(1)} %slice.15.x2), channel_id=1, source_target_pairs={{0,1},{1,0},{2,3},{3,2},{4,5},{5,4},{6,7},{7,6},{8,9},{9,8},{10,11... | collective-permute-start | bytes 1572872 | tf_op jit(solution)/shard_map/ppermute | solution.py:360
  34.6 0.0 copy-start.5
  34.6 2.0 %collective-permute-start.7 = (bf16[64,1024]{1,0:T(8,128)(2,1)S(1)}, bf16[64,1024]{1,0:T(8,128)(2,1)S(1)}, u32[]{:S(2)}, u32[]{:S(2)}) collective-permute-start(bf16[64,1024]{1,0:T(8,128)(2,1)S(1)} %slice_select_fusion.refs_0_), channel_id=1, source_target_pairs={{0,4},{4,0},{8,12},{12,8},{1,5},{5,1},{9,13},{13,9},{2,6},{6,2},{1... | collective-permute-start | bytes 393224 | tf_op jit(solution)/shard_map/ppermute | solution.py:363
  36.6 2.6 %collective-permute-start.8 = (bf16[64,1024]{1,0:T(8,128)(2,1)S(1)}, bf16[64,1024]{1,0:T(8,128)(2,1)S(1)}, u32[]{:S(2)}, u32[]{:S(2)}) collective-permute-start(bf16[64,1024]{1,0:T(8,128)(2,1)S(1)} %slice_select_fusion.refs_0_), channel_id=1, source_target_pairs={{0,8},{4,12},{8,0},{12,4},{1,9},{5,13},{9,1},{13,5},{2,10},{6,14},... | collective-permute-start | bytes 393224 | tf_op jit(solution)/shard_map/ppermute | solution.py:363
  39.2 0.0 collective-permute-start.9
  39.2 0.0 collective-permute-done.11.x3
  39.2 0.0 copy-done
  39.2 7.8 %shard_map.59.refs_4_ = bf16[2,256,1024]{2,1,0:T(8,128)(2,1)S(1)} custom-call(bf16[512,1024]{1,0:T(8,128)(2,1)S(1)} %bitcast.7, bf16[512,1024]{1,0:T(8,128)(2,1)S(1)} %collective-permute-done.4.x1, bf16[256,1024]{1,0:T(8,128)(2,1)S(1)} %slice.15.x2, bf16[256,1024]{1,0:T(8,128)(2,1)S(1)} %collective-permute-done.11.x3, ...), custom_call_target="tpu_custom_call" | custom-call | flops 4800000000 | bytes 1 | tf_op jit(solution)/shard_map/pallas_call | solution.py:332
  47.0 0.0 collective-permute-done.7.refs_1_
  47.0 2.6 %collective-permute-done.8.refs_2_ = bf16[64,1024]{1,0:T(8,128)(2,1)S(1)} collective-permute-done((bf16[64,1024]{1,0:T(8,128)(2,1)S(1)}, bf16[64,1024]{1,0:T(8,128)(2,1)S(1)}, u32[]{:S(2)}, u32[]{:S(2)}) %collective-permute-start.8) | collective-permute-done | bytes 131104 | tf_op jit(solution)/shard_map/ppermute | solution.py:363
  49.6 0.0 collective-permute-done.9.refs_3_
  49.6 5.2 %collective-permute-done.12.refs_5_ = bf16[2,256,1024]{2,1,0:T(8,128)(2,1)} collective-permute-done((bf16[2,256,1024]{2,1,0:T(8,128)(2,1)}, bf16[2,256,1024]{2,1,0:T(8,128)(2,1)}, u32[]{:S(2)}, u32[]{:S(2)}) %collective-permute-start.12) | collective-permute-done | bytes 1048608 | tf_op jit(solution)/shard_map/ppermute | solution.py:369
  54.7 0.0 copy-done.5
  54.7 3.3 %shard_map.60 = (bf16[64,1152]{1,0:T(8,128)(2,1)S(1)}, bf16[64,1152]{1,0:T(8,128)(2,1)S(1)}, bf16[64,1152]{1,0:T(8,128)(2,1)S(1)}, bf16[64,1152]{1,0:T(8,128)(2,1)S(1)}) custom-call(s32[2]{0:T(128)S(1)} %copy-done.5, bf16[64,1024]{1,0:T(8,128)(2,1)S(1)} %slice_select_fusion.refs_0_, bf16[64,1024]{1,0:T(8,128)(2,1)S(1)} %collective-permute-done.7.refs_1_, ...), custom_call_target="tpu_custom_call" | custom-call | flops 1 | bytes 1 | tf_op jit(solution)/shard_map/pallas_call | solution.py:332
  58.1 3.1 %collective-permute-start.13 = (bf16[64,1152]{1,0:T(8,128)(2,1)S(1)}, bf16[64,1152]{1,0:T(8,128)(2,1)S(1)}, u32[]{:S(2)}, u32[]{:S(2)}) collective-permute-start(bf16[64,1152]{1,0:T(8,128)(2,1)S(1)} %get-tuple-element.35), channel_id=1, source_target_pairs={{0,8},{4,12},{8,0},{12,4},{1,9},{5,13},{9,1},{13,5},{2,10},{6,14},... | collective-permute-start | bytes 442376 | tf_op jit(solution)/shard_map/ppermute | solution.py:363
  61.2 1.3 %collective-permute-start.14 = (bf16[64,1152]{1,0:T(8,128)(2,1)S(1)}, bf16[64,1152]{1,0:T(8,128)(2,1)S(1)}, u32[]{:S(2)}, u32[]{:S(2)}) collective-permute-start(bf16[64,1152]{1,0:T(8,128)(2,1)S(1)} %get-tuple-element.36), channel_id=1, source_target_pairs={{0,12},{4,8},{8,4},{12,0},{1,13},{5,9},{9,5},{13,1},{2,14},{6,10},... | collective-permute-start | bytes 442376 | tf_op jit(solution)/shard_map/ppermute | solution.py:363
  62.5 0.2 collective-permute-start.15
  62.7 9.5 %collective-permute-done.13.refs_1_ = bf16[64,1152]{1,0:T(8,128)(2,1)S(1)} collective-permute-done((bf16[64,1152]{1,0:T(8,128)(2,1)S(1)}, bf16[64,1152]{1,0:T(8,128)(2,1)S(1)}, u32[]{:S(2)}, u32[]{:S(2)}) %collective-permute-start.13) | collective-permute-done | bytes 147488 | tf_op jit(solution)/shard_map/ppermute | solution.py:363
  72.2 0.0 collective-permute-done.14.refs_2_
  72.2 0.3 collective-permute-done.15.refs_3_
  72.5 0.8 shard_map.61
  73.3 3.5 %collective-permute-start.16 = (bf16[64,1024]{1,0:T(8,128)(2,1)S(1)}, bf16[64,1024]{1,0:T(8,128)(2,1)S(1)}, u32[]{:S(2)}, u32[]{:S(2)}) collective-permute-start(bf16[64,1024]{1,0:T(8,128)(2,1)S(1)} %shard_map.61), channel_id=1, source_target_pairs={{0,16},{1,17},{2,18},{3,19},{4,20},{5,21},{6,22},{7,23},{8,24},{9,... | collective-permute-start | bytes 393224 | tf_op jit(solution)/shard_map/ppermute | solution.py:369
  76.9 0.1 shard_map.63.weights
  77.0 0.0 copy-start.3
  77.0 2.4 %collective-permute-done.16.second_context = bf16[64,1024]{1,0:T(8,128)(2,1)S(1)} collective-permute-done((bf16[64,1024]{1,0:T(8,128)(2,1)S(1)}, bf16[64,1024]{1,0:T(8,128)(2,1)S(1)}, u32[]{:S(2)}, u32[]{:S(2)}) %collective-permute-start.16) | collective-permute-done | bytes 131104 | tf_op jit(solution)/shard_map/ppermute | solution.py:369
  79.3 0.7 collective-permute-start.17
  80.0 0.0 collective-permute-done.17.other.sibling
  80.1 0.7 collective-permute-start.18
  80.8 1.3 %collective-permute-start.19 = (bf16[512,128]{1,0:T(8,128)(2,1)S(1)}, bf16[512,128]{1,0:T(8,128)(2,1)S(1)}, u32[]{:S(2)}, u32[]{:S(2)}) collective-permute-start(bf16[512,128]{1,0:T(8,128)(2,1)S(1)} %get-tuple-element.41), channel_id=1, source_target_pairs={{16,0},{17,1},{18,2},{19,3},{20,4},{21,5},{22,6},{23,7},{24,8},{25... | collective-permute-start | bytes 393224 | tf_op jit(solution)/shard_map/ppermute | solution.py:366
  82.1 1.3 %collective-permute-start.20 = (bf16[512,128]{1,0:T(8,128)(2,1)S(1)}, bf16[512,128]{1,0:T(8,128)(2,1)S(1)}, u32[]{:S(2)}, u32[]{:S(2)}) collective-permute-start(bf16[512,128]{1,0:T(8,128)(2,1)S(1)} %get-tuple-element.42), channel_id=1, source_target_pairs={{16,2},{17,3},{18,0},{19,1},{20,6},{21,7},{22,4},{23,5},{24,10},{2... | collective-permute-start | bytes 393224 | tf_op jit(solution)/shard_map/ppermute | solution.py:484
  83.4 0.0 collective-permute-done.18.across
  83.4 12.9 %collective-permute-done.19.direct = bf16[512,128]{1,0:T(8,128)(2,1)S(1)} collective-permute-done((bf16[512,128]{1,0:T(8,128)(2,1)S(1)}, bf16[512,128]{1,0:T(8,128)(2,1)S(1)}, u32[]{:S(2)}, u32[]{:S(2)}) %collective-permute-start.19) | collective-permute-done | bytes 131104 | tf_op jit(solution)/shard_map/ppermute | solution.py:366
  96.3 1.7 %collective-permute-done.20.diagonal = bf16[512,128]{1,0:T(8,128)(2,1)S(1)} collective-permute-done((bf16[512,128]{1,0:T(8,128)(2,1)S(1)}, bf16[512,128]{1,0:T(8,128)(2,1)S(1)}, u32[]{:S(2)}, u32[]{:S(2)}) %collective-permute-start.20) | collective-permute-done | bytes 131104 | tf_op jit(solution)/shard_map/ppermute | solution.py:484
  98.0 0.0 copy-done.3
  98.0 0.8 shard_map.67
  (7 shorter events, 0.1 us)
Async XLA Ops:
  0.0 11.0 %collective-permute-start.1 = (bf16[128,1024]{1,0:T(8,128)(2,1)}, bf16[128,1024]{1,0:T(8,128)(2,1)S(1)}, u32[]{:S(2)}, u32[]{:S(2)}) collective-permute-start(bf16[128,1024]{1,0:T(8,128)(2,1)} %bitcast.8), channel_id=1, source_target_pairs={{16,18},{17,19},{18,16},{19,17},{20,22},{21,23},{22,20},{23,21},{2... | collective-permute-start | bytes 786440 | tf_op jit(solution)/shard_map/ppermute | solution.py:360
  1.8 17.5 %collective-permute-start.5 = (bf16[256,1024]{1,0:T(8,128)(2,1)S(1)}, bf16[256,1024]{1,0:T(8,128)(2,1)S(1)}, u32[]{:S(2)}, u32[]{:S(2)}) collective-permute-start(bf16[256,1024]{1,0:T(8,128)(2,1)S(1)} %slice_bitcast_fusion.x0), channel_id=1, source_target_pairs={{0,2},{1,3},{2,0},{3,1},{4,6},{5,7},{6,4},{7,5},{8,10},{9,11},{10,... | collective-permute-start | bytes 1572872 | tf_op jit(solution)/shard_map/ppermute | solution.py:360
  6.6 16.4 %collective-permute-start.4 = (bf16[512,1024]{1,0:T(8,128)(2,1)}, bf16[512,1024]{1,0:T(8,128)(2,1)S(1)}, u32[]{:S(2)}, u32[]{:S(2)}) collective-permute-start(bf16[512,1024]{1,0:T(8,128)(2,1)} %bitcast.5), channel_id=1, source_target_pairs={{0,1},{1,0},{2,3},{3,2},{4,5},{5,4},{6,7},{7,6},{8,9},{9,8},{10,11... | collective-permute-start | bytes 3145736 | tf_op jit(solution)/shard_map/ppermute | solution.py:360
  8.6 6.2 %collective-permute-start = (bf16[128,1024]{1,0:T(8,128)(2,1)}, bf16[128,1024]{1,0:T(8,128)(2,1)S(1)}, u32[]{:S(2)}, u32[]{:S(2)}) collective-permute-start(bf16[128,1024]{1,0:T(8,128)(2,1)} %bitcast.9), channel_id=1, source_target_pairs={{16,17},{17,16},{18,19},{19,18},{20,21},{21,20},{22,23},{23,22},{2... | collective-permute-start | bytes 786440 | tf_op jit(solution)/shard_map/ppermute | solution.py:360
  9.3 1.0 copy-start.1
  10.2 0.7 copy-start.4
  11.0 3.8 %collective-permute-start.2 = (bf16[128,1024]{1,0:T(8,128)(2,1)S(1)}, bf16[128,1024]{1,0:T(8,128)(2,1)S(1)}, u32[]{:S(2)}, u32[]{:S(2)}) collective-permute-start(bf16[128,1024]{1,0:T(8,128)(2,1)S(1)} %collective-permute-done.1.x2), channel_id=1, source_target_pairs={{16,17},{17,16},{18,19},{19,18},{20,21},{21,20},{22,23},{23,22},{2... | collective-permute-start | bytes 786440 | tf_op jit(solution)/shard_map/ppermute | solution.py:360
  12.8 19.8 %collective-permute-start.10 = (bf16[320,1024]{1,0:T(8,128)(2,1)S(1)}, bf16[320,1024]{1,0:T(8,128)(2,1)S(1)}, u32[]{:S(2)}, u32[]{:S(2)}) collective-permute-start(bf16[320,1024]{1,0:T(8,128)(2,1)S(1)} %slice.16), channel_id=1, source_target_pairs={{0,2},{1,3},{2,0},{3,1},{4,6},{5,7},{6,4},{7,5},{8,10},{9,11},{10,... | collective-permute-start | bytes 1966088 | tf_op jit(solution)/shard_map/ppermute | solution.py:360
  14.8 3.5 %copy-start.2 = (bf16[128,512]{1,0:T(8,128)(2,1)}, bf16[128,512]{1,0:T(8,128)(2,1)S(1)}, u32[]{:S(2)}) copy-start(bf16[128,512]{1,0:T(8,128)(2,1)S(1)} %get-tuple-element.40.residual1) | copy-start | bytes 393220
  18.4 20.8 %copy-start = (bf16[2,256,1024]{2,1,0:T(8,128)(2,1)S(1)}, bf16[2,256,1024]{2,1,0:T(8,128)(2,1)}, u32[]{:S(2)}) copy-start(bf16[2,256,1024]{2,1,0:T(8,128)(2,1)} %param.5) | copy-start | bytes 3145732
  19.2 3.8 %collective-permute-start.6 = (bf16[256,1024]{1,0:T(8,128)(2,1)S(1)}, bf16[256,1024]{1,0:T(8,128)(2,1)S(1)}, u32[]{:S(2)}, u32[]{:S(2)}) collective-permute-start(bf16[256,1024]{1,0:T(8,128)(2,1)S(1)} %collective-permute-done.5.x2), channel_id=1, source_target_pairs={{0,1},{1,0},{2,3},{3,2},{4,5},{5,4},{6,7},{7,6},{8,9},{9,8},{10,11... | collective-permute-start | bytes 1572872 | tf_op jit(solution)/shard_map/ppermute | solution.py:360
  21.2 11.2 %collective-permute-start.3 = (bf16[128,1024]{1,0:T(8,128)(2,1)S(1)}, bf16[128,1024]{1,0:T(8,128)(2,1)S(1)}, u32[]{:S(2)}, u32[]{:S(2)}) collective-permute-start(bf16[128,1024]{1,0:T(8,128)(2,1)S(1)} %get-tuple-element.27.before), channel_id=1, source_target_pairs={{16,0},{17,1},{18,2},{19,3},{20,4},{21,5},{22,6},{23,7},{24,8},{25... | collective-permute-start | bytes 786440 | tf_op jit(solution)/shard_map/ppermute | solution.py:366
  30.1 24.6 %collective-permute-start.12 = (bf16[2,256,1024]{2,1,0:T(8,128)(2,1)}, bf16[2,256,1024]{2,1,0:T(8,128)(2,1)}, u32[]{:S(2)}, u32[]{:S(2)}) collective-permute-start(bf16[2,256,1024]{2,1,0:T(8,128)(2,1)} %shard_map.58), channel_id=1, source_target_pairs={{0,16},{1,17},{2,18},{3,19},{4,20},{5,21},{6,22},{7,23},{8,24},{9,... | collective-permute-start | bytes 3145736 | tf_op jit(solution)/shard_map/ppermute | solution.py:369
  32.6 6.6 %collective-permute-start.11 = (bf16[256,1024]{1,0:T(8,128)(2,1)S(1)}, bf16[256,1024]{1,0:T(8,128)(2,1)S(1)}, u32[]{:S(2)}, u32[]{:S(2)}) collective-permute-start(bf16[256,1024]{1,0:T(8,128)(2,1)S(1)} %slice.15.x2), channel_id=1, source_target_pairs={{0,1},{1,0},{2,3},{3,2},{4,5},{5,4},{6,7},{7,6},{8,9},{9,8},{10,11... | collective-permute-start | bytes 1572872 | tf_op jit(solution)/shard_map/ppermute | solution.py:360
  34.6 20.2 %copy-start.5 = (s32[2]{0:T(128)S(1)}, s32[2]{0:T(128)}, u32[]{:S(2)}) copy-start(s32[2]{0:T(128)} %lengths.1) | copy-start | bytes 28
  34.6 12.4 %collective-permute-start.7 = (bf16[64,1024]{1,0:T(8,128)(2,1)S(1)}, bf16[64,1024]{1,0:T(8,128)(2,1)S(1)}, u32[]{:S(2)}, u32[]{:S(2)}) collective-permute-start(bf16[64,1024]{1,0:T(8,128)(2,1)S(1)} %slice_select_fusion.refs_0_), channel_id=1, source_target_pairs={{0,4},{4,0},{8,12},{12,8},{1,5},{5,1},{9,13},{13,9},{2,6},{6,2},{1... | collective-permute-start | bytes 393224 | tf_op jit(solution)/shard_map/ppermute | solution.py:363
  36.6 12.9 %collective-permute-start.8 = (bf16[64,1024]{1,0:T(8,128)(2,1)S(1)}, bf16[64,1024]{1,0:T(8,128)(2,1)S(1)}, u32[]{:S(2)}, u32[]{:S(2)}) collective-permute-start(bf16[64,1024]{1,0:T(8,128)(2,1)S(1)} %slice_select_fusion.refs_0_), channel_id=1, source_target_pairs={{0,8},{4,12},{8,0},{12,4},{1,9},{5,13},{9,1},{13,5},{2,10},{6,14},... | collective-permute-start | bytes 393224 | tf_op jit(solution)/shard_map/ppermute | solution.py:363
  39.2 10.4 %collective-permute-start.9 = (bf16[64,1024]{1,0:T(8,128)(2,1)S(1)}, bf16[64,1024]{1,0:T(8,128)(2,1)S(1)}, u32[]{:S(2)}, u32[]{:S(2)}) collective-permute-start(bf16[64,1024]{1,0:T(8,128)(2,1)S(1)} %slice_select_fusion.refs_0_), channel_id=1, source_target_pairs={{0,12},{4,8},{8,4},{12,0},{1,13},{5,9},{9,5},{13,1},{2,14},{6,10},... | collective-permute-start | bytes 393224 | tf_op jit(solution)/shard_map/ppermute | solution.py:363
  58.1 14.1 %collective-permute-start.13 = (bf16[64,1152]{1,0:T(8,128)(2,1)S(1)}, bf16[64,1152]{1,0:T(8,128)(2,1)S(1)}, u32[]{:S(2)}, u32[]{:S(2)}) collective-permute-start(bf16[64,1152]{1,0:T(8,128)(2,1)S(1)} %get-tuple-element.35), channel_id=1, source_target_pairs={{0,8},{4,12},{8,0},{12,4},{1,9},{5,13},{9,1},{13,5},{2,10},{6,14},... | collective-permute-start | bytes 442376 | tf_op jit(solution)/shard_map/ppermute | solution.py:363
  61.2 11.0 %collective-permute-start.14 = (bf16[64,1152]{1,0:T(8,128)(2,1)S(1)}, bf16[64,1152]{1,0:T(8,128)(2,1)S(1)}, u32[]{:S(2)}, u32[]{:S(2)}) collective-permute-start(bf16[64,1152]{1,0:T(8,128)(2,1)S(1)} %get-tuple-element.36), channel_id=1, source_target_pairs={{0,12},{4,8},{8,4},{12,0},{1,13},{5,9},{9,5},{13,1},{2,14},{6,10},... | collective-permute-start | bytes 442376 | tf_op jit(solution)/shard_map/ppermute | solution.py:363
  62.5 10.0 %collective-permute-start.15 = (bf16[64,1152]{1,0:T(8,128)(2,1)S(1)}, bf16[64,1152]{1,0:T(8,128)(2,1)S(1)}, u32[]{:S(2)}, u32[]{:S(2)}) collective-permute-start(bf16[64,1152]{1,0:T(8,128)(2,1)S(1)} %get-tuple-element.37), channel_id=1, source_target_pairs={{0,4},{4,0},{8,12},{12,8},{1,5},{5,1},{9,13},{13,9},{2,6},{6,2},{1... | collective-permute-start | bytes 442376 | tf_op jit(solution)/shard_map/ppermute | solution.py:363
  73.3 6.0 %collective-permute-start.16 = (bf16[64,1024]{1,0:T(8,128)(2,1)S(1)}, bf16[64,1024]{1,0:T(8,128)(2,1)S(1)}, u32[]{:S(2)}, u32[]{:S(2)}) collective-permute-start(bf16[64,1024]{1,0:T(8,128)(2,1)S(1)} %shard_map.61), channel_id=1, source_target_pairs={{0,16},{1,17},{2,18},{3,19},{4,20},{5,21},{6,22},{7,23},{8,24},{9,... | collective-permute-start | bytes 393224 | tf_op jit(solution)/shard_map/ppermute | solution.py:369
  77.0 21.1 %copy-start.3 = (bf16[128,512]{1,0:T(8,128)(2,1)S(1)}, bf16[128,512]{1,0:T(8,128)(2,1)}, u32[]{:S(2)}) copy-start(bf16[128,512]{1,0:T(8,128)(2,1)} %copy-done.2) | copy-start | bytes 393220
  79.3 0.7 collective-permute-start.17
  80.1 3.3 %collective-permute-start.18 = (bf16[512,128]{1,0:T(8,128)(2,1)S(1)}, bf16[512,128]{1,0:T(8,128)(2,1)S(1)}, u32[]{:S(2)}, u32[]{:S(2)}) collective-permute-start(bf16[512,128]{1,0:T(8,128)(2,1)S(1)} %get-tuple-element.39), channel_id=1, source_target_pairs={{16,18},{17,19},{18,16},{19,17},{20,22},{21,23},{22,20},{23,21},{2... | collective-permute-start | bytes 393224 | tf_op jit(solution)/shard_map/ppermute | solution.py:360
  80.8 15.5 %collective-permute-start.19 = (bf16[512,128]{1,0:T(8,128)(2,1)S(1)}, bf16[512,128]{1,0:T(8,128)(2,1)S(1)}, u32[]{:S(2)}, u32[]{:S(2)}) collective-permute-start(bf16[512,128]{1,0:T(8,128)(2,1)S(1)} %get-tuple-element.41), channel_id=1, source_target_pairs={{16,0},{17,1},{18,2},{19,3},{20,4},{21,5},{22,6},{23,7},{24,8},{25... | collective-permute-start | bytes 393224 | tf_op jit(solution)/shard_map/ppermute | solution.py:366
  82.1 16.0 %collective-permute-start.20 = (bf16[512,128]{1,0:T(8,128)(2,1)S(1)}, bf16[512,128]{1,0:T(8,128)(2,1)S(1)}, u32[]{:S(2)}, u32[]{:S(2)}) collective-permute-start(bf16[512,128]{1,0:T(8,128)(2,1)S(1)} %get-tuple-element.42), channel_id=1, source_target_pairs={{16,2},{17,3},{18,0},{19,1},{20,6},{21,7},{22,4},{23,5},{24,10},{2... | collective-permute-start | bytes 393224 | tf_op jit(solution)/shard_map/ppermute | solution.py:484
